TPU v7x, 32 devices: a whole 2x2x4 slice. The times are simulated.
32 devices in a mesh: group: 8 (over z, y), tensor: 4 (over x, core).
Axes of the slice: x: 2, y: 2, z: 4, core: 2. Of those that a mesh axis runs over, the one named last changes fastest.
Arguments:
- hidden: bfloat16 [4096, 8192], P('group'), may hold values from -1000 to 1000
- norm_gain: float32 [8192], replicated, may hold values from 0.1 to 1.9
- q_weight: bfloat16 [8192, 8192], P('group', 'tensor'), may hold values from -0.0625 to 0.0625
- q_bias: float32 [8192], P('tensor'), may hold values from -3 to 3
- kv_weight: bfloat16 [8192, 2, 1024], P('group'), may hold values from -0.0625 to 0.0625
- kv_bias: float32 [2, 1024], replicated, may hold values from -200 to 200
- prefix_lens: int32 [32], replicated, may hold values from 1 to 256, as said below
- assignment: int32 [32], replicated, may hold values from 0 to 7, as said below
Outputs:
- context: bfloat16 [4096, 8192], P('group', 'tensor')
- kv_cache: bfloat16 [4096, 2, 1024], P('group', None, 'tensor')
Inputs may be any that keep to these rules, and one draw needn't show every extreme that they name: `prefix_lens`: the rollouts of one group have lengths summing to exactly 512; in every group one rollout has exactly 256. `assignment`: every group receives exactly 4 rollouts.
All inputs are finite; a program needn't handle non-finite values.
Results may differ from a plain program's by a relative error of at most 0.004.
The roundings to bfloat16 on the way count: a program that leaves them out, or rounds other values in their place, can miss the bound.
Values may be sent and summed in bfloat16 or wider, within the bound.
No kernel may reach another device: no remote copies, remote signals or barrier semaphores. Data moves between devices by JAX's collectives and lax.ppermute only.
A program may use at most 256 MiB of HBM per device.

v0:
```python
import math

import jax
import jax.numpy as jnp
from jax import lax
from jax.sharding import PartitionSpec as P

HD = 128


EPS = 1e-06
THETA = 1000000.0


def token_layout(prefix_lens, assignment, group_id, tok_rows):
    rollouts = prefix_lens.shape[0]
    member = assignment == group_id
    own_lens = jnp.where(member, prefix_lens, 0)
    starts = jnp.cumsum(own_lens) - own_lens
    places = jnp.arange(tok_rows, dtype=jnp.int32)
    inside = (
        member[None, :]
        & (places[:, None] >= starts[None, :])
        & (places[:, None] < (starts + own_lens)[None, :])
    )
    owner_id = jnp.sum(jnp.where(inside, jnp.arange(rollouts, dtype=jnp.int32)[None, :], 0), axis=1)
    offset = places - jnp.sum(jnp.where(inside, starts[None, :], 0), axis=1)
    return (owner_id, offset, places)


def rotate(values, offset):
    half_dim = values.shape[-1] // 2
    inverse_freq = THETA ** (-2.0 * jnp.arange(half_dim, dtype=jnp.float32) / values.shape[-1])
    angles = offset.astype(jnp.float32)[:, None] * inverse_freq[None, :]
    cosine = jnp.cos(angles)[:, None, :]
    sine_part = jnp.sin(angles)[:, None, :]
    first_half = values[..., :half_dim]
    second_half = values[..., half_dim:]
    return jnp.concatenate(
        [
            first_half * cosine - second_half * sine_part,
            second_half * cosine + first_half * sine_part,
        ],
        axis=-1,
    )


def add_product(normed, portion):
    return jnp.dot(normed, portion, preferred_element_type=jnp.float32)


def on_device(hidden, norm_gain, q_weight, q_bias, kv_weight, kv_bias, prefix_lens, assignment):
    tok_rows, features = hidden.shape
    slice_rows = kv_weight.shape[0]
    q_cols = q_weight.shape[1]
    kv_total = kv_weight.shape[2]
    heads_here = q_cols // HD
    tensor_pos = lax.axis_index("tensor")
    kv_cols = kv_total // lax.axis_size("tensor")
    widened = hidden.astype(jnp.float32)
    normed = (
        widened * lax.rsqrt(jnp.mean(widened * widened, axis=-1, keepdims=True) + EPS) * norm_gain
    ).astype(jnp.bfloat16)
    queries = add_product(normed, lax.all_gather(q_weight, "group", axis=0, tiled=True)) + q_bias
    head_span = max(kv_cols, HD)
    head_base = tensor_pos * kv_cols // head_span * head_span
    local_start = tensor_pos * kv_cols - head_base
    head_rows = lax.dynamic_slice_in_dim(kv_weight, head_base, head_span, 2).reshape(
        slice_rows, 2 * head_span
    )
    projected = add_product(normed, lax.all_gather(head_rows, "group", axis=0, tiled=True))
    projected = projected.reshape(tok_rows, 2, head_span) + lax.dynamic_slice_in_dim(
        kv_bias, head_base, head_span, 1
    )
    kv_here = head_span // HD
    group_size = heads_here // kv_here
    owner_id, offset, places = token_layout(
        prefix_lens, assignment, lax.axis_index("group"), tok_rows
    )
    rotated_queries = rotate(queries.reshape(tok_rows, heads_here, HD), offset).astype(jnp.bfloat16)
    rotated_keys = rotate(projected[:, 0].reshape(tok_rows, kv_here, HD), offset).astype(
        jnp.bfloat16
    )
    value_heads = projected[:, 1].reshape(tok_rows, kv_here, HD).astype(jnp.bfloat16)
    visible = (owner_id[:, None] == owner_id[None, :]) & (places[None, :] <= places[:, None])
    grouped = rotated_queries.reshape(tok_rows, kv_here, group_size, HD)
    scores = jnp.einsum(
        "qgph,kgh->gpqk", grouped, rotated_keys, preferred_element_type=jnp.float32
    ) / math.sqrt(HD)
    scores = jnp.where(visible[None, None], scores, -jnp.inf)
    row_max = jnp.max(scores, axis=-1, keepdims=True)
    exponent = jnp.exp(scores - row_max)
    weights_bf = (exponent / jnp.sum(exponent, axis=-1, keepdims=True)).astype(jnp.bfloat16)
    context = jnp.einsum(
        "gpqk,kgh->qgph", weights_bf, value_heads, preferred_element_type=jnp.float32
    )
    context = context.astype(jnp.bfloat16).reshape(tok_rows, q_cols)
    stacked = jnp.stack(
        [rotated_keys.reshape(tok_rows, head_span), value_heads.reshape(tok_rows, head_span)],
        axis=1,
    )
    kv_cache = lax.dynamic_slice_in_dim(stacked, local_start, kv_cols, 2)
    return (context, kv_cache)


def solution(mesh):
    placed = (
        P("group", None),
        P(),
        P("group", "tensor"),
        P("tensor"),
        P("group", None, None),
        P(),
        P(),
        P(),
    )
    return jax.shard_map(
        on_device,
        mesh=mesh,
        in_specs=placed,
        out_specs=(P("group", "tensor"), P("group", None, "tensor")),
        check_vma=False,
    )
```

profile of v0, /device:TPU:0, one launch (start us, length us, event | category | flops | bytes accessed | tf_op | source)
XLA Modules:
  0.0 845.6 jit_solution(1650823871928386336)
XLA Ops:
  7.2 0.0 all-gather.3.cloned.1.call-start
  7.3 1.9 constant_dynamic-slice_fusion.1
  9.2 1.2 copy.40
  10.5 0.0 all-gather.5.cloned.1.call-start
  10.5 0.7 all-gather.5.cloned.1.call-update
  11.2 0.1 copy.26
  11.3 0.1 reduce-window.8
  11.4 0.1 reduce
  11.6 0.1 select_reduce_fusion.1
  11.7 5.1 fusion.1
  16.8 0.2 fusion.17
  17.0 1.0 multiply_cosine_fusion
  18.0 120.4 %all-gather.3.cloned.1.call-done = bf16[8192,512]{1,0:T(8,128)(2,1)} async-done(((bf16[1024,512]{1,0:T(8,128)(2,1)}), bf16[8192,512]{1,0:T(8,128)(2,1)}) %all-gather.3.cloned.1.call-update) | async-done | bytes 8388624 | tf_op jit(solution)/shard_map/all_gather | solution.py:71
  138.4 11.4 %fusion.10 = f32[512,512]{0,1:T(8,128)S(1)} fusion(bf16[8192,512]{1,0:T(8,128)(2,1)} %all-gather.3.cloned.1.call-done, bf16[512,8192]{1,0:T(8,128)(2,1)} %param.8, f32[8192]{0:T(1024)S(1)} %copy-done.4, f32[512]{0:T(512)S(1)} %add_rsqrt_fusion), kind=kOutput, calls=%fused_computation.17 | convolution fusion | flops 4311744512 | bytes 17860608 | tf_op jit(solution)/shard_map/dot_general | solution.py:49
  149.8 0.1 broadcast_add_fusion
  150.1 0.2 copy.39
  150.3 0.2 copy.38
  150.5 0.1 multiply_subtract_fusion
  150.6 0.1 maximum_convert_fusion
  150.8 0.1 copy.32
  150.9 0.1 pad_maximum_fusion
  151.0 1.1 copy.34
  152.1 623.8 %all-gather.5.cloned.1.call-done = bf16[8192,2048]{1,0:T(8,128)(2,1)} async-done(((bf16[1024,2048]{1,0:T(8,128)(2,1)}), bf16[8192,2048]{1,0:T(8,128)(2,1)}) %all-gather.5.cloned.1.call-update) | async-done | bytes 33554448 | tf_op jit(solution)/shard_map/all_gather | solution.py:64
  775.9 24.0 %add_bitcast_fusion = f32[64,8,16,128]{3,1,2,0:T(8,128)S(1)} fusion(bf16[8192,2048]{1,0:T(8,128)(2,1)} %all-gather.5.cloned.1.call-done, bf16[512,8192]{1,0:T(8,128)(2,1)} %param.8, f32[8192]{0:T(1024)S(1)} %copy-done.4, f32[512]{0:T(512)S(1)} %add_rsqrt_fusion, f32[2048]{0:T(1024)S(1)} %copy-done.5), kind=kOutput, calls=%fused_computation.16 | convolution fusion | flops 17197694976 | bytes 46180352 | tf_op jit(solution)/shard_map/dot_general | solution.py:49
  799.9 0.9 copy.41
  800.8 1.9 subtract_convert_fusion
  802.7 0.5 copy.29
  803.3 0.5 copy.30
  803.8 8.2 fusion.12
  812.0 17.3 %fusion.27 = (f32[2,8,512]{2,1,0:T(8,128)S(1)}, f32[2,8,512,512]{2,3,1,0:T(8,128)}) fusion(f32[2,512,512,8]{2,1,3,0:T(8,128)} %fusion.12, pred[512,512]{0,1:T(8,128)(4,1)S(1)} %fusion.17), kind=kOutput, calls=%fused_computation.53 | output fusion | flops 25166336 | bytes 33849344 | tf_op jit(solution)/shard_map/sub | solution.py:92
  829.2 7.1 fusion.16
  836.3 2.4 copy.33
  (22 shorter events, 0.2 us)
Async XLA Ops:
  7.2 4.4 copy-start
  7.2 4.0 copy-start.2
  7.2 4.0 copy-start.3
  7.2 131.2 %all-gather.3.cloned.1.call-start = ((), (), s32[]{:S(2)}) async-start(), calls=%async_computation | async-start | bytes 9437184 | tf_op jit(solution)/shard_map/all_gather | solution.py:71
  9.2 129.2 %copy-start.4 = (f32[8192]{0:T(1024)S(1)}, f32[8192]{0:T(1024)}, u32[]{:S(2)}) copy-start(f32[8192]{0:T(1024)} %param.9) | copy-start | bytes 98308
  10.5 765.4 %all-gather.5.cloned.1.call-start = ((), (), s32[]{:S(2)}) async-start(), calls=%async_computation.1 | async-start | bytes 37748736 | tf_op jit(solution)/shard_map/all_gather | solution.py:64
  149.8 626.1 %copy-start.5 = (f32[2048]{0:T(1024)S(1)}, f32[2048]{0:T(1024)}, u32[]{:S(2)}) copy-start(f32[2048]{0:T(1024)} %param.11) | copy-start | bytes 24580
  829.2 9.5 %copy-start.1 = (f32[2,1024]{1,0:T(2,128)S(1)}, f32[2,1024]{1,0:T(2,128)}, u32[]{:S(2)}) copy-start(f32[2,1024]{1,0:T(2,128)} %param.13) | copy-start | bytes 24580
Sparse Core Ops, SparseCore 0:
  10.7 127.6 all-gather.2
  139.9 635.8 all-gather.4
where the time goes:
time: 846 us
  waiting for transfers between devices  745 us (88%)
  matrix products  50.6 us (6%)
  other arithmetic  26.2 us (3%)
  between operations  14.3 us (2%)
  local copies, waits for them, and re-layouts  9.42 us (1%)
    all_gather x1, waiting for transfers between devices, on_device(): lax.all_gather(q_weight, 'group', axis=0, tiled=True)  624 us
    all_gather x1, waiting for transfers between devices, on_device(): lax.all_gather(head_rows, 'group', axis=0, tiled=True)  120 us
    dot_general x2, matrix products, add_product(): return jnp.dot(normed, portion, preferred_element_type=jnp.float32)  35.4 us
    sub x1, other arithmetic, on_device(): exponent = jnp.exp(scores - row_max)  17.3 us
  transfers between devices with their start and end apart: 2, of which 2 were waited for; matrix products, arithmetic and copies ran while one was open for 2% of the time, Pallas kernels for 0%

commit v1 on v0

--- a/solution.py
+++ b/solution.py
@@ -1,8 +1,11 @@
+import functools
 import math
 
 import jax
 import jax.numpy as jnp
 from jax import lax
+from jax.experimental import pallas as pl
+from jax.experimental.pallas import tpu as pltpu
 from jax.sharding import PartitionSpec as P
 
 HD = 128
@@ -10,6 +13,8 @@
 
 EPS = 1e-06
 THETA = 1000000.0
+QROWS = 128
+MAXLEN = 256
 
 
 def token_layout(prefix_lens, assignment, group_id, tok_rows):
@@ -49,7 +54,16 @@
     return jnp.dot(normed, portion, preferred_element_type=jnp.float32)
 
 
-def on_device(hidden, norm_gain, q_weight, q_bias, kv_weight, kv_bias, prefix_lens, assignment):
+def normalise(hidden, norm_gain):
+    widened = hidden.astype(jnp.float32)
+    return (
+        widened * lax.rsqrt(jnp.mean(widened * widened, axis=-1, keepdims=True) + EPS) * norm_gain
+    ).astype(jnp.bfloat16)
+
+
+def gathered_form(
+    hidden, norm_gain, q_weight, q_bias, kv_weight, kv_bias, prefix_lens, assignment
+):
     tok_rows, features = hidden.shape
     slice_rows = kv_weight.shape[0]
     q_cols = q_weight.shape[1]
@@ -57,10 +71,7 @@
     heads_here = q_cols // HD
     tensor_pos = lax.axis_index("tensor")
     kv_cols = kv_total // lax.axis_size("tensor")
-    widened = hidden.astype(jnp.float32)
-    normed = (
-        widened * lax.rsqrt(jnp.mean(widened * widened, axis=-1, keepdims=True) + EPS) * norm_gain
-    ).astype(jnp.bfloat16)
+    normed = normalise(hidden, norm_gain)
     queries = add_product(normed, lax.all_gather(q_weight, "group", axis=0, tiled=True)) + q_bias
     head_span = max(kv_cols, HD)
     head_base = tensor_pos * kv_cols // head_span * head_span
@@ -103,6 +114,213 @@
     return (context, kv_cache)
 
 
+def attention_kernel(q_ref, bias_ref, cos_ref, sin_ref, k_ref, v_ref, first_ref, out_ref):
+    rows = q_ref.shape[0]
+    queries = q_ref[...] + bias_ref[...]
+    turned = queries * cos_ref[...] + pltpu.roll(queries, HD // 2, 1) * sin_ref[...]
+    turned = turned.astype(jnp.bfloat16)
+    for block in range(rows // QROWS):
+        top = block * QROWS
+        low = max(0, top - MAXLEN)
+        end = top + QROWS
+        scores = lax.dot_general(
+            turned[top:end],
+            k_ref[low:end],
+            (((1,), (1,)), ((), ())),
+            preferred_element_type=jnp.float32,
+        ) * (1.0 / math.sqrt(HD))
+        row = lax.broadcasted_iota(jnp.int32, scores.shape, 0) + top
+        col = lax.broadcasted_iota(jnp.int32, scores.shape, 1) + low
+        visible = (col <= row) & (col >= first_ref[top:end])
+        scores = jnp.where(visible, scores, -jnp.inf)
+        exponent = jnp.exp(scores - jnp.max(scores, axis=-1, keepdims=True))
+        weights = (exponent / jnp.sum(exponent, axis=-1, keepdims=True)).astype(jnp.bfloat16)
+        out_ref[top:end] = jnp.dot(
+            weights, v_ref[low:end], preferred_element_type=jnp.float32
+        ).astype(jnp.bfloat16)
+
+
+def attend(queries, skip, bias, cosine, sine, keys_values, first):
+    rows, cols = queries.shape
+    heads = cols // HD - skip
+    flops = 4 * heads * rows * 3 * QROWS * HD
+    return pl.pallas_call(
+        attention_kernel,
+        grid=(heads,),
+        in_specs=[
+            pl.BlockSpec((rows, HD), lambda h: (0, h + skip)),
+            pl.BlockSpec((1, HD), lambda h: (0, h)),
+            pl.BlockSpec((rows, HD), lambda h: (0, 0)),
+            pl.BlockSpec((rows, HD), lambda h: (0, 0)),
+            pl.BlockSpec((rows, HD), lambda h: (0, 0)),
+            pl.BlockSpec((rows, HD), lambda h: (0, 1)),
+            pl.BlockSpec((rows, 1), lambda h: (0, 0)),
+        ],
+        out_specs=pl.BlockSpec((rows, HD), lambda h: (0, h)),
+        out_shape=jax.ShapeDtypeStruct((rows, heads * HD), jnp.bfloat16),
+        compiler_params=pltpu.CompilerParams(vmem_limit_bytes=32 * 2**20),
+        cost_estimate=pl.CostEstimate(
+            flops=flops,
+            bytes_accessed=rows * heads * HD * 6 + rows * HD * 12,
+            transcendentals=heads * rows * 3 * QROWS,
+        ),
+    )(queries, bias, cosine, sine, keys_values, keys_values, first)
+
+
+CODES = (0, 1, 6, 7, 2, 3, 4, 5)
+
+
+def pairs_from(sources, code):
+    return [(s, s ^ code) for s in sources]
+
+
+MIDDLE = (2, 3, 4, 5)
+ENDS = (0, 1, 6, 7)
+
+
+def middle_form(hidden, norm_gain, q_weight, q_bias, kv_weight, kv_bias, prefix_lens, assignment):
+    tok_rows, features = hidden.shape
+    slice_rows, q_cols = q_weight.shape
+    half_cols = q_cols // 2
+    group = lax.axis_index("group")
+    tensor = lax.axis_index("tensor")
+    y = group & 1
+    is_middle = (group >= 2) & (group < 6)
+    blocks = features // slice_rows
+
+    def over_group(value, sources, code):
+        return lax.ppermute(value, "group", pairs_from(sources, code))
+
+    def over_tensor(value, code):
+        return lax.ppermute(value, "tensor", pairs_from(range(4), code))
+
+    widths = (2 * HD, half_cols // 2, half_cols // 4)
+
+    def columns(half):
+        head = (2 * tensor + half) * HD
+        kv_part = lax.dynamic_slice_in_dim(kv_weight, head, HD, 2).reshape(slice_rows, 2 * HD)
+        taken, place = [], half * half_cols
+        for chunk, width in enumerate(widths):
+            part = lax.dynamic_slice_in_dim(q_weight, place, width, 1)
+            taken.append(jnp.concatenate([kv_part, part], axis=1) if chunk == 0 else part)
+            place = place + width
+        return taken
+
+    own = columns(y)
+    other = columns(1 - y)
+
+    normed = normalise(hidden, norm_gain)
+    normed = normed.reshape(tok_rows, blocks, slice_rows).transpose(1, 0, 2)
+
+    core = tensor & 1
+    half = lax.dynamic_slice_in_dim(normed, core * (blocks // 2), blocks // 2, 0)
+    quarter = lax.dynamic_slice_in_dim(normed, tensor * 2, 2, 0)
+
+    def placed(parts):
+        whole = jnp.zeros_like(normed)
+        for part, at in parts:
+            whole = lax.dynamic_update_slice_in_dim(whole, part, at, 0)
+        return whole
+
+    def from_half(got):
+        twin = over_tensor(got, 1)
+        return placed([(got, core * (blocks // 2)), (twin, (1 - core) * (blocks // 2))])
+
+    def from_quarter(got):
+        across = over_tensor(got, 2)
+        return placed(
+            [
+                (got, tensor * 2),
+                (across, (tensor ^ 2) * 2),
+                (over_tensor(got, 1), (tensor ^ 1) * 2),
+                (over_tensor(across, 1), (tensor ^ 3) * 2),
+            ]
+        )
+
+    rows_of = [
+        normed,
+        from_half(over_group(half, MIDDLE, 1)),
+        from_quarter(over_group(quarter, ENDS, 2)),
+        from_quarter(over_group(quarter, ENDS, 3)),
+    ]
+
+    pieces = []
+    for mine, its in zip(own, other):
+        end_own = over_group(mine, ENDS, 2)
+        end_swap = over_group(its, ENDS, 3)
+        pieces.append(
+            {
+                0: mine,
+                1: over_group(its, MIDDLE, 1),
+                6: over_group(mine, MIDDLE, 6),
+                7: over_group(its, MIDDLE, 7),
+                2: end_own,
+                3: end_swap,
+                4: over_group(end_own, MIDDLE, 6),
+                5: over_group(end_swap, MIDDLE, 6),
+            }
+        )
+
+    bias = lax.dynamic_slice_in_dim(q_bias, y * half_cols, half_cols, 0)[None, :]
+    kv_bias_here = lax.dynamic_slice_in_dim(kv_bias, (2 * tensor + y) * HD, HD, 1)
+    inverse_freq = THETA ** (-2.0 * jnp.arange(HD // 2, dtype=jnp.float32) / HD)
+
+    results = []
+    for code in range(4):
+        _, offset, places = token_layout(prefix_lens, assignment, group ^ code, tok_rows)
+        angles = offset.astype(jnp.float32)[:, None] * inverse_freq[None, :]
+        cosine, sine = jnp.cos(angles), jnp.sin(angles)
+        cosine = jnp.concatenate([cosine, cosine], axis=1)
+        sine = jnp.concatenate([-sine, sine], axis=1)
+        first = (places - offset)[:, None]
+        place = 0
+        outs = []
+        for chunk, width in enumerate(widths):
+            total = None
+            for piece in CODES:
+                block = lax.dynamic_index_in_dim(rows_of[code], group ^ piece, 0, keepdims=False)
+                term = add_product(block, pieces[chunk][piece])
+                total = term if total is None else total + term
+            if chunk == 0:
+                keys = total[:, :HD] + kv_bias_here[0]
+                swapped = jnp.concatenate([keys[:, HD // 2 :], keys[:, : HD // 2]], axis=1)
+                keys = keys * cosine + swapped * sine
+                values = total[:, HD : 2 * HD] + kv_bias_here[1]
+                keys_values = jnp.concatenate([keys, values], axis=1).astype(jnp.bfloat16)
+            out = attend(
+                total,
+                2 if chunk == 0 else 0,
+                bias[:, place : place + width],
+                cosine,
+                sine,
+                keys_values,
+                first,
+            )
+            place += width
+            outs.append(jnp.concatenate([keys_values, out], axis=1) if chunk == 0 else out)
+        results.append(outs)
+
+    mine, its = [], []
+    for chunk in range(len(widths)):
+        back_own = over_group(results[2][chunk], MIDDLE, 2)
+        back_other = over_group(results[3][chunk], MIDDLE, 3)
+        beside = over_group(results[1][chunk], MIDDLE, 1)
+        mine.append(jnp.where(is_middle, results[0][chunk], back_own))
+        its.append(jnp.where(is_middle, beside, back_other))
+
+    def in_order(a, b):
+        return jnp.where(y == 0, jnp.concatenate([a, b], axis=-1), jnp.concatenate([b, a], axis=-1))
+
+    context = in_order(
+        jnp.concatenate([mine[0][:, 2 * HD :]] + mine[1:], axis=1),
+        jnp.concatenate([its[0][:, 2 * HD :]] + its[1:], axis=1),
+    )
+    kv_cache = in_order(
+        mine[0][:, : 2 * HD].reshape(tok_rows, 2, HD), its[0][:, : 2 * HD].reshape(tok_rows, 2, HD)
+    )
+    return (context, kv_cache)
+
+
 def solution(mesh):
     placed = (
         P("group", None),
@@ -114,8 +332,9 @@
         P(),
         P(),
     )
+    fits = mesh.shape["group"] == 8 and mesh.shape["tensor"] == 4
     return jax.shard_map(
-        on_device,
+        middle_form if fits else gathered_form,
         mesh=mesh,
         in_specs=placed,
         out_specs=(P("group", "tensor"), P("group", None, "tensor")),

time: 846 us -> 693 us (0.82); the launches traced: 846 us -> 681 us
  waiting for transfers between devices: 745 us -> 198 us
  starting transfers between devices: 0.08 us -> 130 us
  local copies, waits for them, and re-layouts: 9.42 us -> 119 us
  matrix products: 50.6 us -> 148 us
  Pallas kernels: 0 us -> 53.2 us
  between operations: 14.3 us -> 3.62 us
    all_gather x2 -> x0, waiting for transfers between devices: 744 us -> none  [the longest x1 624 us: on_device(): lax.all_gather(q_weight, 'group', axis=0, tiled=True)]
    ppermute x0 -> x40, waiting for transfers between devices: none -> 198 us  [the longest x33 174 us: over_group(): return lax.ppermute(value, 'group', pairs_from(sources, code))]
    ppermute x0 -> x40, starting transfers between devices: none -> 130 us  [the longest x33 126 us: over_group(): return lax.ppermute(value, 'group', pairs_from(sources, code))]
    dot_general x2 -> x96, matrix products: 35.4 us -> 148 us  [add_product(): return jnp.dot(normed, portion, preferred_element_type=jnp.float32)]
    pallas_call x0 -> x12, Pallas kernels: none -> 53.2 us  [attend(): pl.pallas_call(attention_kernel, grid=(heads,), in_specs=[pl.BlockSpec((r...]
    ppermute x0 -> x10, local copies, waits for them, and re-layouts: none -> 52.8 us  [the longest x7 38.7 us: over_tensor(): return lax.ppermute(value, 'tensor', pairs_from(range(4), code))]
    dynamic_update_slice x0 -> x9, local copies, waits for them, and re-layouts: none -> 21.8 us  [placed(): whole = lax.dynamic_update_slice_in_dim(whole, part, at, 0)]
    sub x2 -> x0, other arithmetic: 17.4 us -> none  [the longest x1 17.3 us: on_device(): exponent = jnp.exp(scores - row_max)]
  transfers between devices with their start and end apart: 2 -> 40, of which waited for: 2 -> 8; matrix products, arithmetic and copies ran while one was open for 2% -> 37% of each run, Pallas kernels for 0% -> 7%
where the time goes in v1:
time: 693 us; the launch traced here: 681 us
  waiting for transfers between devices  198 us (29%)
  matrix products  148 us (21%)
  starting transfers between devices  130 us (19%)
  local copies, waits for them, and re-layouts  119 us (17%)
  Pallas kernels  53.2 us (8%)
  other arithmetic  29.1 us (4%)
    ppermute x33, waiting for transfers between devices, over_group(): return lax.ppermute(value, 'group', pairs_from(sources, code))  174 us
    dot_general x96, matrix products, add_product(): return jnp.dot(normed, portion, preferred_element_type=jnp.float32)  148 us
    ppermute x33, starting transfers between devices, over_group(): return lax.ppermute(value, 'group', pairs_from(sources, code))  126 us
    pallas_call x12, Pallas kernels, attend(): pl.pallas_call(attention_kernel, grid=(heads,), in_specs=[pl.BlockSpec((r...  53.2 us
    ppermute x7, local copies, waits for them, and re-layouts, over_tensor(): return lax.ppermute(value, 'tensor', pairs_from(range(4), code))  38.7 us
    ppermute x7, waiting for transfers between devices, over_tensor(): return lax.ppermute(value, 'tensor', pairs_from(range(4), code))  24.7 us
    dynamic_update_slice x9, local copies, waits for them, and re-layouts, placed(): whole = lax.dynamic_update_slice_in_dim(whole, part, at, 0)  21.8 us
    unnamed x212, local copies, waits for them, and re-layouts  16.2 us
  transfers between devices with their start and end apart: 40, of which 8 were waited for; matrix products, arithmetic and copies ran while one was open for 37% of the time, Pallas kernels for 7%

profile of v1, /device:TPU:0, one launch (start us, length us, event | category | flops | bytes accessed | tf_op | source)
XLA Modules:
  0.0 681.4 jit_solution(15599861155979477417)
XLA Ops:
  3.3 5.9 collective-permute-start.24
  14.1 4.9 collective-permute-start.4
  24.6 11.9 %copy.161 = bf16[512,8192]{0,1:T(8,128)(2,1)} copy(bf16[512,8192]{1,0:T(8,128)(2,1)} %param.8) | data formatting | bytes 16777216 | tf_op args[0]
  36.6 5.2 fusion
  43.3 7.8 %fusion.2 = bf16[512,8192]{0,1:T(8,128)(2,1)} fusion(bf16[512,8192]{0,1:T(8,128)(2,1)} %copy.161, f32[8192]{0:T(1024)S(1)} %copy-done.80, f32[512]{0:T(512)S(1)} %add_rsqrt_fusion), kind=kLoop, calls=%fused_computation.4 | loop fusion | flops 16777216 | bytes 16812032 | tf_op jit(solution)/shard_map/convert_element_type | solution.py:61
  57.1 30.8 %collective-permute-done.23 = bf16[1024,256]{1,0:T(8,128)(2,1)} collective-permute-done((bf16[1024,256]{1,0:T(8,128)(2,1)S(1)}, bf16[1024,256]{1,0:T(8,128)(2,1)}, u32[]{:S(2)}, u32[]{:S(2)}) %collective-permute-start.23) | collective-permute-done | bytes 524320 | tf_op jit(solution)/shard_map/ppermute | solution.py:192
  88.7 5.5 fusion.326
  95.8 4.5 dynamic-slice_bitcast_fusion
  102.7 13.5 %collective-permute-start.16 = (bf16[1024,512]{1,0:T(8,128)(2,1)}, bf16[1024,512]{1,0:T(8,128)(2,1)}, u32[]{:S(2)}, u32[]{:S(2)}) collective-permute-start(bf16[1024,512]{1,0:T(8,128)(2,1)} %get-tuple-element.23), channel_id=1, source_target_pairs={{0,12},{4,8},{24,20},{28,16},{1,13},{5,9},{25,21},{29,17},{2,14},{... | collective-permute-start | bytes 3145736 | tf_op jit(solution)/shard_map/ppermute | solution.py:192
  134.1 65.3 %collective-permute-start.31 = (bf16[2,512,1024]{1,2,0:T(8,128)(2,1)S(1)}, bf16[2,512,1024]{1,2,0:T(8,128)(2,1)}, u32[]{:S(2)}, u32[]{:S(2)}) collective-permute-start(bf16[2,512,1024]{1,2,0:T(8,128)(2,1)S(1)} %copy-done.55), channel_id=1, source_target_pairs={{0,12},{4,8},{24,20},{28,16},{1,13},{5,9},{25,21},{29,17},{2,14},{... | collective-permute-start | bytes 6291464 | tf_op jit(solution)/shard_map/ppermute | solution.py:192
  225.7 18.3 %collective-permute-done.31 = bf16[2,512,1024]{1,2,0:T(8,128)(2,1)} collective-permute-done((bf16[2,512,1024]{1,2,0:T(8,128)(2,1)S(1)}, bf16[2,512,1024]{1,2,0:T(8,128)(2,1)}, u32[]{:S(2)}, u32[]{:S(2)}) %collective-permute-start.31) | collective-permute-done | bytes 2097184 | tf_op jit(solution)/shard_map/ppermute | solution.py:192
  245.5 42.5 %collective-permute-done.7 = bf16[2,512,1024]{1,2,0:T(8,128)(2,1)} collective-permute-done((bf16[2,512,1024]{1,2,0:T(8,128)(2,1)S(1)}, bf16[2,512,1024]{1,2,0:T(8,128)(2,1)}, u32[]{:S(2)}, u32[]{:S(2)}) %collective-permute-start.7) | collective-permute-done | bytes 2097184 | tf_op jit(solution)/shard_map/ppermute | solution.py:192
  300.4 3.9 copy.210
  304.3 3.9 copy.180
  310.4 24.7 %collective-permute-done.8 = bf16[2,512,1024]{1,2,0:T(8,128)(2,1)} collective-permute-done((bf16[2,512,1024]{1,2,0:T(8,128)(2,1)}, bf16[2,512,1024]{1,2,0:T(8,128)(2,1)}, u32[]{:S(2)}, u32[]{:S(2)}) %collective-permute-start.8) | collective-permute-done | bytes 2097184 | tf_op jit(solution)/shard_map/ppermute | solution.py:195
  348.6 4.0 copy.181
  352.5 6.3 copy.198
  359.3 3.9 copy.212
  363.3 4.0 copy.182
  376.6 4.4 broadcast.34.clone.2
  383.5 3.9 copy.213
  387.4 12.6 %copy.183 = bf16[2,512,1024]{2,1,0:T(8,128)(2,1)} copy(bf16[2,512,1024]{1,2,0:T(8,128)(2,1)} %collective-permute-done.10) | data formatting | bytes 4194304 | tf_op jit(solution)/shard_map/ppermute | solution.py:195
  400.0 4.6 constant_dynamic-update-slice_fusion
  462.5 6.4 copy.199
  469.0 4.8 constant_dynamic-update-slice_fusion.4
  524.1 6.6 shard_map.103
  531.5 6.6 shard_map.104
  567.6 6.6 shard_map.97
  574.3 6.6 shard_map.98
  588.3 25.2 %collective-permute-done.37 = bf16[512,512]{1,0:T(8,128)(2,1)S(1)} collective-permute-done((bf16[512,512]{1,0:T(8,128)(2,1)S(1)}, bf16[512,512]{1,0:T(8,128)(2,1)S(1)}, u32[]{:S(2)}, u32[]{:S(2)}) %collective-permute-start.37) | collective-permute-done | bytes 524320 | tf_op jit(solution)/shard_map/ppermute | solution.py:192
  615.0 42.6 %collective-permute-done.39 = bf16[512,256]{1,0:T(8,128)(2,1)S(1)} collective-permute-done((bf16[512,256]{1,0:T(8,128)(2,1)S(1)}, bf16[512,256]{1,0:T(8,128)(2,1)S(1)}, u32[]{:S(2)}, u32[]{:S(2)}) %collective-permute-start.39) | collective-permute-done | bytes 262176 | tf_op jit(solution)/shard_map/ppermute | solution.py:192
  658.6 10.4 %collective-permute-done.19 = bf16[512,512]{1,0:T(8,128)(2,1)S(1)} collective-permute-done((bf16[512,512]{1,0:T(8,128)(2,1)S(1)}, bf16[512,512]{1,0:T(8,128)(2,1)S(1)}, u32[]{:S(2)}, u32[]{:S(2)}) %collective-permute-start.19) | collective-permute-done | bytes 524320 | tf_op jit(solution)/shard_map/ppermute | solution.py:192
  (464 shorter events, 269.7 us)
Async XLA Ops:
  3.3 52.9 %collective-permute-start.24 = (bf16[1024,256]{1,0:T(8,128)(2,1)}, bf16[1024,256]{1,0:T(8,128)(2,1)S(1)}, u32[]{:S(2)}, u32[]{:S(2)}) collective-permute-start(bf16[1024,256]{1,0:T(8,128)(2,1)} %get-tuple-element.21), channel_id=1, source_target_pairs={{0,12},{4,8},{24,20},{28,16},{1,13},{5,9},{25,21},{29,17},{2,14},{... | collective-permute-start | bytes 1572872 | tf_op jit(solution)/shard_map/ppermute | solution.py:192
  9.2 84.9 %collective-permute-start.22 = (bf16[1024,256]{1,0:T(8,128)(2,1)}, bf16[1024,256]{1,0:T(8,128)(2,1)S(1)}, u32[]{:S(2)}, u32[]{:S(2)}) collective-permute-start(bf16[1024,256]{1,0:T(8,128)(2,1)} %get-tuple-element.21), channel_id=1, source_target_pairs={{8,20},{12,16},{16,12},{20,8},{9,21},{13,17},{17,13},{21,9},{10,22... | collective-permute-start | bytes 1572872 | tf_op jit(solution)/shard_map/ppermute | solution.py:192
  14.1 88.6 %collective-permute-start.4 = (bf16[1024,512]{1,0:T(8,128)(2,1)}, bf16[1024,512]{1,0:T(8,128)(2,1)}, u32[]{:S(2)}, u32[]{:S(2)}) collective-permute-start(bf16[1024,512]{1,0:T(8,128)(2,1)} %pad_maximum_fusion.1), channel_id=1, source_target_pairs={{0,12},{4,8},{24,20},{28,16},{1,13},{5,9},{25,21},{29,17},{2,14},{... | collective-permute-start | bytes 3145736 | tf_op jit(solution)/shard_map/ppermute | solution.py:192
  20.3 98.9 %collective-permute-start.3 = (bf16[1024,512]{1,0:T(8,128)(2,1)}, bf16[1024,512]{1,0:T(8,128)(2,1)}, u32[]{:S(2)}, u32[]{:S(2)}) collective-permute-start(bf16[1024,512]{1,0:T(8,128)(2,1)} %pad_maximum_fusion), channel_id=1, source_target_pairs={{0,8},{4,12},{24,16},{28,20},{1,9},{5,13},{25,17},{29,21},{2,10},{... | collective-permute-start | bytes 3145736 | tf_op jit(solution)/shard_map/ppermute | solution.py:192
  22.6 65.4 %collective-permute-start.23 = (bf16[1024,256]{1,0:T(8,128)(2,1)S(1)}, bf16[1024,256]{1,0:T(8,128)(2,1)}, u32[]{:S(2)}, u32[]{:S(2)}) collective-permute-start(bf16[1024,256]{1,0:T(8,128)(2,1)S(1)} %get-tuple-element.18), channel_id=1, source_target_pairs={{0,8},{4,12},{24,16},{28,20},{1,9},{5,13},{25,17},{29,21},{2,10},{... | collective-permute-start | bytes 1572872 | tf_op jit(solution)/shard_map/ppermute | solution.py:192
  56.2 44.0 %collective-permute-start.20 = (bf16[1024,256]{1,0:T(8,128)(2,1)}, bf16[1024,256]{1,0:T(8,128)(2,1)S(1)}, u32[]{:S(2)}, u32[]{:S(2)}) collective-permute-start(bf16[1024,256]{1,0:T(8,128)(2,1)} %get-tuple-element.21), channel_id=1, source_target_pairs={{8,12},{12,8},{16,20},{20,16},{9,13},{13,9},{17,21},{21,17},{10,14... | collective-permute-start | bytes 1572872 | tf_op jit(solution)/shard_map/ppermute | solution.py:192
  94.1 37.3 %collective-permute-start.2 = (bf16[1024,512]{1,0:T(8,128)(2,1)}, bf16[1024,512]{1,0:T(8,128)(2,1)}, u32[]{:S(2)}, u32[]{:S(2)}) collective-permute-start(bf16[1024,512]{1,0:T(8,128)(2,1)} %pad_maximum_fusion.1), channel_id=1, source_target_pairs={{8,20},{12,16},{16,12},{20,8},{9,21},{13,17},{17,13},{21,9},{10,22... | collective-permute-start | bytes 3145736 | tf_op jit(solution)/shard_map/ppermute | solution.py:192
  100.3 33.8 %collective-permute-start = (bf16[1024,512]{1,0:T(8,128)(2,1)}, bf16[1024,512]{1,0:T(8,128)(2,1)}, u32[]{:S(2)}, u32[]{:S(2)}) collective-permute-start(bf16[1024,512]{1,0:T(8,128)(2,1)} %pad_maximum_fusion.1), channel_id=1, source_target_pairs={{8,12},{12,8},{16,20},{20,16},{9,13},{13,9},{17,21},{21,17},{10,14... | collective-permute-start | bytes 3145736 | tf_op jit(solution)/shard_map/ppermute | solution.py:192
  101.9 97.4 %collective-permute-start.1 = (bf16[1024,512]{1,0:T(8,128)(2,1)}, bf16[1024,512]{1,0:T(8,128)(2,1)S(1)}, u32[]{:S(2)}, u32[]{:S(2)}) collective-permute-start(bf16[1024,512]{1,0:T(8,128)(2,1)} %pad_maximum_fusion), channel_id=1, source_target_pairs={{8,16},{12,20},{16,8},{20,12},{9,17},{13,21},{17,9},{21,13},{10,18... | collective-permute-start | bytes 3145736 | tf_op jit(solution)/shard_map/ppermute | solution.py:192
  102.7 99.3 %collective-permute-start.16 = (bf16[1024,512]{1,0:T(8,128)(2,1)}, bf16[1024,512]{1,0:T(8,128)(2,1)}, u32[]{:S(2)}, u32[]{:S(2)}) collective-permute-start(bf16[1024,512]{1,0:T(8,128)(2,1)} %get-tuple-element.23), channel_id=1, source_target_pairs={{0,12},{4,8},{24,20},{28,16},{1,13},{5,9},{25,21},{29,17},{2,14},{... | collective-permute-start | bytes 3145736 | tf_op jit(solution)/shard_map/ppermute | solution.py:192
  119.2 85.4 %collective-permute-start.15 = (bf16[1024,512]{1,0:T(8,128)(2,1)S(1)}, bf16[1024,512]{1,0:T(8,128)(2,1)}, u32[]{:S(2)}, u32[]{:S(2)}) collective-permute-start(bf16[1024,512]{1,0:T(8,128)(2,1)S(1)} %get-tuple-element.22), channel_id=1, source_target_pairs={{0,8},{4,12},{24,16},{28,20},{1,9},{5,13},{25,17},{29,21},{2,10},{... | collective-permute-start | bytes 3145736 | tf_op jit(solution)/shard_map/ppermute | solution.py:192
  131.5 77.6 %collective-permute-start.14 = (bf16[1024,512]{1,0:T(8,128)(2,1)}, bf16[1024,512]{1,0:T(8,128)(2,1)S(1)}, u32[]{:S(2)}, u32[]{:S(2)}) collective-permute-start(bf16[1024,512]{1,0:T(8,128)(2,1)} %get-tuple-element.23), channel_id=1, source_target_pairs={{8,20},{12,16},{16,12},{20,8},{9,21},{13,17},{17,13},{21,9},{10,22... | collective-permute-start | bytes 3145736 | tf_op jit(solution)/shard_map/ppermute | solution.py:192
  134.1 109.9 %collective-permute-start.31 = (bf16[2,512,1024]{1,2,0:T(8,128)(2,1)S(1)}, bf16[2,512,1024]{1,2,0:T(8,128)(2,1)}, u32[]{:S(2)}, u32[]{:S(2)}) collective-permute-start(bf16[2,512,1024]{1,2,0:T(8,128)(2,1)S(1)} %copy-done.55), channel_id=1, source_target_pairs={{0,12},{4,8},{24,20},{28,16},{1,13},{5,9},{25,21},{29,17},{2,14},{... | collective-permute-start | bytes 6291464 | tf_op jit(solution)/shard_map/ppermute | solution.py:192
  199.3 88.7 %collective-permute-start.7 = (bf16[2,512,1024]{1,2,0:T(8,128)(2,1)S(1)}, bf16[2,512,1024]{1,2,0:T(8,128)(2,1)}, u32[]{:S(2)}, u32[]{:S(2)}) collective-permute-start(bf16[2,512,1024]{1,2,0:T(8,128)(2,1)S(1)} %copy-done.55), channel_id=1, source_target_pairs={{0,8},{4,12},{24,16},{28,20},{1,9},{5,13},{25,17},{29,21},{2,10},{... | collective-permute-start | bytes 6291464 | tf_op jit(solution)/shard_map/ppermute | solution.py:192
  214.5 75.8 %collective-permute-start.6 = (bf16[1024,512]{1,0:T(8,128)(2,1)}, bf16[1024,512]{1,0:T(8,128)(2,1)S(1)}, u32[]{:S(2)}, u32[]{:S(2)}) collective-permute-start(bf16[1024,512]{1,0:T(8,128)(2,1)} %collective-permute-done.4), channel_id=1, source_target_pairs={{8,16},{12,20},{16,8},{20,12},{9,17},{13,21},{17,9},{21,13},{10,18... | collective-permute-start | bytes 3145736 | tf_op jit(solution)/shard_map/ppermute | solution.py:192
  215.4 75.6 %collective-permute-start.5 = (bf16[1024,512]{1,0:T(8,128)(2,1)}, bf16[1024,512]{1,0:T(8,128)(2,1)}, u32[]{:S(2)}, u32[]{:S(2)}) collective-permute-start(bf16[1024,512]{1,0:T(8,128)(2,1)} %collective-permute-done.3), channel_id=1, source_target_pairs={{8,16},{12,20},{16,8},{20,12},{9,17},{13,21},{17,9},{21,13},{10,18... | collective-permute-start | bytes 3145736 | tf_op jit(solution)/shard_map/ppermute | solution.py:192
  219.0 133.5 %collective-permute-start.28 = (bf16[4,512,1024]{1,2,0:T(8,128)(2,1)}, bf16[4,512,1024]{1,2,0:T(8,128)(2,1)}, u32[]{:S(2)}, u32[]{:S(2)}) collective-permute-start(bf16[4,512,1024]{1,2,0:T(8,128)(2,1)} %dynamic-slice_bitcast_fusion), channel_id=1, source_target_pairs={{8,12},{12,8},{16,20},{20,16},{9,13},{13,9},{17,21},{21,17},{10,14... | collective-permute-start | bytes 12582920 | tf_op jit(solution)/shard_map/ppermute | solution.py:192
  244.0 66.2 %collective-permute-start.32 = (bf16[2,512,1024]{1,2,0:T(8,128)(2,1)}, bf16[2,512,1024]{1,2,0:T(8,128)(2,1)}, u32[]{:S(2)}, u32[]{:S(2)}) collective-permute-start(bf16[2,512,1024]{1,2,0:T(8,128)(2,1)} %collective-permute-done.31), channel_id=1, source_target_pairs={{0,2},{1,3},{2,0},{3,1},{4,6},{5,7},{6,4},{7,5},{8,10},{9,11},{10,... | collective-permute-start | bytes 6291464 | tf_op jit(solution)/shard_map/ppermute | solution.py:195
  288.0 47.0 %collective-permute-start.8 = (bf16[2,512,1024]{1,2,0:T(8,128)(2,1)}, bf16[2,512,1024]{1,2,0:T(8,128)(2,1)}, u32[]{:S(2)}, u32[]{:S(2)}) collective-permute-start(bf16[2,512,1024]{1,2,0:T(8,128)(2,1)} %collective-permute-done.7), channel_id=1, source_target_pairs={{0,2},{1,3},{2,0},{3,1},{4,6},{5,7},{6,4},{7,5},{8,10},{9,11},{10,... | collective-permute-start | bytes 6291464 | tf_op jit(solution)/shard_map/ppermute | solution.py:195
  296.8 62.5 %collective-permute-start.33 = (bf16[2,512,1024]{1,2,0:T(8,128)(2,1)}, bf16[2,512,1024]{1,2,0:T(8,128)(2,1)}, u32[]{:S(2)}, u32[]{:S(2)}) collective-permute-start(bf16[2,512,1024]{1,2,0:T(8,128)(2,1)} %collective-permute-done.31), channel_id=1, source_target_pairs={{0,1},{1,0},{2,3},{3,2},{4,5},{5,4},{6,7},{7,6},{8,9},{9,8},{10,11... | collective-permute-start | bytes 6291464 | tf_op jit(solution)/shard_map/ppermute | solution.py:195
  296.9 66.4 %collective-permute-start.9 = (bf16[2,512,1024]{1,2,0:T(8,128)(2,1)}, bf16[2,512,1024]{1,2,0:T(8,128)(2,1)}, u32[]{:S(2)}, u32[]{:S(2)}) collective-permute-start(bf16[2,512,1024]{1,2,0:T(8,128)(2,1)} %collective-permute-done.7), channel_id=1, source_target_pairs={{0,1},{1,0},{2,3},{3,2},{4,5},{5,4},{6,7},{7,6},{8,9},{9,8},{10,11... | collective-permute-start | bytes 6291464 | tf_op jit(solution)/shard_map/ppermute | solution.py:195
  310.2 73.3 %collective-permute-start.34 = (bf16[2,512,1024]{1,2,0:T(8,128)(2,1)}, bf16[2,512,1024]{1,2,0:T(8,128)(2,1)}, u32[]{:S(2)}, u32[]{:S(2)}) collective-permute-start(bf16[2,512,1024]{1,2,0:T(8,128)(2,1)} %collective-permute-done.32), channel_id=1, source_target_pairs={{0,1},{1,0},{2,3},{3,2},{4,5},{5,4},{6,7},{7,6},{8,9},{9,8},{10,11... | collective-permute-start | bytes 6291464 | tf_op jit(solution)/shard_map/ppermute | solution.py:195
  335.0 52.4 %collective-permute-start.10 = (bf16[2,512,1024]{1,2,0:T(8,128)(2,1)}, bf16[2,512,1024]{1,2,0:T(8,128)(2,1)}, u32[]{:S(2)}, u32[]{:S(2)}) collective-permute-start(bf16[2,512,1024]{1,2,0:T(8,128)(2,1)} %collective-permute-done.8), channel_id=1, source_target_pairs={{0,1},{1,0},{2,3},{3,2},{4,5},{5,4},{6,7},{7,6},{8,9},{9,8},{10,11... | collective-permute-start | bytes 6291464 | tf_op jit(solution)/shard_map/ppermute | solution.py:195
  358.8 103.7 %collective-permute-start.29 = (bf16[4,512,1024]{1,2,0:T(8,128)(2,1)}, bf16[4,512,1024]{1,2,0:T(8,128)(2,1)}, u32[]{:S(2)}, u32[]{:S(2)}) collective-permute-start(bf16[4,512,1024]{1,2,0:T(8,128)(2,1)} %collective-permute-done.28), channel_id=1, source_target_pairs={{0,1},{1,0},{2,3},{3,2},{4,5},{5,4},{6,7},{7,6},{8,9},{9,8},{10,11... | collective-permute-start | bytes 12582920 | tf_op jit(solution)/shard_map/ppermute | solution.py:195
  495.5 162.2 %collective-permute-start.11 = (bf16[512,512]{1,0:T(8,128)(2,1)S(1)}, bf16[512,512]{1,0:T(8,128)(2,1)S(1)}, u32[]{:S(2)}, u32[]{:S(2)}) collective-permute-start(bf16[512,512]{1,0:T(8,128)(2,1)S(1)} %pad_maximum_fusion.2), channel_id=1, source_target_pairs={{8,0},{12,4},{16,24},{20,28},{9,1},{13,5},{17,25},{21,29},{10,2},{... | collective-permute-start | bytes 1572872 | tf_op jit(solution)/shard_map/ppermute | solution.py:192
  501.0 83.2 %collective-permute-start.30 = (bf16[512,512]{1,0:T(8,128)(2,1)S(1)}, bf16[512,512]{1,0:T(8,128)(2,1)S(1)}, u32[]{:S(2)}, u32[]{:S(2)}) collective-permute-start(bf16[512,512]{1,0:T(8,128)(2,1)S(1)} %pad_maximum_fusion.3), channel_id=1, source_target_pairs={{8,12},{12,8},{16,20},{20,16},{9,13},{13,9},{17,21},{21,17},{10,14... | collective-permute-start | bytes 1572872 | tf_op jit(solution)/shard_map/ppermute | solution.py:192
  505.8 79.1 %collective-permute-start.35 = (bf16[512,512]{1,0:T(8,128)(2,1)S(1)}, bf16[512,512]{1,0:T(8,128)(2,1)S(1)}, u32[]{:S(2)}, u32[]{:S(2)}) collective-permute-start(bf16[512,512]{1,0:T(8,128)(2,1)S(1)} %pad_maximum_fusion.4), channel_id=1, source_target_pairs={{8,4},{12,0},{16,28},{20,24},{9,5},{13,1},{17,29},{21,25},{10,6},{... | collective-permute-start | bytes 1572872 | tf_op jit(solution)/shard_map/ppermute | solution.py:192
  530.7 56.4 %collective-permute-start.36 = (bf16[512,512]{1,0:T(8,128)(2,1)S(1)}, bf16[512,512]{1,0:T(8,128)(2,1)S(1)}, u32[]{:S(2)}, u32[]{:S(2)}) collective-permute-start(bf16[512,512]{1,0:T(8,128)(2,1)S(1)} %shard_map.103), channel_id=1, source_target_pairs={{8,12},{12,8},{16,20},{20,16},{9,13},{13,9},{17,21},{21,17},{10,14... | collective-permute-start | bytes 1572872 | tf_op jit(solution)/shard_map/ppermute | solution.py:192
  538.2 75.4 %collective-permute-start.37 = (bf16[512,512]{1,0:T(8,128)(2,1)S(1)}, bf16[512,512]{1,0:T(8,128)(2,1)S(1)}, u32[]{:S(2)}, u32[]{:S(2)}) collective-permute-start(bf16[512,512]{1,0:T(8,128)(2,1)S(1)} %shard_map.104), channel_id=1, source_target_pairs={{8,4},{12,0},{16,28},{20,24},{9,5},{13,1},{17,29},{21,25},{10,6},{... | collective-permute-start | bytes 1572872 | tf_op jit(solution)/shard_map/ppermute | solution.py:192
  584.9 72.7 %collective-permute-start.39 = (bf16[512,256]{1,0:T(8,128)(2,1)S(1)}, bf16[512,256]{1,0:T(8,128)(2,1)S(1)}, u32[]{:S(2)}, u32[]{:S(2)}) collective-permute-start(bf16[512,256]{1,0:T(8,128)(2,1)S(1)} %shard_map.106), channel_id=1, source_target_pairs={{8,4},{12,0},{16,28},{20,24},{9,5},{13,1},{17,29},{21,25},{10,6},{... | collective-permute-start | bytes 786440 | tf_op jit(solution)/shard_map/ppermute | solution.py:192
  587.0 81.9 %collective-permute-start.19 = (bf16[512,512]{1,0:T(8,128)(2,1)S(1)}, bf16[512,512]{1,0:T(8,128)(2,1)S(1)}, u32[]{:S(2)}, u32[]{:S(2)}) collective-permute-start(bf16[512,512]{1,0:T(8,128)(2,1)S(1)} %shard_map.98), channel_id=1, source_target_pairs={{8,0},{12,4},{16,24},{20,28},{9,1},{13,5},{17,25},{21,29},{10,2},{... | collective-permute-start | bytes 1572872 | tf_op jit(solution)/shard_map/ppermute | solution.py:192
  613.5 59.4 %collective-permute-start.27 = (bf16[512,256]{1,0:T(8,128)(2,1)S(1)}, bf16[512,256]{1,0:T(8,128)(2,1)S(1)}, u32[]{:S(2)}, u32[]{:S(2)}) collective-permute-start(bf16[512,256]{1,0:T(8,128)(2,1)S(1)} %shard_map.100), channel_id=1, source_target_pairs={{8,0},{12,4},{16,24},{20,28},{9,1},{13,5},{17,25},{21,29},{10,2},{... | collective-permute-start | bytes 786440 | tf_op jit(solution)/shard_map/ppermute | solution.py:192
  (112 other events, 2728.6 us)

commit v2 on v0

--- a/solution.py
+++ b/solution.py
@@ -1,8 +1,11 @@
+import functools
 import math
 
 import jax
 import jax.numpy as jnp
 from jax import lax
+from jax.experimental import pallas as pl
+from jax.experimental.pallas import tpu as pltpu
 from jax.sharding import PartitionSpec as P
 
 HD = 128
@@ -10,6 +13,8 @@
 
 EPS = 1e-06
 THETA = 1000000.0
+QROWS = 128
+MAXLEN = 256
 
 
 def token_layout(prefix_lens, assignment, group_id, tok_rows):
@@ -49,7 +54,16 @@
     return jnp.dot(normed, portion, preferred_element_type=jnp.float32)
 
 
-def on_device(hidden, norm_gain, q_weight, q_bias, kv_weight, kv_bias, prefix_lens, assignment):
+def normalise(hidden, norm_gain):
+    widened = hidden.astype(jnp.float32)
+    return (
+        widened * lax.rsqrt(jnp.mean(widened * widened, axis=-1, keepdims=True) + EPS) * norm_gain
+    ).astype(jnp.bfloat16)
+
+
+def gathered_form(
+    hidden, norm_gain, q_weight, q_bias, kv_weight, kv_bias, prefix_lens, assignment
+):
     tok_rows, features = hidden.shape
     slice_rows = kv_weight.shape[0]
     q_cols = q_weight.shape[1]
@@ -57,10 +71,7 @@
     heads_here = q_cols // HD
     tensor_pos = lax.axis_index("tensor")
     kv_cols = kv_total // lax.axis_size("tensor")
-    widened = hidden.astype(jnp.float32)
-    normed = (
-        widened * lax.rsqrt(jnp.mean(widened * widened, axis=-1, keepdims=True) + EPS) * norm_gain
-    ).astype(jnp.bfloat16)
+    normed = normalise(hidden, norm_gain)
     queries = add_product(normed, lax.all_gather(q_weight, "group", axis=0, tiled=True)) + q_bias
     head_span = max(kv_cols, HD)
     head_base = tensor_pos * kv_cols // head_span * head_span
@@ -103,6 +114,305 @@
     return (context, kv_cache)
 
 
+def attention_kernel(q_ref, bias_ref, cos_ref, sin_ref, k_ref, v_ref, first_ref, out_ref):
+    rows, cols = out_ref.shape
+    heads = cols // HD
+    skip = q_ref.shape[1] - cols
+    cosine, sine = cos_ref[...], sin_ref[...]
+    turned = []
+    for head in range(heads):
+        at = head * HD
+        query = q_ref[:, skip + at : skip + at + HD] + bias_ref[:, at : at + HD]
+        query = query * cosine + pltpu.roll(query, HD // 2, 1) * sine
+        turned.append(query.astype(jnp.bfloat16))
+    for block in range(rows // QROWS):
+        top = block * QROWS
+        low = max(0, top - MAXLEN)
+        end = top + QROWS
+        span = end - low
+        stacked = jnp.concatenate([query[top:end] for query in turned], axis=0)
+        scores = lax.dot_general(
+            stacked, k_ref[low:end], (((1,), (1,)), ((), ())), preferred_element_type=jnp.float32
+        ) * (1.0 / math.sqrt(HD))
+        row = lax.broadcasted_iota(jnp.int32, (QROWS, span), 0) + top
+        col = lax.broadcasted_iota(jnp.int32, (QROWS, span), 1) + low
+        visible = (col <= row) & (col >= first_ref[top:end])
+        scores = jnp.where(visible[None], scores.reshape(heads, QROWS, span), -jnp.inf)
+        exponent = jnp.exp(scores - jnp.max(scores, axis=-1, keepdims=True))
+        weights = (exponent / jnp.sum(exponent, axis=-1, keepdims=True)).astype(jnp.bfloat16)
+        context = jnp.dot(
+            weights.reshape(heads * QROWS, span), v_ref[low:end], preferred_element_type=jnp.float32
+        ).astype(jnp.bfloat16)
+        for head in range(heads):
+            out_ref[top:end, head * HD : (head + 1) * HD] = context[
+                head * QROWS : (head + 1) * QROWS
+            ]
+
+
+def attend(queries, heads, bias, cosine, sine, keys, values, first):
+    rows = queries.shape[0]
+    return pl.pallas_call(
+        attention_kernel,
+        out_shape=jax.ShapeDtypeStruct((rows, heads * HD), jnp.bfloat16),
+        compiler_params=pltpu.CompilerParams(vmem_limit_bytes=40 * 2**20),
+        cost_estimate=pl.CostEstimate(
+            flops=4 * heads * rows * 3 * QROWS * HD,
+            bytes_accessed=rows * heads * HD * 6 + rows * HD * 12,
+            transcendentals=heads * rows * 3 * QROWS,
+        ),
+    )(queries, bias, cosine, sine, keys, values, first)
+
+
+def project_kernel(count, at_ref, *refs):
+    blocks, pieces = refs[:count], refs[count : 2 * count]
+    out_ref = refs[-1]
+    total = None if len(refs) == 2 * count + 1 else refs[2 * count][...]
+    for block, piece in zip(blocks, pieces):
+        weight = piece[...].reshape(piece.shape[-2:])
+        term = jnp.dot(block[0], weight, preferred_element_type=jnp.float32)
+        total = term if total is None else total + term
+    out_ref[...] = total
+
+
+def project(rows, at, pieces, width, total=None):
+    count = len(pieces)
+    tokens, depth = rows.shape[1], pieces[0][0].shape[-2]
+    tile = 2 * HD
+    in_specs = [
+        pl.BlockSpec((1, tokens, depth), functools.partial(lambda p, j, at: (at[0, p], 0, at[1, p]), p))
+        for p in range(count)
+    ]
+    for array, lead, skip in pieces:
+        if array.ndim == 3:
+            in_specs.append(
+                pl.BlockSpec(
+                    (1, depth, tile),
+                    functools.partial(lambda l, s, j, at: (l, 0, j + s), lead, skip // tile),
+                )
+            )
+        else:
+            in_specs.append(
+                pl.BlockSpec(
+                    (depth, tile), functools.partial(lambda s, j, at: (0, j + s), skip // tile)
+                )
+            )
+    operands = [rows] * count + [array for array, _, _ in pieces]
+    if total is not None:
+        in_specs.append(pl.BlockSpec((tokens, tile), lambda j, at: (0, j)))
+        operands.append(total)
+    return pl.pallas_call(
+        functools.partial(project_kernel, count),
+        grid_spec=pltpu.PrefetchScalarGridSpec(
+            num_scalar_prefetch=1,
+            grid=(width // tile,),
+            in_specs=in_specs,
+            out_specs=pl.BlockSpec((tokens, tile), lambda j, at: (0, j)),
+        ),
+        out_shape=jax.ShapeDtypeStruct((tokens, width), jnp.float32),
+        compiler_params=pltpu.CompilerParams(vmem_limit_bytes=48 * 2**20),
+        cost_estimate=pl.CostEstimate(
+            flops=2 * count * tokens * depth * width,
+            bytes_accessed=2 * count * depth * (tokens + width) + 8 * tokens * width,
+            transcendentals=0,
+        ),
+    )(at, *operands)
+
+
+MIDDLE = (2, 3, 4, 5)
+ENDS = (0, 1, 6, 7)
+FIRST_CODES = (0, 1, 6, 7)
+LAST_CODES = (2, 3, 4, 5)
+
+
+def pairs_from(sources, code):
+    return [(s, s ^ code) for s in sources]
+
+
+def after(value, *others):
+    return lax.optimization_barrier((value,) + others)[0]
+
+
+def middle_form(hidden, norm_gain, q_weight, q_bias, kv_weight, kv_bias, prefix_lens, assignment):
+    tok_rows, features = hidden.shape
+    slice_rows, q_cols = q_weight.shape
+    half_cols = q_cols // 2
+    group = lax.axis_index("group")
+    tensor = lax.axis_index("tensor")
+    core = tensor & 1
+    y = group & 1
+    is_middle = (group >= 2) & (group < 6)
+
+    def over_group(value, sources, code):
+        return lax.ppermute(value, "group", pairs_from(sources, code))
+
+    def over_y(value):
+        return over_group(value, range(8), 1)
+
+    def to_middle(value):
+        return over_group(value, ENDS, 2)
+
+    def across_middle(value):
+        return over_group(value, MIDDLE, 6)
+
+    def over_x(value):
+        return lax.ppermute(value, "tensor", pairs_from(range(4), 2))
+
+    def over_core(value):
+        return lax.ppermute(value, "tensor", pairs_from(range(4), 1))
+
+    heads = (2, 4, 2)
+    cut = heads[0] * HD
+
+    def columns(half):
+        head = (2 * tensor + half) * HD
+        kv_part = lax.dynamic_slice_in_dim(kv_weight, head, HD, 2).reshape(slice_rows, 2 * HD)
+        early = lax.dynamic_slice_in_dim(q_weight, half * half_cols, cut, 1)
+        late = lax.dynamic_slice_in_dim(q_weight, half * half_cols + cut, half_cols - cut, 1)
+        return jnp.concatenate([kv_part, early], axis=1), late
+
+    own0, own12 = columns(y)
+    other0, other12 = columns(1 - y)
+    mid_cols = heads[1] * HD
+
+    m_own0 = across_middle(own0)
+    swap0 = over_y(other0)
+    normed = normalise(hidden, norm_gain)
+    quarter = lax.dynamic_slice_in_dim(normed, tensor * (features // 4), features // 4, 1)
+    half = lax.dynamic_slice_in_dim(normed, core * (features // 2), features // 2, 1)
+    end2 = to_middle(quarter)
+    m_swap0 = across_middle(swap0)
+    swap12 = over_y(after(other12, swap0, m_own0))
+    m_own12 = across_middle(after(own12, m_own0))
+    e0 = to_middle(after(jnp.stack([own0, swap0]), end2))
+    across2 = over_x(end2)
+    m_swap12 = across_middle(after(swap12, m_swap0))
+    end3 = over_group(after(end2, swap12), MIDDLE, 1)
+
+    def whole(near, across):
+        both = jnp.stack([near, across])
+        return jnp.concatenate([both, over_core(both)])
+
+    rows0 = normed[None]
+    rows2 = whole(end2, across2)
+
+    def spots(codes, places):
+        block = jnp.stack([group ^ code for code in codes])
+        if places == 1:
+            return jnp.stack([block * 0, block])
+        if places == 2:
+            return jnp.stack([(block >> 2) ^ core, block & 3])
+        apart = (block >> 1) ^ tensor
+        return jnp.stack([(apart >> 1) | ((apart & 1) << 1), block & 1])
+
+    places_of = (1, 2, 4, 4)
+    first_at = [spots(FIRST_CODES, n) for n in places_of]
+    last_at = [spots(LAST_CODES, n) for n in places_of]
+
+    first0 = [(own0, 0, 0), (swap0, 0, 0), (m_own0, 0, 0), (m_swap0, 0, 0)]
+    first1 = [(own12, 0, 0), (swap12, 0, 0), (m_own12, 0, 0), (m_swap12, 0, 0)]
+    first2 = [(array, 0, mid_cols) for array, _, _ in first1]
+    firsts = (first0, first1, first2)
+    widths = (2 * HD + cut, mid_cols, heads[2] * HD)
+
+    def first_part(code, rows, chunk):
+        return project(rows, first_at[code], firsts[chunk], widths[chunk])
+
+    sums = {}
+    sums[0, 0] = first_part(0, rows0, 0)
+    m_e0 = across_middle(after(e0, m_own12, sums[0, 0]))
+    late = jnp.stack([own12, swap12])
+    e1 = to_middle(after(late[:, :, :mid_cols], e0))
+    across3 = over_x(after(end3, across2))
+    beside_half = over_group(after(half, end3), MIDDLE, 1)
+    for chunk in (1, 2):
+        sums[0, chunk] = first_part(0, rows0, chunk)
+    for chunk in range(3):
+        sums[2, chunk] = first_part(2, rows2, chunk)
+    rows3 = whole(end3, across3)
+    m_e1 = across_middle(after(e1, m_swap12, *[sums[0, c] for c in (1, 2)], *[sums[2, c] for c in range(3)]))
+    e2 = to_middle(after(late[:, :, mid_cols:], e1))
+    for chunk in range(3):
+        sums[3, chunk] = first_part(3, rows3, chunk)
+
+    bias = lax.dynamic_slice_in_dim(q_bias, y * half_cols, half_cols, 0)[None, :]
+    kv_bias_here = lax.dynamic_slice_in_dim(kv_bias, (2 * tensor + y) * HD, HD, 1)
+    inverse_freq = THETA ** (-2.0 * jnp.arange(HD // 2, dtype=jnp.float32) / HD)
+    tables = []
+    for code in range(4):
+        _, offset, places = token_layout(prefix_lens, assignment, group ^ code, tok_rows)
+        angles = offset.astype(jnp.float32)[:, None] * inverse_freq[None, :]
+        cosine, sine = jnp.cos(angles), jnp.sin(angles)
+        cosine = jnp.concatenate([cosine, cosine], axis=1)
+        sine = jnp.concatenate([-sine, sine], axis=1)
+        tables.append((cosine, sine, (places - offset)[:, None]))
+
+    last0 = [(e0, 0, 0), (e0, 1, 0), (m_e0, 0, 0), (m_e0, 1, 0)]
+    keys_values, outs = {}, {}
+
+    def finish(code, rows, chunk, lasts, total, place):
+        total = project(rows, last_at[code], lasts, widths[chunk], total)
+        cosine, sine, first = tables[code]
+        if chunk == 0:
+            keys = total[:, :HD] + kv_bias_here[0]
+            swapped = jnp.concatenate([keys[:, HD // 2 :], keys[:, : HD // 2]], axis=1)
+            keys = (keys * cosine + swapped * sine).astype(jnp.bfloat16)
+            values = (total[:, HD : 2 * HD] + kv_bias_here[1]).astype(jnp.bfloat16)
+            keys_values[code] = (keys, values)
+        keys, values = keys_values[code]
+        out = attend(
+            total,
+            heads[chunk],
+            bias[:, place : place + heads[chunk] * HD],
+            cosine,
+            sine,
+            keys,
+            values,
+            first,
+        )
+        outs[code, chunk] = jnp.concatenate([keys, values, out], axis=1) if chunk == 0 else out
+
+    def send_back(chunk):
+        return (
+            over_group(outs[1, chunk], MIDDLE, 1),
+            over_group(outs[2, chunk], MIDDLE, 2),
+            over_group(outs[3, chunk], MIDDLE, 3),
+        )
+
+    for code, rows in ((0, rows0), (2, rows2), (3, rows3)):
+        finish(code, rows, 0, last0, sums[code, 0], 0)
+    m_e2 = across_middle(after(e2, m_e0, *[outs[c, 0] for c in (0, 2, 3)]))
+    rows1 = jnp.stack([beside_half, over_core(beside_half)])
+    for chunk in range(3):
+        sums[1, chunk] = first_part(1, rows1, chunk)
+    finish(1, rows1, 0, last0, sums[1, 0], 0)
+    all_rows = (rows0, rows1, rows2, rows3)
+    back = [send_back(0)]
+    last1 = [(e1, 0, 0), (e1, 1, 0), (m_e1, 0, 0), (m_e1, 1, 0)]
+    last2 = [(e2, 0, 0), (e2, 1, 0), (m_e2, 0, 0), (m_e2, 1, 0)]
+    for chunk, lasts, place in ((1, last1, cut), (2, last2, cut + mid_cols)):
+        for code in (2, 3, 1, 0):
+            finish(code, all_rows[code], chunk, lasts, sums[code, chunk], place)
+        back.append(send_back(chunk))
+
+    mine, its = [], []
+    for chunk in range(3):
+        beside, back_own, back_other = back[chunk]
+        mine.append(jnp.where(is_middle, outs[0, chunk], back_own))
+        its.append(jnp.where(is_middle, beside, back_other))
+
+    def in_order(a, b):
+        return jnp.where(y == 0, jnp.concatenate([a, b], axis=-1), jnp.concatenate([b, a], axis=-1))
+
+    context = in_order(
+        jnp.concatenate([mine[0][:, 2 * HD :]] + mine[1:], axis=1),
+        jnp.concatenate([its[0][:, 2 * HD :]] + its[1:], axis=1),
+    )
+    kv_cache = in_order(
+        mine[0][:, : 2 * HD].reshape(tok_rows, 2, HD), its[0][:, : 2 * HD].reshape(tok_rows, 2, HD)
+    )
+    return (context, kv_cache)
+
+
 def solution(mesh):
     placed = (
         P("group", None),
@@ -114,8 +424,9 @@
         P(),
         P(),
     )
+    fits = mesh.shape["group"] == 8 and mesh.shape["tensor"] == 4
     return jax.shard_map(
-        on_device,
+        middle_form if fits else gathered_form,
         mesh=mesh,
         in_specs=placed,
         out_specs=(P("group", "tensor"), P("group", None, "tensor")),

time: 846 us -> 499 us (0.59)
  the two profiles are of different devices: /device:TPU:0 before, /device:TPU:20 now
where the time goes in v2:
time: 499 us; the launch traced here: 490 us
  waiting for transfers between devices  157 us (31%)
  Pallas kernels  155 us (31%)
  other arithmetic  85.4 us (17%)
  starting transfers between devices  57.6 us (12%)
  local copies, waits for them, and re-layouts  31.3 us (6%)
    pallas_call x24, Pallas kernels, project(): pl.pallas_call(functools.partial(project_kernel, count), grid_spec=pltpu....  129 us
    ppermute x24, waiting for transfers between devices, over_group(): return lax.ppermute(value, 'group', pairs_from(sources, code))  103 us
    ppermute x24, starting transfers between devices, over_group(): return lax.ppermute(value, 'group', pairs_from(sources, code))  54.5 us
    ppermute x2, waiting for transfers between devices, over_x(): return lax.ppermute(value, 'tensor', pairs_from(range(4), 2))  54 us
    pallas_call x12, Pallas kernels, attend(): pl.pallas_call(attention_kernel, out_shape=jax.ShapeDtypeStruct((rows, he...  25.8 us
    concatenate x2, other arithmetic, whole(): return jnp.concatenate([both, over_core(both)])  14.5 us
  transfers between devices with their start and end apart: 29, of which 9 were waited for; matrix products, arithmetic and copies ran while one was open for 20% of the time, Pallas kernels for 32%

profile of v2, /device:TPU:20, one launch (start us, length us, event | category | flops | bytes accessed | tf_op | source)
XLA Modules:
  0.0 489.5 jit_solution(5148072799218145082)
XLA Ops:
  9.1 5.1 %fusion = f32[512]{0:T(512)S(1)} fusion(bf16[512,8192]{1,0:T(8,128)(2,1)} %param.8), kind=kLoop, calls=%fused_computation.2 | loop fusion | flops 12582400 | bytes 8390656 | tf_op jit(solution)/shard_map/reduce_sum | solution.py:60
  14.2 10.0 %fusion.2 = bf16[512,8192]{1,0:T(8,128)(2,1)} fusion(bf16[512,8192]{1,0:T(8,128)(2,1)} %param.8, f32[8192]{0:T(1024)S(1)} %copy-done.82, f32[512]{0:T(512)S(1)} %add_rsqrt_fusion), kind=kLoop, calls=%fused_computation.4 | loop fusion | flops 16777216 | bytes 16812032 | tf_op jit(solution)/shard_map/convert_element_type | solution.py:61
  34.0 42.3 %collective-permute-done.1 = bf16[512,2048]{1,0:T(8,128)(2,1)} collective-permute-done((bf16[512,2048]{1,0:T(8,128)(2,1)}, bf16[512,2048]{1,0:T(8,128)(2,1)}, u32[]{:S(2)}, u32[]{:S(2)}) %collective-permute-start.1) | collective-permute-done | bytes 2097184 | tf_op jit(solution)/shard_map/ppermute | solution.py:246
  81.3 4.8 constant_dynamic-slice_fusion
  93.6 29.0 %collective-permute-done.7 = bf16[512,2048]{1,0:T(8,128)(2,1)} collective-permute-done((bf16[512,2048]{1,0:T(8,128)(2,1)}, bf16[512,2048]{1,0:T(8,128)(2,1)}, u32[]{:S(2)}, u32[]{:S(2)}) %collective-permute-start.7) | collective-permute-done | bytes 2097184 | tf_op jit(solution)/shard_map/ppermute | solution.py:258
  122.5 4.7 pad_maximum_fusion.3
  132.2 10.0 %fusion.52.refs_0_.refs_1_.refs_2_.refs_3_ = bf16[1,512,8192]{2,1,0:T(8,128)(2,1)} fusion(f32[8192]{0:T(1024)S(1)} %copy-done.82, f32[512]{0:T(512)S(1)} %add_rsqrt_fusion, bf16[512,8192]{1,0:T(8,128)(2,1)} %param.8), kind=kLoop, calls=%fused_computation.164 | loop fusion | flops 16777216 | bytes 16812032 | tf_op jit(solution)/shard_map/broadcast_in_dim | solution.py:295
  150.6 25.0 %collective-permute-done.17 = bf16[512,2048]{1,0:T(8,128)(2,1)} collective-permute-done((bf16[512,2048]{1,0:T(8,128)(2,1)}, bf16[512,2048]{1,0:T(8,128)(2,1)}, u32[]{:S(2)}, u32[]{:S(2)}) %collective-permute-start.17) | collective-permute-done | bytes 2097184 | tf_op jit(solution)/shard_map/ppermute | solution.py:258
  176.9 4.6 pad_maximum_fusion.4
  181.7 5.9 %shard_map.95.refs_8_ = f32[512,512]{1,0:T(8,128)S(1)} custom-call(s32[2,4]{1,0:T(2,128)S(1)} %stack.179.at_ref, bf16[1,512,8192]{2,1,0:T(8,128)(2,1)} %fusion.52.refs_0_.refs_1_.refs_2_.refs_3_, bf16[1,512,8192]{2,1,0:T(8,128)(2,1)} %fusion.52.refs_0_.refs_1_.refs_2_.refs_3_, bf16[1,512,8192]{2,1,0:T(8,128)(2,1)} %fusion.52.refs_0_.refs_1_.refs_2_.refs_3_, ...), custom_call_target="tpu_custom_call" | custom-call | flops 2147483648 | bytes 10485760 | tf_op jit(solution)/shard_map/pallas_call | solution.py:203
  188.7 25.5 %collective-permute-done.12.refs_7_ = bf16[1024,768]{1,0:T(8,128)(2,1)S(1)} collective-permute-done((bf16[1024,768]{1,0:T(8,128)(2,1)S(1)}, bf16[1024,768]{1,0:T(8,128)(2,1)S(1)}, u32[]{:S(2)}, u32[]{:S(2)}) %collective-permute-start.12) | collective-permute-done | bytes 1572896 | tf_op jit(solution)/shard_map/ppermute | solution.py:246
  217.7 4.3 shard_map.102.refs_8_
  222.8 5.8 %shard_map.101.refs_8_ = f32[512,512]{1,0:T(8,128)S(1)} custom-call(s32[2,4]{1,0:T(2,128)S(1)} %stack.179.at_ref, bf16[1,512,8192]{2,1,0:T(8,128)(2,1)} %fusion.52.refs_0_.refs_1_.refs_2_.refs_3_, bf16[1,512,8192]{2,1,0:T(8,128)(2,1)} %fusion.52.refs_0_.refs_1_.refs_2_.refs_3_, bf16[1,512,8192]{2,1,0:T(8,128)(2,1)} %fusion.52.refs_0_.refs_1_.refs_2_.refs_3_, ...), custom_call_target="tpu_custom_call" | custom-call | flops 2147483648 | bytes 10485760 | tf_op jit(solution)/shard_map/pallas_call | solution.py:203
  229.6 7.1 %pad_maximum_fusion.refs_0_.refs_1_.refs_2_.refs_3_ = bf16[4,512,2048]{2,1,0:T(8,128)(2,1)} fusion(bf16[2,512,2048]{2,1,0:T(8,128)(2,1)} %collective-permute-done.8, bf16[1,512,2048]{2,1,0:T(8,128)(2,1)} %bitcast.23, bf16[1,512,2048]{2,1,0:T(8,128)(2,1)} %bitcast.22), kind=kLoop, calls=%fused_computation.5 | loop fusion | flops 8388608 | bytes 16777216 | tf_op jit(solution)/shard_map/concatenate | solution.py:293
  236.6 5.9 %shard_map.98.refs_8_ = f32[512,512]{1,0:T(8,128)S(1)} custom-call(s32[2,4]{1,0:T(2,128)S(1)} %pad_add_fusion.1.at_ref, bf16[4,512,2048]{2,1,0:T(8,128)(2,1)} %pad_maximum_fusion.refs_0_.refs_1_.refs_2_.refs_3_, bf16[4,512,2048]{2,1,0:T(8,128)(2,1)} %pad_maximum_fusion.refs_0_.refs_1_.refs_2_.refs_3_, ...), custom_call_target="tpu_custom_call" | custom-call | flops 2147483648 | bytes 10485760 | tf_op jit(solution)/shard_map/pallas_call | solution.py:203
  242.7 5.8 %shard_map.103.refs_8_ = f32[512,512]{1,0:T(8,128)S(1)} custom-call(s32[2,4]{1,0:T(2,128)S(1)} %pad_add_fusion.1.at_ref, bf16[4,512,2048]{2,1,0:T(8,128)(2,1)} %pad_maximum_fusion.refs_0_.refs_1_.refs_2_.refs_3_, bf16[4,512,2048]{2,1,0:T(8,128)(2,1)} %pad_maximum_fusion.refs_0_.refs_1_.refs_2_.refs_3_, ...), custom_call_target="tpu_custom_call" | custom-call | flops 2147483648 | bytes 10485760 | tf_op jit(solution)/shard_map/pallas_call | solution.py:203
  258.9 5.4 %fusion.27 = (f32[512,64]{1,0:T(8,128)}, f32[512,64]{1,0:T(8,128)}, f32[512,64]{1,0:T(8,128)}, f32[512,64]{1,0:T(8,128)}, f32[512,64]{1,0:T(8,128)}, /*index=5*/...) fusion(f32[64]{0:T(128)S(1)} %multiply_power_fusion, ...), kind=kLoop, calls=%fused_computation.86 | loop fusion | flops 262144 | bytes 1581312 | tf_op jit(solution)/shard_map/neg | solution.py:346
  267.2 6.1 %shard_map.96.q_ref = f32[512,512]{1,0:T(8,128)S(1)} custom-call(s32[2,4]{1,0:T(2,128)S(1)} %stack.169.at_ref, bf16[1,512,8192]{2,1,0:T(8,128)(2,1)} %fusion.52.refs_0_.refs_1_.refs_2_.refs_3_, bf16[1,512,8192]{2,1,0:T(8,128)(2,1)} %fusion.52.refs_0_.refs_1_.refs_2_.refs_3_, bf16[1,512,8192]{2,1,0:T(8,128)(2,1)} %fusion.52.refs_0_.refs_1_.refs_2_.refs_3_, ...), custom_call_target="tpu_custom_call" | custom-call | flops 2147483648 | bytes 10485760 | tf_op jit(solution)/shard_map/pallas_call | solution.py:203
  273.3 6.1 %shard_map.99.q_ref = f32[512,512]{1,0:T(8,128)S(1)} custom-call(s32[2,4]{1,0:T(2,128)S(1)} %pad_add_fusion.at_ref, bf16[4,512,2048]{2,1,0:T(8,128)(2,1)} %pad_maximum_fusion.refs_0_.refs_1_.refs_2_.refs_3_, bf16[4,512,2048]{2,1,0:T(8,128)(2,1)} %pad_maximum_fusion.refs_0_.refs_1_.refs_2_.refs_3_, ...), custom_call_target="tpu_custom_call" | custom-call | flops 2147483648 | bytes 10485760 | tf_op jit(solution)/shard_map/pallas_call | solution.py:203
  279.4 28.5 %collective-permute-done.13.refs_6_.refs_7_ = bf16[2,1024,512]{2,1,0:T(8,128)(2,1)} collective-permute-done((bf16[2,1024,512]{2,1,0:T(8,128)(2,1)}, bf16[2,1024,512]{2,1,0:T(8,128)(2,1)}, u32[]{:S(2)}, u32[]{:S(2)}) %collective-permute-start.13) | collective-permute-done | bytes 2097184 | tf_op jit(solution)/shard_map/ppermute | solution.py:246
  308.0 6.1 %shard_map.107.q_ref = f32[512,512]{1,0:T(8,128)S(1)} custom-call(s32[2,4]{1,0:T(2,128)S(1)} %pad_add_fusion.at_ref, bf16[4,512,2048]{2,1,0:T(8,128)(2,1)} %pad_maximum_fusion.refs_0_.refs_1_.refs_2_.refs_3_, bf16[4,512,2048]{2,1,0:T(8,128)(2,1)} %pad_maximum_fusion.refs_0_.refs_1_.refs_2_.refs_3_, ...), custom_call_target="tpu_custom_call" | custom-call | flops 2147483648 | bytes 10485760 | tf_op jit(solution)/shard_map/pallas_call | solution.py:203
  315.0 6.1 %shard_map.105.q_ref = f32[512,512]{1,0:T(8,128)S(1)} custom-call(s32[2,4]{1,0:T(2,128)S(1)} %stack.169.at_ref, bf16[1,512,8192]{2,1,0:T(8,128)(2,1)} %fusion.52.refs_0_.refs_1_.refs_2_.refs_3_, bf16[1,512,8192]{2,1,0:T(8,128)(2,1)} %fusion.52.refs_0_.refs_1_.refs_2_.refs_3_, bf16[1,512,8192]{2,1,0:T(8,128)(2,1)} %fusion.52.refs_0_.refs_1_.refs_2_.refs_3_, ...), custom_call_target="tpu_custom_call" | custom-call | flops 2147483648 | bytes 10485760 | tf_op jit(solution)/shard_map/pallas_call | solution.py:203
  321.1 7.4 %pad_maximum_fusion.1.refs_0_.refs_1_.refs_2_.refs_3_ = bf16[4,512,2048]{2,1,0:T(8,128)(2,1)} fusion(bf16[2,512,2048]{2,1,0:T(8,128)(2,1)} %collective-permute-done.18, bf16[1,512,2048]{2,1,0:T(8,128)(2,1)} %bitcast.33, bf16[1,512,2048]{2,1,0:T(8,128)(2,1)} %bitcast.32), kind=kLoop, calls=%fused_computation.6 | loop fusion | flops 8388608 | bytes 16777216 | tf_op jit(solution)/shard_map/concatenate | solution.py:293
  332.9 5.9 %shard_map.109.refs_8_ = f32[512,512]{1,0:T(8,128)S(1)} custom-call(s32[2,4]{1,0:T(2,128)S(1)} %pad_add_fusion.1.at_ref, bf16[4,512,2048]{2,1,0:T(8,128)(2,1)} %pad_maximum_fusion.1.refs_0_.refs_1_.refs_2_.refs_3_, bf16[4,512,2048]{2,1,0:T(8,128)(2,1)} %pad_maximum_fusion.1.refs_0_.refs_1_.refs_2_.refs_3_, ...), custom_call_target="tpu_custom_call" | custom-call | flops 2147483648 | bytes 10485760 | tf_op jit(solution)/shard_map/pallas_call | solution.py:203
  338.8 5.8 %shard_map.122.refs_8_ = f32[512,512]{1,0:T(8,128)S(1)} custom-call(s32[2,4]{1,0:T(2,128)S(1)} %pad_add_fusion.1.at_ref, bf16[4,512,2048]{2,1,0:T(8,128)(2,1)} %pad_maximum_fusion.1.refs_0_.refs_1_.refs_2_.refs_3_, bf16[4,512,2048]{2,1,0:T(8,128)(2,1)} %pad_maximum_fusion.1.refs_0_.refs_1_.refs_2_.refs_3_, ...), custom_call_target="tpu_custom_call" | custom-call | flops 2147483648 | bytes 10485760 | tf_op jit(solution)/shard_map/pallas_call | solution.py:203
  344.6 6.1 %shard_map.110.q_ref = f32[512,512]{1,0:T(8,128)S(1)} custom-call(s32[2,4]{1,0:T(2,128)S(1)} %pad_add_fusion.at_ref, bf16[4,512,2048]{2,1,0:T(8,128)(2,1)} %pad_maximum_fusion.1.refs_0_.refs_1_.refs_2_.refs_3_, bf16[4,512,2048]{2,1,0:T(8,128)(2,1)} %pad_maximum_fusion.1.refs_0_.refs_1_.refs_2_.refs_3_, ...), custom_call_target="tpu_custom_call" | custom-call | flops 2147483648 | bytes 10485760 | tf_op jit(solution)/shard_map/pallas_call | solution.py:203
  351.7 6.1 %shard_map.123.q_ref = f32[512,512]{1,0:T(8,128)S(1)} custom-call(s32[2,4]{1,0:T(2,128)S(1)} %pad_add_fusion.at_ref, bf16[4,512,2048]{2,1,0:T(8,128)(2,1)} %pad_maximum_fusion.1.refs_0_.refs_1_.refs_2_.refs_3_, bf16[4,512,2048]{2,1,0:T(8,128)(2,1)} %pad_maximum_fusion.1.refs_0_.refs_1_.refs_2_.refs_3_, ...), custom_call_target="tpu_custom_call" | custom-call | flops 2147483648 | bytes 10485760 | tf_op jit(solution)/shard_map/pallas_call | solution.py:203
  358.8 7.5 %pad_maximum_fusion.2.refs_0_.refs_1_.refs_2_.refs_3_ = bf16[2,512,4096]{2,1,0:T(8,128)(2,1)} fusion(bf16[1,512,4096]{2,1,0:T(8,128)(2,1)} %bitcast.37, bf16[1,512,4096]{2,1,0:T(8,128)(2,1)} %bitcast.36), kind=kLoop, calls=%fused_computation.7 | loop fusion | flops 4194304 | bytes 16777216 | tf_op jit(solution)/shard_map/stack | solution.py:384
  366.3 5.9 %shard_map.116.refs_8_ = f32[512,512]{1,0:T(8,128)S(1)} custom-call(s32[2,4]{1,0:T(2,128)S(1)} %pad_add_fusion.3.at_ref, bf16[2,512,4096]{2,1,0:T(8,128)(2,1)} %pad_maximum_fusion.2.refs_0_.refs_1_.refs_2_.refs_3_, bf16[2,512,4096]{2,1,0:T(8,128)(2,1)} %pad_maximum_fusion.2.refs_0_.refs_1_.refs_2_.refs_3_, ...), custom_call_target="tpu_custom_call" | custom-call | flops 2147483648 | bytes 10485760 | tf_op jit(solution)/shard_map/pallas_call | solution.py:203
  372.2 6.3 %shard_map.117.q_ref = f32[512,512]{1,0:T(8,128)S(1)} custom-call(s32[2,4]{1,0:T(2,128)S(1)} %pad_add_fusion.2.at_ref, bf16[2,512,4096]{2,1,0:T(8,128)(2,1)} %pad_maximum_fusion.2.refs_0_.refs_1_.refs_2_.refs_3_, bf16[2,512,4096]{2,1,0:T(8,128)(2,1)} %pad_maximum_fusion.2.refs_0_.refs_1_.refs_2_.refs_3_, ...), custom_call_target="tpu_custom_call" | custom-call | flops 2147483648 | bytes 10485760 | tf_op jit(solution)/shard_map/pallas_call | solution.py:203
  397.4 6.0 %shard_map.119.refs_8_ = f32[512,512]{1,0:T(8,128)S(1)} custom-call(s32[2,4]{1,0:T(2,128)S(1)} %copy-done.57, bf16[2,512,4096]{2,1,0:T(8,128)(2,1)} %pad_maximum_fusion.2.refs_0_.refs_1_.refs_2_.refs_3_, bf16[2,512,4096]{2,1,0:T(8,128)(2,1)} %pad_maximum_fusion.2.refs_0_.refs_1_.refs_2_.refs_3_, ...), custom_call_target="tpu_custom_call" | custom-call | flops 2147483648 | bytes 10485760 | tf_op jit(solution)/shard_map/pallas_call | solution.py:203
  403.4 6.1 %shard_map.120.q_ref = f32[512,512]{1,0:T(8,128)S(1)} custom-call(s32[2,4]{1,0:T(2,128)S(1)} %pad_add_fusion.2.at_ref, bf16[2,512,4096]{2,1,0:T(8,128)(2,1)} %pad_maximum_fusion.2.refs_0_.refs_1_.refs_2_.refs_3_, bf16[2,512,4096]{2,1,0:T(8,128)(2,1)} %pad_maximum_fusion.2.refs_0_.refs_1_.refs_2_.refs_3_, ...), custom_call_target="tpu_custom_call" | custom-call | flops 2147483648 | bytes 10485760 | tf_op jit(solution)/shard_map/pallas_call | solution.py:203
  (328 shorter events, 169.7 us)
Async XLA Ops:
  0.6 141.5 %copy-start = (f32[2,1024]{1,0:T(2,128)S(1)}, f32[2,1024]{1,0:T(2,128)}, u32[]{:S(2)}) copy-start(f32[2,1024]{1,0:T(2,128)} %param.13) | copy-start | bytes 24580
  5.1 26.9 %collective-permute-start.3 = (bf16[1024,512]{1,0:T(8,128)(2,1)S(1)}, bf16[1024,512]{1,0:T(8,128)(2,1)}, u32[]{:S(2)}, u32[]{:S(2)}) collective-permute-start(bf16[1024,512]{1,0:T(8,128)(2,1)S(1)} %get-tuple-element.62.refs_4_), channel_id=1, source_target_pairs={{8,16},{12,20},{16,8},{20,12},{9,17},{13,21},{17,9},{21,13},{10,18... | collective-permute-start | bytes 3145736 | tf_op jit(solution)/shard_map/ppermute | solution.py:246
  8.6 24.9 %collective-permute-start = (bf16[1024,512]{1,0:T(8,128)(2,1)}, bf16[1024,512]{1,0:T(8,128)(2,1)}, u32[]{:S(2)}, u32[]{:S(2)}) collective-permute-start(bf16[1024,512]{1,0:T(8,128)(2,1)} %pad_maximum_fusion.8), channel_id=1, source_target_pairs={{0,4},{4,0},{8,12},{12,8},{16,20},{20,16},{24,28},{28,24},{1,5},{5... | collective-permute-start | bytes 3145736 | tf_op jit(solution)/shard_map/ppermute | solution.py:246
  27.3 49.0 %collective-permute-start.1 = (bf16[512,2048]{1,0:T(8,128)(2,1)}, bf16[512,2048]{1,0:T(8,128)(2,1)}, u32[]{:S(2)}, u32[]{:S(2)}) collective-permute-start(bf16[512,2048]{1,0:T(8,128)(2,1)} %constant_dynamic-slice_fusion.4), channel_id=1, source_target_pairs={{0,8},{4,12},{24,16},{28,20},{1,9},{5,13},{25,17},{29,21},{2,10},{... | collective-permute-start | bytes 6291464 | tf_op jit(solution)/shard_map/ppermute | solution.py:246
  33.5 44.3 %collective-permute-start.10 = (bf16[1024,768]{1,0:T(8,128)(2,1)S(1)}, bf16[1024,768]{1,0:T(8,128)(2,1)S(1)}, u32[]{:S(2)}, u32[]{:S(2)}) collective-permute-start(bf16[1024,768]{1,0:T(8,128)(2,1)S(1)} %get-tuple-element.17), channel_id=1, source_target_pairs={{0,4},{4,0},{8,12},{12,8},{16,20},{20,16},{24,28},{28,24},{1,5},{5... | collective-permute-start | bytes 4718600 | tf_op jit(solution)/shard_map/ppermute | solution.py:246
  76.3 46.2 %collective-permute-start.7 = (bf16[512,2048]{1,0:T(8,128)(2,1)}, bf16[512,2048]{1,0:T(8,128)(2,1)}, u32[]{:S(2)}, u32[]{:S(2)}) collective-permute-start(bf16[512,2048]{1,0:T(8,128)(2,1)} %collective-permute-done.1), channel_id=1, source_target_pairs={{0,2},{1,3},{2,0},{3,1},{4,6},{5,7},{6,4},{7,5},{8,10},{9,11},{10,... | collective-permute-start | bytes 6291464 | tf_op jit(solution)/shard_map/ppermute | solution.py:258
  77.8 49.4 %collective-permute-start.16 = (bf16[512,2048]{1,0:T(8,128)(2,1)}, bf16[512,2048]{1,0:T(8,128)(2,1)}, u32[]{:S(2)}, u32[]{:S(2)}) collective-permute-start(bf16[512,2048]{1,0:T(8,128)(2,1)} %collective-permute-done.1), channel_id=1, source_target_pairs={{8,12},{12,8},{16,20},{20,16},{9,13},{13,9},{17,21},{21,17},{10,14... | collective-permute-start | bytes 6291464 | tf_op jit(solution)/shard_map/ppermute | solution.py:246
  86.0 56.3 %collective-permute-start.5 = (bf16[1024,512]{1,0:T(8,128)(2,1)}, bf16[1024,512]{1,0:T(8,128)(2,1)}, u32[]{:S(2)}, u32[]{:S(2)}) collective-permute-start(bf16[1024,512]{1,0:T(8,128)(2,1)} %collective-permute-done.refs_5_), channel_id=1, source_target_pairs={{8,16},{12,20},{16,8},{20,12},{9,17},{13,21},{17,9},{21,13},{10,18... | collective-permute-start | bytes 3145736 | tf_op jit(solution)/shard_map/ppermute | solution.py:246
  92.3 54.9 %collective-permute-start.2 = (bf16[2,1024,512]{2,1,0:T(8,128)(2,1)}, bf16[2,1024,512]{2,1,0:T(8,128)(2,1)}, u32[]{:S(2)}, u32[]{:S(2)}) collective-permute-start(bf16[2,1024,512]{2,1,0:T(8,128)(2,1)} %pad_maximum_fusion.5), channel_id=1, source_target_pairs={{0,8},{4,12},{24,16},{28,20},{1,9},{5,13},{25,17},{29,21},{2,10},{... | collective-permute-start | bytes 6291464 | tf_op jit(solution)/shard_map/ppermute | solution.py:246
  127.2 102.4 %collective-permute-start.8 = (bf16[2,512,2048]{2,1,0:T(8,128)(2,1)}, bf16[2,512,2048]{2,1,0:T(8,128)(2,1)}, u32[]{:S(2)}, u32[]{:S(2)}) collective-permute-start(bf16[2,512,2048]{2,1,0:T(8,128)(2,1)} %pad_maximum_fusion.3), channel_id=1, source_target_pairs={{0,1},{1,0},{2,3},{3,2},{4,5},{5,4},{6,7},{7,6},{8,9},{9,8},{10,11... | collective-permute-start | bytes 12582920 | tf_op jit(solution)/shard_map/ppermute | solution.py:261
  127.2 48.4 %collective-permute-start.17 = (bf16[512,2048]{1,0:T(8,128)(2,1)}, bf16[512,2048]{1,0:T(8,128)(2,1)}, u32[]{:S(2)}, u32[]{:S(2)}) collective-permute-start(bf16[512,2048]{1,0:T(8,128)(2,1)} %collective-permute-done.16), channel_id=1, source_target_pairs={{0,2},{1,3},{2,0},{3,1},{4,6},{5,7},{6,4},{7,5},{8,10},{9,11},{10,... | collective-permute-start | bytes 6291464 | tf_op jit(solution)/shard_map/ppermute | solution.py:258
  128.8 113.8 %collective-permute-start.21 = (bf16[512,4096]{1,0:T(8,128)(2,1)}, bf16[512,4096]{1,0:T(8,128)(2,1)}, u32[]{:S(2)}, u32[]{:S(2)}) collective-permute-start(bf16[512,4096]{1,0:T(8,128)(2,1)} %constant_dynamic-slice_fusion), channel_id=1, source_target_pairs={{8,12},{12,8},{16,20},{20,16},{9,13},{13,9},{17,21},{21,17},{10,14... | collective-permute-start | bytes 12582920 | tf_op jit(solution)/shard_map/ppermute | solution.py:246
  142.4 39.3 %collective-permute-start.4 = (bf16[1024,768]{1,0:T(8,128)(2,1)S(1)}, bf16[1024,768]{1,0:T(8,128)(2,1)}, u32[]{:S(2)}, u32[]{:S(2)}) collective-permute-start(bf16[1024,768]{1,0:T(8,128)(2,1)S(1)} %get-tuple-element.15.refs_4_), channel_id=1, source_target_pairs={{8,16},{12,20},{16,8},{20,12},{9,17},{13,21},{17,9},{21,13},{10,18... | collective-permute-start | bytes 4718600 | tf_op jit(solution)/shard_map/ppermute | solution.py:246
  147.2 219.1 %copy-start.56 = (s32[2,4]{1,0:T(2,128)}, s32[2,4]{1,0:T(2,128)S(1)}, u32[]{:S(2)}) copy-start(s32[2,4]{1,0:T(2,128)S(1)} %pad_add_fusion.3.at_ref) | copy-start | bytes 100
  147.2 67.0 %collective-permute-start.12 = (bf16[1024,768]{1,0:T(8,128)(2,1)S(1)}, bf16[1024,768]{1,0:T(8,128)(2,1)S(1)}, u32[]{:S(2)}, u32[]{:S(2)}) collective-permute-start(bf16[1024,768]{1,0:T(8,128)(2,1)S(1)} %collective-permute-done.10.refs_5_), channel_id=1, source_target_pairs={{8,16},{12,20},{16,8},{20,12},{9,17},{13,21},{17,9},{21,13},{10,18... | collective-permute-start | bytes 4718600 | tf_op jit(solution)/shard_map/ppermute | solution.py:246
  175.6 78.0 %collective-permute-start.11 = (bf16[2,1024,512]{2,1,0:T(8,128)(2,1)S(1)}, bf16[2,1024,512]{2,1,0:T(8,128)(2,1)}, u32[]{:S(2)}, u32[]{:S(2)}) collective-permute-start(bf16[2,1024,512]{2,1,0:T(8,128)(2,1)S(1)} %fusion.3), channel_id=1, source_target_pairs={{0,8},{4,12},{24,16},{28,20},{1,9},{5,13},{25,17},{29,21},{2,10},{... | collective-permute-start | bytes 6291464 | tf_op jit(solution)/shard_map/ppermute | solution.py:246
  181.7 139.5 %collective-permute-start.18 = (bf16[2,512,2048]{2,1,0:T(8,128)(2,1)}, bf16[2,512,2048]{2,1,0:T(8,128)(2,1)}, u32[]{:S(2)}, u32[]{:S(2)}) collective-permute-start(bf16[2,512,2048]{2,1,0:T(8,128)(2,1)} %pad_maximum_fusion.4), channel_id=1, source_target_pairs={{0,1},{1,0},{2,3},{3,2},{4,5},{5,4},{6,7},{7,6},{8,9},{9,8},{10,11... | collective-permute-start | bytes 12582920 | tf_op jit(solution)/shard_map/ppermute | solution.py:261
  214.2 53.0 %collective-permute-start.6 = (bf16[2,1024,512]{2,1,0:T(8,128)(2,1)}, bf16[2,1024,512]{2,1,0:T(8,128)(2,1)}, u32[]{:S(2)}, u32[]{:S(2)}) collective-permute-start(bf16[2,1024,512]{2,1,0:T(8,128)(2,1)} %collective-permute-done.2.refs_4_.refs_5_), channel_id=1, source_target_pairs={{8,16},{12,20},{16,8},{20,12},{9,17},{13,21},{17,9},{21,13},{10,18... | collective-permute-start | bytes 6291464 | tf_op jit(solution)/shard_map/ppermute | solution.py:246
  242.6 116.2 %collective-permute-start.22 = (bf16[512,4096]{1,0:T(8,128)(2,1)}, bf16[512,4096]{1,0:T(8,128)(2,1)}, u32[]{:S(2)}, u32[]{:S(2)}) collective-permute-start(bf16[512,4096]{1,0:T(8,128)(2,1)} %collective-permute-done.21), channel_id=1, source_target_pairs={{0,1},{1,0},{2,3},{3,2},{4,5},{5,4},{6,7},{7,6},{8,9},{9,8},{10,11... | collective-permute-start | bytes 12582920 | tf_op jit(solution)/shard_map/ppermute | solution.py:261
  253.6 54.3 %collective-permute-start.13 = (bf16[2,1024,512]{2,1,0:T(8,128)(2,1)}, bf16[2,1024,512]{2,1,0:T(8,128)(2,1)}, u32[]{:S(2)}, u32[]{:S(2)}) collective-permute-start(bf16[2,1024,512]{2,1,0:T(8,128)(2,1)} %collective-permute-done.11.refs_4_.refs_5_), channel_id=1, source_target_pairs={{8,16},{12,20},{16,8},{20,12},{9,17},{13,21},{17,9},{21,13},{10,18... | collective-permute-start | bytes 6291464 | tf_op jit(solution)/shard_map/ppermute | solution.py:246
  256.2 123.7 %copy-start.32 = (s32[512,1]{1,0:T(8,128)}, s32[512,1]{1,0:T(8,128)S(1)}, u32[]{:S(2)}) copy-start(s32[512,1]{1,0:T(8,128)S(1)} %copy.37.first_ref) | copy-start | bytes 6148
  265.4 122.6 %collective-permute-start.15 = (bf16[2,1024,256]{2,1,0:T(8,128)(2,1)}, bf16[2,1024,256]{2,1,0:T(8,128)(2,1)S(1)}, u32[]{:S(2)}, u32[]{:S(2)}) collective-permute-start(bf16[2,1024,256]{2,1,0:T(8,128)(2,1)} %pad_maximum_fusion.6), channel_id=1, source_target_pairs={{0,8},{4,12},{24,16},{28,20},{1,9},{5,13},{25,17},{29,21},{2,10},{... | collective-permute-start | bytes 3145736 | tf_op jit(solution)/shard_map/ppermute | solution.py:246
  382.7 48.6 %collective-permute-start.24 = (bf16[512,512]{1,0:T(8,128)(2,1)}, bf16[512,512]{1,0:T(8,128)(2,1)}, u32[]{:S(2)}, u32[]{:S(2)}) collective-permute-start(bf16[512,512]{1,0:T(8,128)(2,1)} %pad_maximum_fusion.11), channel_id=1, source_target_pairs={{8,4},{12,0},{16,28},{20,24},{9,5},{13,1},{17,29},{21,25},{10,6},{... | collective-permute-start | bytes 1572872 | tf_op jit(solution)/shard_map/ppermute | solution.py:246
  387.9 54.3 %collective-permute-start.19 = (bf16[2,1024,256]{2,1,0:T(8,128)(2,1)S(1)}, bf16[2,1024,256]{2,1,0:T(8,128)(2,1)S(1)}, u32[]{:S(2)}, u32[]{:S(2)}) collective-permute-start(bf16[2,1024,256]{2,1,0:T(8,128)(2,1)S(1)} %collective-permute-done.15.refs_4_.refs_5_), channel_id=1, source_target_pairs={{8,16},{12,20},{16,8},{20,12},{9,17},{13,21},{17,9},{21,13},{10,18... | collective-permute-start | bytes 3145736 | tf_op jit(solution)/shard_map/ppermute | solution.py:246
  393.9 47.2 %collective-permute-start.26 = (bf16[512,512]{1,0:T(8,128)(2,1)S(1)}, bf16[512,512]{1,0:T(8,128)(2,1)S(1)}, u32[]{:S(2)}, u32[]{:S(2)}) collective-permute-start(bf16[512,512]{1,0:T(8,128)(2,1)S(1)} %shard_map.124), channel_id=1, source_target_pairs={{8,4},{12,0},{16,28},{20,24},{9,5},{13,1},{17,29},{21,25},{10,6},{... | collective-permute-start | bytes 1572872 | tf_op jit(solution)/shard_map/ppermute | solution.py:246
  411.8 29.3 %collective-permute-start.25 = (bf16[512,512]{1,0:T(8,128)(2,1)S(1)}, bf16[512,512]{1,0:T(8,128)(2,1)S(1)}, u32[]{:S(2)}, u32[]{:S(2)}) collective-permute-start(bf16[512,512]{1,0:T(8,128)(2,1)S(1)} %shard_map.121), channel_id=1, source_target_pairs={{8,12},{12,8},{16,20},{20,16},{9,13},{13,9},{17,21},{21,17},{10,14... | collective-permute-start | bytes 1572872 | tf_op jit(solution)/shard_map/ppermute | solution.py:246
  415.2 21.7 %collective-permute-start.23 = (bf16[512,512]{1,0:T(8,128)(2,1)}, bf16[512,512]{1,0:T(8,128)(2,1)}, u32[]{:S(2)}, u32[]{:S(2)}) collective-permute-start(bf16[512,512]{1,0:T(8,128)(2,1)} %pad_maximum_fusion.12), channel_id=1, source_target_pairs={{8,12},{12,8},{16,20},{20,16},{9,13},{13,9},{17,21},{21,17},{10,14... | collective-permute-start | bytes 1572872 | tf_op jit(solution)/shard_map/ppermute | solution.py:246
  431.3 28.3 %collective-permute-start.9 = (bf16[512,512]{1,0:T(8,128)(2,1)S(1)}, bf16[512,512]{1,0:T(8,128)(2,1)S(1)}, u32[]{:S(2)}, u32[]{:S(2)}) collective-permute-start(bf16[512,512]{1,0:T(8,128)(2,1)S(1)} %copy-done.81), channel_id=1, source_target_pairs={{8,0},{12,4},{16,24},{20,28},{9,1},{13,5},{17,25},{21,29},{10,2},{... | collective-permute-start | bytes 1572872 | tf_op jit(solution)/shard_map/ppermute | solution.py:246
  436.9 44.4 %collective-permute-start.14 = (bf16[512,512]{1,0:T(8,128)(2,1)}, bf16[512,512]{1,0:T(8,128)(2,1)}, u32[]{:S(2)}, u32[]{:S(2)}) collective-permute-start(bf16[512,512]{1,0:T(8,128)(2,1)} %shard_map.108), channel_id=1, source_target_pairs={{8,0},{12,4},{16,24},{20,28},{9,1},{13,5},{17,25},{21,29},{10,2},{... | collective-permute-start | bytes 1572872 | tf_op jit(solution)/shard_map/ppermute | solution.py:246
  448.7 28.3 %collective-permute-start.28 = (bf16[512,256]{1,0:T(8,128)(2,1)}, bf16[512,256]{1,0:T(8,128)(2,1)}, u32[]{:S(2)}, u32[]{:S(2)}) collective-permute-start(bf16[512,256]{1,0:T(8,128)(2,1)} %shard_map.130), channel_id=1, source_target_pairs={{8,4},{12,0},{16,28},{20,24},{9,5},{13,1},{17,29},{21,25},{10,6},{... | collective-permute-start | bytes 786440 | tf_op jit(solution)/shard_map/ppermute | solution.py:246
  457.2 19.8 %collective-permute-start.27 = (bf16[512,256]{1,0:T(8,128)(2,1)}, bf16[512,256]{1,0:T(8,128)(2,1)}, u32[]{:S(2)}, u32[]{:S(2)}) collective-permute-start(bf16[512,256]{1,0:T(8,128)(2,1)} %shard_map.127), channel_id=1, source_target_pairs={{8,12},{12,8},{16,20},{20,16},{9,13},{13,9},{17,21},{21,17},{10,14... | collective-permute-start | bytes 786440 | tf_op jit(solution)/shard_map/ppermute | solution.py:246
  469.0 13.3 %collective-permute-start.20 = (bf16[512,256]{1,0:T(8,128)(2,1)}, bf16[512,256]{1,0:T(8,128)(2,1)}, u32[]{:S(2)}, u32[]{:S(2)}) collective-permute-start(bf16[512,256]{1,0:T(8,128)(2,1)} %shard_map.115), channel_id=1, source_target_pairs={{8,0},{12,4},{16,24},{20,28},{9,1},{13,5},{17,25},{21,29},{10,2},{... | collective-permute-start | bytes 786440 | tf_op jit(solution)/shard_map/ppermute | solution.py:246
  (85 other events, 771.9 us)

commit v3 on v2

--- a/solution.py
+++ b/solution.py
@@ -163,73 +163,148 @@
     )(queries, bias, cosine, sine, keys, values, first)
 
 
-def project_kernel(count, at_ref, *refs):
-    blocks, pieces = refs[:count], refs[count : 2 * count]
-    out_ref = refs[-1]
-    total = None if len(refs) == 2 * count + 1 else refs[2 * count][...]
-    for block, piece in zip(blocks, pieces):
-        weight = piece[...].reshape(piece.shape[-2:])
-        term = jnp.dot(block[0], weight, preferred_element_type=jnp.float32)
-        total = term if total is None else total + term
-    out_ref[...] = total
-
-
-def project(rows, at, pieces, width, total=None):
-    count = len(pieces)
-    tokens, depth = rows.shape[1], pieces[0][0].shape[-2]
-    tile = 2 * HD
-    in_specs = [
-        pl.BlockSpec((1, tokens, depth), functools.partial(lambda p, j, at: (at[0, p], 0, at[1, p]), p))
-        for p in range(count)
-    ]
-    for array, lead, skip in pieces:
-        if array.ndim == 3:
-            in_specs.append(
-                pl.BlockSpec(
-                    (1, depth, tile),
-                    functools.partial(lambda l, s, j, at: (l, 0, j + s), lead, skip // tile),
-                )
-            )
-        else:
-            in_specs.append(
-                pl.BlockSpec(
-                    (depth, tile), functools.partial(lambda s, j, at: (0, j + s), skip // tile)
-                )
-            )
-    operands = [rows] * count + [array for array, _, _ in pieces]
-    if total is not None:
-        in_specs.append(pl.BlockSpec((tokens, tile), lambda j, at: (0, j)))
-        operands.append(total)
+def norm_kernel(part_ref, hidden_ref, gain_ref, out_ref, part_out_ref):
+    widened = hidden_ref[...].astype(jnp.float32)
+    scale = lax.rsqrt(jnp.mean(widened * widened, axis=-1, keepdims=True) + EPS)
+    out_ref[...] = (widened * scale * gain_ref[...]).astype(jnp.bfloat16)
+    width = part_out_ref.shape[1]
+    part_out_ref[...] = out_ref[:, pl.ds(pl.multiple_of(part_ref[0] * width, width), width)]
+
+
+def norm(hidden, norm_gain, part, width):
+    rows, features = hidden.shape
+    step = 64
     return pl.pallas_call(
-        functools.partial(project_kernel, count),
+        norm_kernel,
         grid_spec=pltpu.PrefetchScalarGridSpec(
             num_scalar_prefetch=1,
-            grid=(width // tile,),
+            grid=(rows // step,),
+            in_specs=[
+                pl.BlockSpec((step, features), lambda i, part: (i, 0)),
+                pl.BlockSpec((1, features), lambda i, part: (0, 0)),
+            ],
+            out_specs=[
+                pl.BlockSpec((step, features), lambda i, part: (i, 0)),
+                pl.BlockSpec((step, width), lambda i, part: (i, 0)),
+            ],
+        ),
+        out_shape=[
+            jax.ShapeDtypeStruct((rows, features), jnp.bfloat16),
+            jax.ShapeDtypeStruct((rows, width), jnp.bfloat16),
+        ],
+        compiler_params=pltpu.CompilerParams(vmem_limit_bytes=32 * 2**20),
+        cost_estimate=pl.CostEstimate(
+            flops=4 * rows * features, bytes_accessed=5 * rows * features, transcendentals=rows
+        ),
+    )(part[None], hidden, norm_gain[None])
+
+
+def project_kernel(sources, leads, first_col, width, with_totals, pick_ref, *refs):
+    sets, count = len(sources), len(leads)
+    refs = list(refs)
+
+    def take(number):
+        taken = refs[:number]
+        del refs[:number]
+        return taken
+
+    row_refs = [take(number) for number in sources]
+    weight_refs = take(count)
+    totals = take(sets) if with_totals else [None] * sets
+    outs = take(sets)
+    row_buf, weight_buf, row_sem, weight_sem = refs
+    depth = weight_buf.shape[1]
+
+    def weight_copy(piece):
+        ref, lead = weight_refs[piece], leads[piece]
+        ref = ref if lead is None else ref.at[lead]
+        skip = first_col if ref.shape[1] > width else 0
+        return pltpu.make_async_copy(
+            ref.at[:, skip : skip + width], weight_buf.at[piece], weight_sem.at[piece]
+        )
+
+    def row_copy(which, piece, source):
+        at = pl.multiple_of(pick_ref[which, 1, piece] * depth, depth)
+        return pltpu.make_async_copy(
+            row_refs[which][source].at[:, pl.ds(at, depth)],
+            row_buf.at[which, piece],
+            row_sem.at[which, piece],
+        )
+
+    for piece in range(count):
+        weight_copy(piece).start()
+        for which in range(sets):
+            if sources[which] == 1:
+                row_copy(which, piece, 0).start()
+            else:
+                for source in range(sources[which]):
+
+                    @pl.when(pick_ref[which, 0, piece] == source)
+                    def _():
+                        row_copy(which, piece, source).start()
+
+    for piece in range(count):
+        weight_copy(piece).wait()
+        for which in range(sets):
+            row_copy(which, piece, 0).wait()
+            term = jnp.dot(
+                row_buf[which, piece], weight_buf[piece], preferred_element_type=jnp.float32
+            )
+            if piece > 0:
+                outs[which][...] += term
+            elif totals[which] is None:
+                outs[which][...] = term
+            else:
+                outs[which][...] = totals[which][...] + term
+
+
+def project(row_sets, picks, pieces, first_col, width, totals=None):
+    sets, count = len(row_sets), len(pieces)
+    sources = tuple(len(rows) for rows in row_sets)
+    leads = tuple(lead for _, lead in pieces)
+    tokens, depth = row_sets[0][0].shape[0], pieces[0][0].shape[-2]
+    operands = [array for rows in row_sets for array in rows] + [array for array, _ in pieces]
+    in_specs = [pl.BlockSpec(memory_space=pl.ANY)] * len(operands)
+    if totals is not None:
+        for total in totals:
+            at = first_col // width if total.shape[1] > width else 0
+            in_specs.append(
+                pl.BlockSpec((tokens, width), functools.partial(lambda at, i, pick: (0, at), at))
+            )
+            operands.append(total)
+    out = pl.BlockSpec((tokens, width), lambda i, pick: (0, 0))
+    return pl.pallas_call(
+        functools.partial(
+            project_kernel, sources, leads, first_col, width, totals is not None
+        ),
+        grid_spec=pltpu.PrefetchScalarGridSpec(
+            num_scalar_prefetch=1,
+            grid=(1,),
             in_specs=in_specs,
-            out_specs=pl.BlockSpec((tokens, tile), lambda j, at: (0, j)),
+            out_specs=[out] * sets,
+            scratch_shapes=[
+                pltpu.VMEM((sets, count, tokens, depth), jnp.bfloat16),
+                pltpu.VMEM((count, depth, width), jnp.bfloat16),
+                pltpu.SemaphoreType.DMA((sets, count)),
+                pltpu.SemaphoreType.DMA((count,)),
+            ],
         ),
-        out_shape=jax.ShapeDtypeStruct((tokens, width), jnp.float32),
-        compiler_params=pltpu.CompilerParams(vmem_limit_bytes=48 * 2**20),
+        out_shape=[jax.ShapeDtypeStruct((tokens, width), jnp.float32)] * sets,
+        compiler_params=pltpu.CompilerParams(vmem_limit_bytes=52 * 2**20),
         cost_estimate=pl.CostEstimate(
-            flops=2 * count * tokens * depth * width,
-            bytes_accessed=2 * count * depth * (tokens + width) + 8 * tokens * width,
+            flops=2 * sets * count * tokens * depth * width,
+            bytes_accessed=2 * count * depth * (sets * tokens + width) + 8 * sets * tokens * width,
             transcendentals=0,
         ),
-    )(at, *operands)
+    )(jnp.stack(picks), *operands)
 
 
 MIDDLE = (2, 3, 4, 5)
 ENDS = (0, 1, 6, 7)
-FIRST_CODES = (0, 1, 6, 7)
-LAST_CODES = (2, 3, 4, 5)
 
 
 def pairs_from(sources, code):
     return [(s, s ^ code) for s in sources]
-
-
-def after(value, *others):
-    return lax.optimization_barrier((value,) + others)[0]
 
 
 def middle_form(hidden, norm_gain, q_weight, q_bias, kv_weight, kv_bias, prefix_lens, assignment):
@@ -238,16 +313,13 @@
     half_cols = q_cols // 2
     group = lax.axis_index("group")
     tensor = lax.axis_index("tensor")
-    core = tensor & 1
     y = group & 1
     is_middle = (group >= 2) & (group < 6)
+    barrier = lax.optimization_barrier
 
     def over_group(value, sources, code):
         return lax.ppermute(value, "group", pairs_from(sources, code))
 
-    def over_y(value):
-        return over_group(value, range(8), 1)
-
     def to_middle(value):
         return over_group(value, ENDS, 2)
 
@@ -261,82 +333,57 @@
         return lax.ppermute(value, "tensor", pairs_from(range(4), 1))
 
     heads = (2, 4, 2)
-    cut = heads[0] * HD
+    widths = (2 * HD + heads[0] * HD, heads[1] * HD, heads[2] * HD)
+    begin = (0, widths[0], widths[0] + widths[1])
+    every = sum(widths)
 
     def columns(half):
         head = (2 * tensor + half) * HD
         kv_part = lax.dynamic_slice_in_dim(kv_weight, head, HD, 2).reshape(slice_rows, 2 * HD)
-        early = lax.dynamic_slice_in_dim(q_weight, half * half_cols, cut, 1)
-        late = lax.dynamic_slice_in_dim(q_weight, half * half_cols + cut, half_cols - cut, 1)
-        return jnp.concatenate([kv_part, early], axis=1), late
-
-    own0, own12 = columns(y)
-    other0, other12 = columns(1 - y)
-    mid_cols = heads[1] * HD
-
-    m_own0 = across_middle(own0)
-    swap0 = over_y(other0)
-    normed = normalise(hidden, norm_gain)
-    quarter = lax.dynamic_slice_in_dim(normed, tensor * (features // 4), features // 4, 1)
-    half = lax.dynamic_slice_in_dim(normed, core * (features // 2), features // 2, 1)
+        q_part = lax.dynamic_slice_in_dim(q_weight, half * half_cols, half_cols, 1)
+        return jnp.concatenate([kv_part, q_part], axis=1)
+
+    def both(one, two, chunk):
+        low, high = begin[chunk], begin[chunk] + widths[chunk]
+        return jnp.stack([one[:, low:high], two[:, low:high]])
+
+    def pick(code_of_rows, codes):
+        block = jnp.stack([group ^ code for code in codes])
+        if code_of_rows == 0:
+            return jnp.stack([block * 0, block])
+        return jnp.stack([(block >> 1) ^ tensor, block & 1])
+
+    def projected(sets, codes, pieces, chunk, totals=None):
+        first, width = (0, every) if chunk is None else (begin[chunk], widths[chunk])
+        return project(
+            [rows_of[c] for c in sets],
+            [pick(c, codes) for c in sets],
+            [pieces[code] for code in codes],
+            first,
+            width,
+            totals,
+        )
+
+    own = columns(y)
+    other = columns(1 - y)
+    m_own = across_middle(own)
+    swap = over_group(other, range(8), 1)
+    normed, quarter = norm(hidden, norm_gain, tensor, features // 4)
     end2 = to_middle(quarter)
-    m_swap0 = across_middle(swap0)
-    swap12 = over_y(after(other12, swap0, m_own0))
-    m_own12 = across_middle(after(own12, m_own0))
-    e0 = to_middle(after(jnp.stack([own0, swap0]), end2))
-    across2 = over_x(end2)
-    m_swap12 = across_middle(after(swap12, m_swap0))
-    end3 = over_group(after(end2, swap12), MIDDLE, 1)
-
-    def whole(near, across):
-        both = jnp.stack([near, across])
-        return jnp.concatenate([both, over_core(both)])
-
-    rows0 = normed[None]
-    rows2 = whole(end2, across2)
-
-    def spots(codes, places):
-        block = jnp.stack([group ^ code for code in codes])
-        if places == 1:
-            return jnp.stack([block * 0, block])
-        if places == 2:
-            return jnp.stack([(block >> 2) ^ core, block & 3])
-        apart = (block >> 1) ^ tensor
-        return jnp.stack([(apart >> 1) | ((apart & 1) << 1), block & 1])
-
-    places_of = (1, 2, 4, 4)
-    first_at = [spots(FIRST_CODES, n) for n in places_of]
-    last_at = [spots(LAST_CODES, n) for n in places_of]
-
-    first0 = [(own0, 0, 0), (swap0, 0, 0), (m_own0, 0, 0), (m_swap0, 0, 0)]
-    first1 = [(own12, 0, 0), (swap12, 0, 0), (m_own12, 0, 0), (m_swap12, 0, 0)]
-    first2 = [(array, 0, mid_cols) for array, _, _ in first1]
-    firsts = (first0, first1, first2)
-    widths = (2 * HD + cut, mid_cols, heads[2] * HD)
-
-    def first_part(code, rows, chunk):
-        return project(rows, first_at[code], firsts[chunk], widths[chunk])
-
-    sums = {}
-    sums[0, 0] = first_part(0, rows0, 0)
-    m_e0 = across_middle(after(e0, m_own12, sums[0, 0]))
-    late = jnp.stack([own12, swap12])
-    e1 = to_middle(after(late[:, :, :mid_cols], e0))
-    across3 = over_x(after(end3, across2))
-    beside_half = over_group(after(half, end3), MIDDLE, 1)
-    for chunk in (1, 2):
-        sums[0, chunk] = first_part(0, rows0, chunk)
-    for chunk in range(3):
-        sums[2, chunk] = first_part(2, rows2, chunk)
-    rows3 = whole(end3, across3)
-    m_e1 = across_middle(after(e1, m_swap12, *[sums[0, c] for c in (1, 2)], *[sums[2, c] for c in range(3)]))
-    e2 = to_middle(after(late[:, :, mid_cols:], e1))
-    for chunk in range(3):
-        sums[3, chunk] = first_part(3, rows3, chunk)
 
     bias = lax.dynamic_slice_in_dim(q_bias, y * half_cols, half_cols, 0)[None, :]
     kv_bias_here = lax.dynamic_slice_in_dim(kv_bias, (2 * tensor + y) * HD, HD, 1)
     inverse_freq = THETA ** (-2.0 * jnp.arange(HD // 2, dtype=jnp.float32) / HD)
+    own, swap, m_own, normed, quarter, end2 = barrier((own, swap, m_own, normed, quarter, end2))
+
+    rows_of = {0: [normed]}
+    m_swap = across_middle(swap[:, : begin[2]])
+    e0 = to_middle(both(own, swap, 0))
+    end3 = over_group(end2, MIDDLE, 1)
+    across2 = over_x(end2)
+    twin2 = over_core(end2)
+    early = {0: (own, None), 1: (swap, None), 6: (m_own, None)}
+    sums = {0: projected([0], (0, 1, 6), early, None)[0]}
     tables = []
     for code in range(4):
         _, offset, places = token_layout(prefix_lens, assignment, group ^ code, tok_rows)
@@ -345,12 +392,33 @@
         cosine = jnp.concatenate([cosine, cosine], axis=1)
         sine = jnp.concatenate([-sine, sine], axis=1)
         tables.append((cosine, sine, (places - offset)[:, None]))
-
-    last0 = [(e0, 0, 0), (e0, 1, 0), (m_e0, 0, 0), (m_e0, 1, 0)]
+    (own, swap, m_swap, e0, end2, end3, across2, twin2, sums[0], tables, quarter) = barrier(
+        (own, swap, m_swap, e0, end2, end3, across2, twin2, sums[0], tables, quarter)
+    )
+
+    m_e0 = across_middle(e0)
+    e1 = to_middle(both(own, swap, 1))
+    end1 = over_group(quarter, MIDDLE, 1)
+    across3 = over_x(end3)
+    far2 = over_core(across2)
+    rows_of[2] = [end2, twin2, across2, far2]
+    sums[2] = projected([2], (0, 1, 6), early, None)[0]
+    (own, swap, m_e0, e0, e1, end1, end3, across3, far2, sums[2]) = barrier(
+        (own, swap, m_e0, e0, e1, end1, end3, across3, far2, sums[2])
+    )
+    rows_of[2] = [end2, twin2, across2, far2]
+
+    m_e1 = across_middle(e1)
+    e2 = to_middle(both(own, swap, 2))
+    across1 = over_x(end1)
+    twin3 = over_core(end3)
+    far3 = over_core(across3)
+    rows_of[3] = [end3, twin3, across3, far3]
+    sums[3] = projected([3], (0, 1, 6), early, None)[0]
+
     keys_values, outs = {}, {}
 
-    def finish(code, rows, chunk, lasts, total, place):
-        total = project(rows, last_at[code], lasts, widths[chunk], total)
+    def attended(code, chunk, total):
         cosine, sine, first = tables[code]
         if chunk == 0:
             keys = total[:, :HD] + kv_bias_here[0]
@@ -359,6 +427,7 @@
             values = (total[:, HD : 2 * HD] + kv_bias_here[1]).astype(jnp.bfloat16)
             keys_values[code] = (keys, values)
         keys, values = keys_values[code]
+        place = sum(heads[:chunk]) * HD
         out = attend(
             total,
             heads[chunk],
@@ -371,32 +440,50 @@
         )
         outs[code, chunk] = jnp.concatenate([keys, values, out], axis=1) if chunk == 0 else out
 
-    def send_back(chunk):
-        return (
-            over_group(outs[1, chunk], MIDDLE, 1),
-            over_group(outs[2, chunk], MIDDLE, 2),
-            over_group(outs[3, chunk], MIDDLE, 3),
-        )
-
-    for code, rows in ((0, rows0), (2, rows2), (3, rows3)):
-        finish(code, rows, 0, last0, sums[code, 0], 0)
-    m_e2 = across_middle(after(e2, m_e0, *[outs[c, 0] for c in (0, 2, 3)]))
-    rows1 = jnp.stack([beside_half, over_core(beside_half)])
-    for chunk in range(3):
-        sums[1, chunk] = first_part(1, rows1, chunk)
-    finish(1, rows1, 0, last0, sums[1, 0], 0)
-    all_rows = (rows0, rows1, rows2, rows3)
-    back = [send_back(0)]
-    last1 = [(e1, 0, 0), (e1, 1, 0), (m_e1, 0, 0), (m_e1, 1, 0)]
-    last2 = [(e2, 0, 0), (e2, 1, 0), (m_e2, 0, 0), (m_e2, 1, 0)]
-    for chunk, lasts, place in ((1, last1, cut), (2, last2, cut + mid_cols)):
-        for code in (2, 3, 1, 0):
-            finish(code, all_rows[code], chunk, lasts, sums[code, chunk], place)
-        back.append(send_back(chunk))
+    def send_back(code, chunk):
+        return over_group(outs[code, chunk], MIDDLE, code)
+
+    late = (7, 2, 3, 4, 5)
+    late0 = {7: (m_swap, None), 2: (e0, 0), 3: (e0, 1), 4: (m_e0, 0), 5: (m_e0, 1)}
+    three = (2, 3, 0)
+    totals = projected(three, late, late0, 0, [sums[c] for c in three])
+    for code, total in zip(three, totals):
+        attended(code, 0, total)
+    back = {(code, 0): send_back(code, 0) for code in (2, 3)}
+    (swap, m_e1, e1, e2, end1, across1, back[2, 0], back[3, 0], outs[0, 0], sums[3]) = barrier(
+        (swap, m_e1, e1, e2, end1, across1, back[2, 0], back[3, 0], outs[0, 0], sums[3])
+    )
+
+    last = jnp.concatenate([swap[None, :, begin[2] :], e2])
+    m_last = across_middle(last)
+    twin1 = over_core(end1)
+    far1 = over_core(across1)
+    rows_of[1] = [end1, twin1, across1, far1]
+    late1 = {7: (m_swap, None), 2: (e1, 0), 3: (e1, 1), 4: (m_e1, 0), 5: (m_e1, 1)}
+    totals = projected(three, late, late1, 1, [sums[c] for c in three])
+    for code, total in zip(three, totals):
+        attended(code, 1, total)
+    sums[1] = projected([1], (0, 1, 6), early, None)[0]
+    for chunk, pieces in ((0, late0), (1, late1)):
+        attended(1, chunk, projected([1], late, pieces, chunk, [sums[1]])[0])
+    back[1, 0] = send_back(1, 0)
+    for code in (2, 3, 1):
+        back[code, 1] = send_back(code, 1)
+    (m_last, *ready) = barrier((m_last, *[outs[c, 1] for c in range(4)]))
+    for code in range(4):
+        outs[code, 1] = ready[code]
+
+    late2 = {7: (m_last, 0), 2: (e2, 0), 3: (e2, 1), 4: (m_last, 1), 5: (m_last, 2)}
+    order = (3, 2, 1, 0)
+    totals = projected(order, late, late2, 2, [sums[c] for c in order])
+    for code, total in zip(order, totals):
+        attended(code, 2, total)
+        if code > 0:
+            back[code, 2] = send_back(code, 2)
 
     mine, its = [], []
     for chunk in range(3):
-        beside, back_own, back_other = back[chunk]
+        beside, back_own, back_other = (back[code, chunk] for code in (1, 2, 3))
         mine.append(jnp.where(is_middle, outs[0, chunk], back_own))
         its.append(jnp.where(is_middle, beside, back_other))
 

time: 499 us -> 406 us (0.81)
  the two profiles are of different devices: /device:TPU:20 before, /device:TPU:0 now
where the time goes in v3:
time: 406 us; the launch traced here: 401 us
  waiting for transfers between devices  143 us (35%)
  Pallas kernels  142 us (35%)
  starting transfers between devices  55 us (14%)
  local copies, waits for them, and re-layouts  30.9 us (8%)
  other arithmetic  27.4 us (7%)
    ppermute x21, waiting for transfers between devices, over_group(): return lax.ppermute(value, 'group', pairs_from(sources, code))  131 us
    pallas_call x9, Pallas kernels, project(): pl.pallas_call(functools.partial(project_kernel, sources, leads, first_co...  114 us
    ppermute x21, starting transfers between devices, over_group(): return lax.ppermute(value, 'group', pairs_from(sources, code))  51.3 us
    pallas_call x12, Pallas kernels, attend(): pl.pallas_call(attention_kernel, out_shape=jax.ShapeDtypeStruct((rows, he...  23 us
    ppermute x3, waiting for transfers between devices, over_x(): return lax.ppermute(value, 'tensor', pairs_from(range(4), 2))  12.5 us
    unnamed x97, local copies, waits for them, and re-layouts  9.02 us
  transfers between devices with their start and end apart: 30, of which 9 were waited for; matrix products, arithmetic and copies ran while one was open for 9% of the time, Pallas kernels for 35%

profile of v3, /device:TPU:0, one launch (start us, length us, event | category | flops | bytes accessed | tf_op | source)
XLA Modules:
  0.0 400.6 jit_solution(3339814087829505637)
XLA Ops:
  2.7 2.8 constant_dynamic-slice_fusion.1
  7.3 3.0 collective-permute-start
  14.3 5.4 %shard_map.95 = (bf16[512,8192]{1,0:T(8,128)(2,1)S(1)}, bf16[512,2048]{1,0:T(8,128)(2,1)S(1)}) custom-call(s32[1]{0:T(128)} %bitcast.part_ref, bf16[512,8192]{1,0:T(8,128)(2,1)S(1)} %bitcast.69, f32[1,8192]{1,0:T(1,128)S(1)} %bitcast.70), custom_call_target="tpu_custom_call" | custom-call | flops 16777216 | bytes 20971520 | tf_op jit(solution)/shard_map/pallas_call | solution.py:177
  19.7 3.3 copy-done.2
  23.0 6.1 %collective-permute-start.2 = (bf16[512,2048]{1,0:T(8,128)(2,1)S(1)}, bf16[512,2048]{1,0:T(8,128)(2,1)}, u32[]{:S(2)}, u32[]{:S(2)}) collective-permute-start(bf16[512,2048]{1,0:T(8,128)(2,1)S(1)} %get-tuple-element.75), channel_id=1, source_target_pairs={{0,8},{4,12},{24,16},{28,20},{1,9},{5,13},{25,17},{29,21},{2,10},{... | collective-permute-start | bytes 6291464 | tf_op jit(solution)/shard_map/ppermute | solution.py:321
  30.6 41.5 %collective-permute-done.2.refs_0_.refs_4_ = bf16[512,2048]{1,0:T(8,128)(2,1)} collective-permute-done((bf16[512,2048]{1,0:T(8,128)(2,1)S(1)}, bf16[512,2048]{1,0:T(8,128)(2,1)}, u32[]{:S(2)}, u32[]{:S(2)}) %collective-permute-start.2) | collective-permute-done | bytes 2097184 | tf_op jit(solution)/shard_map/ppermute | solution.py:321
  75.7 3.1 slice.114
  82.8 8.6 %collective-permute-start.4 = (bf16[2,1024,512]{2,1,0:T(8,128)(2,1)}, bf16[2,1024,512]{2,1,0:T(8,128)(2,1)}, u32[]{:S(2)}, u32[]{:S(2)}) collective-permute-start(bf16[2,1024,512]{2,1,0:T(8,128)(2,1)} %pad_maximum_fusion.2), channel_id=1, source_target_pairs={{0,8},{4,12},{24,16},{28,20},{1,9},{5,13},{25,17},{29,21},{2,10},{... | collective-permute-start | bytes 6291464 | tf_op jit(solution)/shard_map/ppermute | solution.py:321
  91.4 3.7 fusion.20
  96.3 9.5 %shard_map.96.refs_16_.refs_21_ = f32[512,1280]{1,0:T(8,128)} custom-call(s32[1,2,3]{2,1,0:T(2,128)S(1)} %pad_bitcast_fusion.1.pick_ref, bf16[512,8192]{1,0:T(8,128)(2,1)} %copy-done.2, bf16[1024,1280]{1,0:T(8,128)(2,1)} %pad_maximum_fusion.refs_1_.refs_4_, bf16[1024,1280]{1,0:T(8,128)(2,1)} %collective-permute-done.refs_2_.refs_5_, ...), custom_call_target="tpu_custom_call" | custom-call | flops 4026531840 | bytes 16252928 | tf_op jit(solution)/shard_map/pallas_call | solution.py:276
  105.8 29.6 %collective-permute-done.4.refs_10_.refs_11_.refs_5_.refs_6_ = bf16[2,1024,512]{2,1,0:T(8,128)(2,1)} collective-permute-done((bf16[2,1024,512]{2,1,0:T(8,128)(2,1)}, bf16[2,1024,512]{2,1,0:T(8,128)(2,1)}, u32[]{:S(2)}, u32[]{:S(2)}) %collective-permute-start.4) | collective-permute-done | bytes 2097184 | tf_op jit(solution)/shard_map/ppermute | solution.py:321
  135.4 2.4 collective-permute-start.8
  142.0 6.2 %collective-permute-start.9 = (bf16[2,1024,512]{2,1,0:T(8,128)(2,1)}, bf16[2,1024,512]{2,1,0:T(8,128)(2,1)}, u32[]{:S(2)}, u32[]{:S(2)}) collective-permute-start(bf16[2,1024,512]{2,1,0:T(8,128)(2,1)} %pad_maximum_fusion.3), channel_id=1, source_target_pairs={{0,8},{4,12},{24,16},{28,20},{1,9},{5,13},{25,17},{29,21},{2,10},{... | collective-permute-start | bytes 6291464 | tf_op jit(solution)/shard_map/ppermute | solution.py:321
  148.2 2.6 collective-permute-start.10
  152.8 9.8 %shard_map.97.refs_14_.refs_19_ = f32[512,1280]{1,0:T(8,128)} custom-call(s32[1,2,3]{2,1,0:T(2,128)S(1)} %add_bitcast_fusion.pick_ref, bf16[512,2048]{1,0:T(8,128)(2,1)} %collective-permute-done.2.refs_0_.refs_4_, bf16[512,2048]{1,0:T(8,128)(2,1)} %copy-done.23, bf16[512,2048]{1,0:T(8,128)(2,1)} %copy-done.22, bf16[512,2048]{1,0:T(8,128)(2,1)} %copy-done.24, ...), custom_call_target="tpu_custom_call" | custom-call | flops 4026531840 | bytes 16252928 | tf_op jit(solution)/shard_map/pallas_call | solution.py:276
  162.6 30.1 %collective-permute-done.9.refs_10_.refs_11_.refs_5_.refs_6_ = bf16[2,1024,512]{2,1,0:T(8,128)(2,1)} collective-permute-done((bf16[2,1024,512]{2,1,0:T(8,128)(2,1)}, bf16[2,1024,512]{2,1,0:T(8,128)(2,1)}, u32[]{:S(2)}, u32[]{:S(2)}) %collective-permute-start.9) | collective-permute-done | bytes 2097184 | tf_op jit(solution)/shard_map/ppermute | solution.py:321
  192.7 6.1 %collective-permute-done.11.refs_2_.refs_6_ = bf16[512,2048]{1,0:T(8,128)(2,1)} collective-permute-done((bf16[512,2048]{1,0:T(8,128)(2,1)}, bf16[512,2048]{1,0:T(8,128)(2,1)}, u32[]{:S(2)}, u32[]{:S(2)}) %collective-permute-start.11) | collective-permute-done | bytes 2097184 | tf_op jit(solution)/shard_map/ppermute | solution.py:330
  204.4 3.3 collective-permute-start.14
  208.3 9.8 %shard_map.98.refs_15_.refs_18_ = f32[512,1280]{1,0:T(8,128)} custom-call(s32[1,2,3]{2,1,0:T(2,128)S(1)} %add_bitcast_fusion.pick_ref, bf16[512,2048]{1,0:T(8,128)(2,1)} %collective-permute-done.5.refs_0_.refs_4_, bf16[512,2048]{1,0:T(8,128)(2,1)} %collective-permute-done.16.refs_1_.refs_5_, bf16[512,2048]{1,0:T(8,128)(2,1)} %collective-permute-done.11.refs_2_.refs_6_, ...), custom_call_target="tpu_custom_call" | custom-call | flops 4026531840 | bytes 16252928 | tf_op jit(solution)/shard_map/pallas_call | solution.py:276
  218.1 18.9 %shard_map.99 = (f32[512,512]{1,0:T(8,128)S(1)}, f32[512,512]{1,0:T(8,128)}, f32[512,512]{1,0:T(8,128)}) custom-call(s32[3,2,5]{2,1,0:T(2,128)S(1)} %pad_add_fusion.1.pick_ref, bf16[512,2048]{1,0:T(8,128)(2,1)} %collective-permute-done.2.refs_0_.refs_4_, bf16[512,2048]{1,0:T(8,128)(2,1)} %copy-done.23, bf16[512,2048]{1,0:T(8,128)(2,1)} %copy-done.22, ...), custom_call_target="tpu_custom_call" | custom-call | flops 8053063680 | bytes 27262976 | tf_op jit(solution)/shard_map/pallas_call | solution.py:276
  248.7 6.3 %collective-permute-done.15.refs_2_.refs_10_ = bf16[512,2048]{1,0:T(8,128)(2,1)} collective-permute-done((bf16[512,2048]{1,0:T(8,128)(2,1)}, bf16[512,2048]{1,0:T(8,128)(2,1)}, u32[]{:S(2)}, u32[]{:S(2)}) %collective-permute-start.15) | collective-permute-done | bytes 2097184 | tf_op jit(solution)/shard_map/ppermute | solution.py:330
  255.0 2.5 collective-permute-done.18
  257.6 9.8 %collective-permute-done.19 = bf16[512,512]{1,0:T(8,128)(2,1)} collective-permute-done((bf16[512,512]{1,0:T(8,128)(2,1)S(1)}, bf16[512,512]{1,0:T(8,128)(2,1)}, u32[]{:S(2)}, u32[]{:S(2)}) %collective-permute-start.19) | collective-permute-done | bytes 524320 | tf_op jit(solution)/shard_map/ppermute | solution.py:321
  269.3 18.9 %shard_map.103 = (f32[512,512]{1,0:T(8,128)S(1)}, f32[512,512]{1,0:T(8,128)}, f32[512,512]{1,0:T(8,128)}) custom-call(s32[3,2,5]{2,1,0:T(2,128)S(1)} %pad_add_fusion.1.pick_ref, bf16[512,2048]{1,0:T(8,128)(2,1)} %collective-permute-done.2.refs_0_.refs_4_, bf16[512,2048]{1,0:T(8,128)(2,1)} %copy-done.23, bf16[512,2048]{1,0:T(8,128)(2,1)} %copy-done.22, ...), custom_call_target="tpu_custom_call" | custom-call | flops 8053063680 | bytes 27262976 | tf_op jit(solution)/shard_map/pallas_call | solution.py:276
  294.3 2.5 pad_maximum_fusion.4
  297.9 2.2 shard_map.109
  304.9 9.9 %shard_map.105.refs_9_.refs_20_ = f32[512,1280]{1,0:T(8,128)} custom-call(s32[1,2,3]{2,1,0:T(2,128)S(1)} %copy-done.18, bf16[512,2048]{1,0:T(8,128)(2,1)} %collective-permute-done.10.refs_0_.refs_8_, bf16[512,2048]{1,0:T(8,128)(2,1)} %collective-permute-done.21.refs_1_.refs_9_, bf16[512,2048]{1,0:T(8,128)(2,1)} %collective-permute-done.15.refs_2_.refs_10_, ...), custom_call_target="tpu_custom_call" | custom-call | flops 4026531840 | bytes 16252928 | tf_op jit(solution)/shard_map/pallas_call | solution.py:276
  314.8 7.5 %shard_map.107.q_ref = f32[512,512]{1,0:T(8,128)S(1)} custom-call(s32[1,2,5]{2,1,0:T(2,128)S(1)} %copy-done.16, bf16[512,2048]{1,0:T(8,128)(2,1)} %collective-permute-done.10.refs_0_.refs_8_, bf16[512,2048]{1,0:T(8,128)(2,1)} %collective-permute-done.21.refs_1_.refs_9_, bf16[512,2048]{1,0:T(8,128)(2,1)} %collective-permute-done.15.refs_2_.refs_10_, ...), custom_call_target="tpu_custom_call" | custom-call | flops 2684354560 | bytes 12582912 | tf_op jit(solution)/shard_map/pallas_call | solution.py:276
  326.4 7.5 %shard_map.106.q_ref = f32[512,512]{1,0:T(8,128)S(1)} custom-call(s32[1,2,5]{2,1,0:T(2,128)S(1)} %copy-done.16, bf16[512,2048]{1,0:T(8,128)(2,1)} %collective-permute-done.10.refs_0_.refs_8_, bf16[512,2048]{1,0:T(8,128)(2,1)} %collective-permute-done.21.refs_1_.refs_9_, bf16[512,2048]{1,0:T(8,128)(2,1)} %collective-permute-done.15.refs_2_.refs_10_, ...), custom_call_target="tpu_custom_call" | custom-call | flops 2684354560 | bytes 12582912 | tf_op jit(solution)/shard_map/pallas_call | solution.py:276
  333.9 2.2 shard_map.108
  338.0 21.9 %shard_map.111 = (f32[512,256]{1,0:T(8,128)S(1)}, f32[512,256]{1,0:T(8,128)S(1)}, f32[512,256]{1,0:T(8,128)S(1)}, f32[512,256]{1,0:T(8,128)}) custom-call(s32[4,2,5]{2,1,0:T(2,128)S(1)} %copy-done.19, bf16[512,2048]{1,0:T(8,128)(2,1)} %collective-permute-done.5.refs_0_.refs_4_, bf16[512,2048]{1,0:T(8,128)(2,1)} %collective-permute-done.16.refs_1_.refs_5_, ...), custom_call_target="tpu_custom_call" | custom-call | flops 5368709120 | bytes 27787264 | tf_op jit(solution)/shard_map/pallas_call | solution.py:276
  372.6 15.3 %collective-permute-done.29 = bf16[512,256]{1,0:T(8,128)(2,1)S(1)} collective-permute-done((bf16[512,256]{1,0:T(8,128)(2,1)S(1)}, bf16[512,256]{1,0:T(8,128)(2,1)S(1)}, u32[]{:S(2)}, u32[]{:S(2)}) %collective-permute-start.29) | collective-permute-done | bytes 262176 | tf_op jit(solution)/shard_map/ppermute | solution.py:321
  (241 shorter events, 86.0 us)
Async XLA Ops:
  0.6 199.0 %copy-start = (f32[2,1024]{1,0:T(2,128)S(1)}, f32[2,1024]{1,0:T(2,128)}, u32[]{:S(2)}) copy-start(f32[2,1024]{1,0:T(2,128)} %param.13) | copy-start | bytes 24580
  7.3 64.8 %collective-permute-start = (bf16[1024,1280]{1,0:T(8,128)(2,1)}, bf16[1024,1280]{1,0:T(8,128)(2,1)}, u32[]{:S(2)}, u32[]{:S(2)}) collective-permute-start(bf16[1024,1280]{1,0:T(8,128)(2,1)} %pad_maximum_fusion.1), channel_id=1, source_target_pairs={{0,4},{4,0},{8,12},{12,8},{16,20},{20,16},{24,28},{28,24},{1,5},{5... | collective-permute-start | bytes 7864328 | tf_op jit(solution)/shard_map/ppermute | solution.py:321
  12.1 60.0 %collective-permute-start.1 = (bf16[1024,1280]{1,0:T(8,128)(2,1)}, bf16[1024,1280]{1,0:T(8,128)(2,1)}, u32[]{:S(2)}, u32[]{:S(2)}) collective-permute-start(bf16[1024,1280]{1,0:T(8,128)(2,1)} %pad_maximum_fusion.refs_1_.refs_4_), channel_id=1, source_target_pairs={{8,16},{12,20},{16,8},{20,12},{9,17},{13,21},{17,9},{21,13},{10,18... | collective-permute-start | bytes 7864328 | tf_op jit(solution)/shard_map/ppermute | solution.py:321
  23.0 49.1 %collective-permute-start.2 = (bf16[512,2048]{1,0:T(8,128)(2,1)S(1)}, bf16[512,2048]{1,0:T(8,128)(2,1)}, u32[]{:S(2)}, u32[]{:S(2)}) collective-permute-start(bf16[512,2048]{1,0:T(8,128)(2,1)S(1)} %get-tuple-element.75), channel_id=1, source_target_pairs={{0,8},{4,12},{24,16},{28,20},{1,9},{5,13},{25,17},{29,21},{2,10},{... | collective-permute-start | bytes 6291464 | tf_op jit(solution)/shard_map/ppermute | solution.py:321
  72.1 63.3 %collective-permute-start.5 = (bf16[512,2048]{1,0:T(8,128)(2,1)}, bf16[512,2048]{1,0:T(8,128)(2,1)}, u32[]{:S(2)}, u32[]{:S(2)}) collective-permute-start(bf16[512,2048]{1,0:T(8,128)(2,1)} %collective-permute-done.2.refs_0_.refs_4_), channel_id=1, source_target_pairs={{8,12},{12,8},{16,20},{20,16},{9,13},{13,9},{17,21},{21,17},{10,14... | collective-permute-start | bytes 6291464 | tf_op jit(solution)/shard_map/ppermute | solution.py:321
  74.2 61.2 %collective-permute-start.6 = (bf16[512,2048]{1,0:T(8,128)(2,1)}, bf16[512,2048]{1,0:T(8,128)(2,1)S(1)}, u32[]{:S(2)}, u32[]{:S(2)}) collective-permute-start(bf16[512,2048]{1,0:T(8,128)(2,1)} %collective-permute-done.2.refs_0_.refs_4_), channel_id=1, source_target_pairs={{0,2},{1,3},{2,0},{3,1},{4,6},{5,7},{6,4},{7,5},{8,10},{9,11},{10,... | collective-permute-start | bytes 6291464 | tf_op jit(solution)/shard_map/ppermute | solution.py:330
  75.7 59.7 %collective-permute-start.7 = (bf16[512,2048]{1,0:T(8,128)(2,1)}, bf16[512,2048]{1,0:T(8,128)(2,1)S(1)}, u32[]{:S(2)}, u32[]{:S(2)}) collective-permute-start(bf16[512,2048]{1,0:T(8,128)(2,1)} %collective-permute-done.2.refs_0_.refs_4_), channel_id=1, source_target_pairs={{0,1},{1,0},{2,3},{3,2},{4,5},{5,4},{6,7},{7,6},{8,9},{9,8},{10,11... | collective-permute-start | bytes 6291464 | tf_op jit(solution)/shard_map/ppermute | solution.py:333
  78.8 27.0 %collective-permute-start.3 = (bf16[1024,1024]{1,0:T(8,128)(2,1)}, bf16[1024,1024]{1,0:T(8,128)(2,1)S(1)}, u32[]{:S(2)}, u32[]{:S(2)}) collective-permute-start(bf16[1024,1024]{1,0:T(8,128)(2,1)} %slice.114), channel_id=1, source_target_pairs={{8,16},{12,20},{16,8},{20,12},{9,17},{13,21},{17,9},{21,13},{10,18... | collective-permute-start | bytes 6291464 | tf_op jit(solution)/shard_map/ppermute | solution.py:321
  82.8 52.6 %collective-permute-start.4 = (bf16[2,1024,512]{2,1,0:T(8,128)(2,1)}, bf16[2,1024,512]{2,1,0:T(8,128)(2,1)}, u32[]{:S(2)}, u32[]{:S(2)}) collective-permute-start(bf16[2,1024,512]{2,1,0:T(8,128)(2,1)} %pad_maximum_fusion.2), channel_id=1, source_target_pairs={{0,8},{4,12},{24,16},{28,20},{1,9},{5,13},{25,17},{29,21},{2,10},{... | collective-permute-start | bytes 6291464 | tf_op jit(solution)/shard_map/ppermute | solution.py:321
  135.4 27.2 %collective-permute-start.8 = (bf16[2,1024,512]{2,1,0:T(8,128)(2,1)}, bf16[2,1024,512]{2,1,0:T(8,128)(2,1)}, u32[]{:S(2)}, u32[]{:S(2)}) collective-permute-start(bf16[2,1024,512]{2,1,0:T(8,128)(2,1)} %collective-permute-done.4.refs_10_.refs_11_.refs_5_.refs_6_), channel_id=1, source_target_pairs={{8,16},{12,20},{16,8},{20,12},{9,17},{13,21},{17,9},{21,13},{10,18... | collective-permute-start | bytes 6291464 | tf_op jit(solution)/shard_map/ppermute | solution.py:321
  139.1 12.3 %collective-permute-start.12 = (bf16[512,2048]{1,0:T(8,128)(2,1)S(1)}, bf16[512,2048]{1,0:T(8,128)(2,1)S(1)}, u32[]{:S(2)}, u32[]{:S(2)}) collective-permute-start(bf16[512,2048]{1,0:T(8,128)(2,1)S(1)} %collective-permute-done.6.refs_2_.refs_6_), channel_id=1, source_target_pairs={{0,1},{1,0},{2,3},{3,2},{4,5},{5,4},{6,7},{7,6},{8,9},{9,8},{10,11... | collective-permute-start | bytes 6291464 | tf_op jit(solution)/shard_map/ppermute | solution.py:333
  142.0 50.7 %collective-permute-start.9 = (bf16[2,1024,512]{2,1,0:T(8,128)(2,1)}, bf16[2,1024,512]{2,1,0:T(8,128)(2,1)}, u32[]{:S(2)}, u32[]{:S(2)}) collective-permute-start(bf16[2,1024,512]{2,1,0:T(8,128)(2,1)} %pad_maximum_fusion.3), channel_id=1, source_target_pairs={{0,8},{4,12},{24,16},{28,20},{1,9},{5,13},{25,17},{29,21},{2,10},{... | collective-permute-start | bytes 6291464 | tf_op jit(solution)/shard_map/ppermute | solution.py:321
  148.2 44.6 %collective-permute-start.10 = (bf16[512,2048]{1,0:T(8,128)(2,1)S(1)}, bf16[512,2048]{1,0:T(8,128)(2,1)}, u32[]{:S(2)}, u32[]{:S(2)}) collective-permute-start(bf16[512,2048]{1,0:T(8,128)(2,1)S(1)} %copy-done.21), channel_id=1, source_target_pairs={{8,12},{12,8},{16,20},{20,16},{9,13},{13,9},{17,21},{21,17},{10,14... | collective-permute-start | bytes 6291464 | tf_op jit(solution)/shard_map/ppermute | solution.py:321
  150.7 48.1 %collective-permute-start.11 = (bf16[512,2048]{1,0:T(8,128)(2,1)}, bf16[512,2048]{1,0:T(8,128)(2,1)}, u32[]{:S(2)}, u32[]{:S(2)}) collective-permute-start(bf16[512,2048]{1,0:T(8,128)(2,1)} %collective-permute-done.5.refs_0_.refs_4_), channel_id=1, source_target_pairs={{0,2},{1,3},{2,0},{3,1},{4,6},{5,7},{6,4},{7,5},{8,10},{9,11},{10,... | collective-permute-start | bytes 6291464 | tf_op jit(solution)/shard_map/ppermute | solution.py:330
  198.9 9.4 %collective-permute-start.16 = (bf16[512,2048]{1,0:T(8,128)(2,1)}, bf16[512,2048]{1,0:T(8,128)(2,1)}, u32[]{:S(2)}, u32[]{:S(2)}) collective-permute-start(bf16[512,2048]{1,0:T(8,128)(2,1)} %collective-permute-done.5.refs_0_.refs_4_), channel_id=1, source_target_pairs={{0,1},{1,0},{2,3},{3,2},{4,5},{5,4},{6,7},{7,6},{8,9},{9,8},{10,11... | collective-permute-start | bytes 6291464 | tf_op jit(solution)/shard_map/ppermute | solution.py:333
  198.9 9.4 %collective-permute-start.17 = (bf16[512,2048]{1,0:T(8,128)(2,1)}, bf16[512,2048]{1,0:T(8,128)(2,1)}, u32[]{:S(2)}, u32[]{:S(2)}) collective-permute-start(bf16[512,2048]{1,0:T(8,128)(2,1)} %collective-permute-done.11.refs_2_.refs_6_), channel_id=1, source_target_pairs={{0,1},{1,0},{2,3},{3,2},{4,5},{5,4},{6,7},{7,6},{8,9},{9,8},{10,11... | collective-permute-start | bytes 6291464 | tf_op jit(solution)/shard_map/ppermute | solution.py:333
  199.6 68.3 %copy-start.15 = (s32[1,2,5]{2,1,0:T(2,128)}, s32[1,2,5]{2,1,0:T(2,128)S(1)}, u32[]{:S(2)}) copy-start(s32[1,2,5]{2,1,0:T(2,128)S(1)} %get-tuple-element.206.pick_ref) | copy-start | bytes 124
  200.1 48.6 %collective-permute-start.13 = (bf16[2,1024,512]{2,1,0:T(8,128)(2,1)}, bf16[2,1024,512]{2,1,0:T(8,128)(2,1)}, u32[]{:S(2)}, u32[]{:S(2)}) collective-permute-start(bf16[2,1024,512]{2,1,0:T(8,128)(2,1)} %collective-permute-done.9.refs_10_.refs_11_.refs_5_.refs_6_), channel_id=1, source_target_pairs={{8,16},{12,20},{16,8},{20,12},{9,17},{13,21},{17,9},{21,13},{10,18... | collective-permute-start | bytes 6291464 | tf_op jit(solution)/shard_map/ppermute | solution.py:321
  204.4 44.3 %collective-permute-start.14 = (bf16[2,1024,256]{2,1,0:T(8,128)(2,1)S(1)}, bf16[2,1024,256]{2,1,0:T(8,128)(2,1)}, u32[]{:S(2)}, u32[]{:S(2)}) collective-permute-start(bf16[2,1024,256]{2,1,0:T(8,128)(2,1)S(1)} %pad_maximum_fusion.5), channel_id=1, source_target_pairs={{0,8},{4,12},{24,16},{28,20},{1,9},{5,13},{25,17},{29,21},{2,10},{... | collective-permute-start | bytes 3145736 | tf_op jit(solution)/shard_map/ppermute | solution.py:321
  207.7 47.3 %collective-permute-start.15 = (bf16[512,2048]{1,0:T(8,128)(2,1)}, bf16[512,2048]{1,0:T(8,128)(2,1)}, u32[]{:S(2)}, u32[]{:S(2)}) collective-permute-start(bf16[512,2048]{1,0:T(8,128)(2,1)} %collective-permute-done.10.refs_0_.refs_8_), channel_id=1, source_target_pairs={{0,2},{1,3},{2,0},{3,1},{4,6},{5,7},{6,4},{7,5},{8,10},{9,11},{10,... | collective-permute-start | bytes 6291464 | tf_op jit(solution)/shard_map/ppermute | solution.py:330
  240.6 17.0 %collective-permute-start.18 = (bf16[512,512]{1,0:T(8,128)(2,1)S(1)}, bf16[512,512]{1,0:T(8,128)(2,1)}, u32[]{:S(2)}, u32[]{:S(2)}) collective-permute-start(bf16[512,512]{1,0:T(8,128)(2,1)S(1)} %pad_maximum_fusion.6), channel_id=1, source_target_pairs={{8,0},{12,4},{16,24},{20,28},{9,1},{13,5},{17,25},{21,29},{10,2},{... | collective-permute-start | bytes 1572872 | tf_op jit(solution)/shard_map/ppermute | solution.py:321
  244.3 23.1 %collective-permute-start.19 = (bf16[512,512]{1,0:T(8,128)(2,1)S(1)}, bf16[512,512]{1,0:T(8,128)(2,1)}, u32[]{:S(2)}, u32[]{:S(2)}) collective-permute-start(bf16[512,512]{1,0:T(8,128)(2,1)S(1)} %pad_maximum_fusion.7), channel_id=1, source_target_pairs={{8,4},{12,0},{16,28},{20,24},{9,5},{13,1},{17,29},{21,25},{10,6},{... | collective-permute-start | bytes 1572872 | tf_op jit(solution)/shard_map/ppermute | solution.py:321
  267.4 37.4 %collective-permute-start.21 = (bf16[512,2048]{1,0:T(8,128)(2,1)}, bf16[512,2048]{1,0:T(8,128)(2,1)}, u32[]{:S(2)}, u32[]{:S(2)}) collective-permute-start(bf16[512,2048]{1,0:T(8,128)(2,1)} %collective-permute-done.10.refs_0_.refs_8_), channel_id=1, source_target_pairs={{0,1},{1,0},{2,3},{3,2},{4,5},{5,4},{6,7},{7,6},{8,9},{9,8},{10,11... | collective-permute-start | bytes 6291464 | tf_op jit(solution)/shard_map/ppermute | solution.py:333
  267.4 37.4 %collective-permute-start.22 = (bf16[512,2048]{1,0:T(8,128)(2,1)}, bf16[512,2048]{1,0:T(8,128)(2,1)}, u32[]{:S(2)}, u32[]{:S(2)}) collective-permute-start(bf16[512,2048]{1,0:T(8,128)(2,1)} %collective-permute-done.15.refs_2_.refs_10_), channel_id=1, source_target_pairs={{0,1},{1,0},{2,3},{3,2},{4,5},{5,4},{6,7},{7,6},{8,9},{9,8},{10,11... | collective-permute-start | bytes 6291464 | tf_op jit(solution)/shard_map/ppermute | solution.py:333
  291.7 79.4 %collective-permute-start.27 = (bf16[512,512]{1,0:T(8,128)(2,1)S(1)}, bf16[512,512]{1,0:T(8,128)(2,1)S(1)}, u32[]{:S(2)}, u32[]{:S(2)}) collective-permute-start(bf16[512,512]{1,0:T(8,128)(2,1)S(1)} %shard_map.110), channel_id=1, source_target_pairs={{8,4},{12,0},{16,28},{20,24},{9,5},{13,1},{17,29},{21,25},{10,6},{... | collective-permute-start | bytes 1572872 | tf_op jit(solution)/shard_map/ppermute | solution.py:321
  296.8 40.0 %collective-permute-start.20 = (bf16[3,1024,256]{2,1,0:T(8,128)(2,1)}, bf16[3,1024,256]{2,1,0:T(8,128)(2,1)S(1)}, u32[]{:S(2)}, u32[]{:S(2)}) collective-permute-start(bf16[3,1024,256]{2,1,0:T(8,128)(2,1)} %pad_maximum_fusion.4), channel_id=1, source_target_pairs={{8,16},{12,20},{16,8},{20,12},{9,17},{13,21},{17,9},{21,13},{10,18... | collective-permute-start | bytes 4718600 | tf_op jit(solution)/shard_map/ppermute | solution.py:321
  300.1 88.6 %collective-permute-start.23 = (bf16[512,512]{1,0:T(8,128)(2,1)S(1)}, bf16[512,512]{1,0:T(8,128)(2,1)}, u32[]{:S(2)}, u32[]{:S(2)}) collective-permute-start(bf16[512,512]{1,0:T(8,128)(2,1)S(1)} %shard_map.109), channel_id=1, source_target_pairs={{8,0},{12,4},{16,24},{20,28},{9,1},{13,5},{17,25},{21,29},{10,2},{... | collective-permute-start | bytes 1572872 | tf_op jit(solution)/shard_map/ppermute | solution.py:321
  325.3 42.7 %collective-permute-start.25 = (bf16[512,512]{1,0:T(8,128)(2,1)}, bf16[512,512]{1,0:T(8,128)(2,1)S(1)}, u32[]{:S(2)}, u32[]{:S(2)}) collective-permute-start(bf16[512,512]{1,0:T(8,128)(2,1)} %pad_maximum_fusion.9), channel_id=1, source_target_pairs={{8,12},{12,8},{16,20},{20,16},{9,13},{13,9},{17,21},{21,17},{10,14... | collective-permute-start | bytes 1572872 | tf_op jit(solution)/shard_map/ppermute | solution.py:321
  336.1 36.3 %collective-permute-start.26 = (bf16[512,512]{1,0:T(8,128)(2,1)S(1)}, bf16[512,512]{1,0:T(8,128)(2,1)S(1)}, u32[]{:S(2)}, u32[]{:S(2)}) collective-permute-start(bf16[512,512]{1,0:T(8,128)(2,1)S(1)} %shard_map.108), channel_id=1, source_target_pairs={{8,12},{12,8},{16,20},{20,16},{9,13},{13,9},{17,21},{21,17},{10,14... | collective-permute-start | bytes 1572872 | tf_op jit(solution)/shard_map/ppermute | solution.py:321
  361.7 10.8 %collective-permute-start.28 = (bf16[512,256]{1,0:T(8,128)(2,1)S(1)}, bf16[512,256]{1,0:T(8,128)(2,1)S(1)}, u32[]{:S(2)}, u32[]{:S(2)}) collective-permute-start(bf16[512,256]{1,0:T(8,128)(2,1)S(1)} %shard_map.115), channel_id=1, source_target_pairs={{8,12},{12,8},{16,20},{20,16},{9,13},{13,9},{17,21},{21,17},{10,14... | collective-permute-start | bytes 786440 | tf_op jit(solution)/shard_map/ppermute | solution.py:321
  367.9 19.9 %collective-permute-start.29 = (bf16[512,256]{1,0:T(8,128)(2,1)S(1)}, bf16[512,256]{1,0:T(8,128)(2,1)S(1)}, u32[]{:S(2)}, u32[]{:S(2)}) collective-permute-start(bf16[512,256]{1,0:T(8,128)(2,1)S(1)} %shard_map.116), channel_id=1, source_target_pairs={{8,4},{12,0},{16,28},{20,24},{9,5},{13,1},{17,29},{21,25},{10,6},{... | collective-permute-start | bytes 786440 | tf_op jit(solution)/shard_map/ppermute | solution.py:321
  371.1 20.5 %collective-permute-start.24 = (bf16[512,256]{1,0:T(8,128)(2,1)S(1)}, bf16[512,256]{1,0:T(8,128)(2,1)S(1)}, u32[]{:S(2)}, u32[]{:S(2)}) collective-permute-start(bf16[512,256]{1,0:T(8,128)(2,1)S(1)} %shard_map.113), channel_id=1, source_target_pairs={{8,0},{12,4},{16,24},{20,28},{9,1},{13,5},{17,25},{21,29},{10,2},{... | collective-permute-start | bytes 786440 | tf_op jit(solution)/shard_map/ppermute | solution.py:321
  (45 other events, 586.5 us)

commit v4 on v3

--- a/solution.py
+++ b/solution.py
@@ -213,21 +213,26 @@
     totals = take(sets) if with_totals else [None] * sets
     outs = take(sets)
     row_buf, weight_buf, row_sem, weight_sem = refs
-    depth = weight_buf.shape[1]
+    depth = weight_buf.shape[0] // count
+    tokens = row_buf.shape[0] // sets
 
     def weight_copy(piece):
         ref, lead = weight_refs[piece], leads[piece]
         ref = ref if lead is None else ref.at[lead]
         skip = first_col if ref.shape[1] > width else 0
         return pltpu.make_async_copy(
-            ref.at[:, skip : skip + width], weight_buf.at[piece], weight_sem.at[piece]
+            ref.at[:, skip : skip + width],
+            weight_buf.at[piece * depth : (piece + 1) * depth],
+            weight_sem.at[piece],
         )
 
     def row_copy(which, piece, source):
         at = pl.multiple_of(pick_ref[which, 1, piece] * depth, depth)
         return pltpu.make_async_copy(
             row_refs[which][source].at[:, pl.ds(at, depth)],
-            row_buf.at[which, piece],
+            row_buf.at[
+                which * tokens : (which + 1) * tokens, piece * depth : (piece + 1) * depth
+            ],
             row_sem.at[which, piece],
         )
 
@@ -243,19 +248,28 @@
                     def _():
                         row_copy(which, piece, source).start()
 
-    for piece in range(count):
-        weight_copy(piece).wait()
+    done = 0
+    for ready in (count // 2, count):
+        for piece in range(done, ready):
+            weight_copy(piece).wait()
+            for which in range(sets):
+                row_copy(which, piece, 0).wait()
+        low, high = done * depth, ready * depth
         for which in range(sets):
-            row_copy(which, piece, 0).wait()
-            term = jnp.dot(
-                row_buf[which, piece], weight_buf[piece], preferred_element_type=jnp.float32
-            )
-            if piece > 0:
-                outs[which][...] += term
-            elif totals[which] is None:
-                outs[which][...] = term
-            else:
-                outs[which][...] = totals[which][...] + term
+            for col in range(0, width, 2 * HD):
+                cols = slice(col, col + 2 * HD)
+                term = jnp.dot(
+                    row_buf[which * tokens : (which + 1) * tokens, low:high],
+                    weight_buf[low:high, cols],
+                    preferred_element_type=jnp.float32,
+                )
+                if done > 0:
+                    outs[which][:, cols] += term
+                elif totals[which] is None:
+                    outs[which][:, cols] = term
+                else:
+                    outs[which][:, cols] = totals[which][:, cols] + term
+        done = ready
 
 
 def project(row_sets, picks, pieces, first_col, width, totals=None):
@@ -283,8 +297,8 @@
             in_specs=in_specs,
             out_specs=[out] * sets,
             scratch_shapes=[
-                pltpu.VMEM((sets, count, tokens, depth), jnp.bfloat16),
-                pltpu.VMEM((count, depth, width), jnp.bfloat16),
+                pltpu.VMEM((sets * tokens, count * depth), jnp.bfloat16),
+                pltpu.VMEM((count * depth, width), jnp.bfloat16),
                 pltpu.SemaphoreType.DMA((sets, count)),
                 pltpu.SemaphoreType.DMA((count,)),
             ],
@@ -303,6 +317,10 @@
 ENDS = (0, 1, 6, 7)
 
 
+def after(value, *others):
+    return lax.optimization_barrier((value,) + others)[0]
+
+
 def pairs_from(sources, code):
     return [(s, s ^ code) for s in sources]
 
@@ -374,11 +392,12 @@
     bias = lax.dynamic_slice_in_dim(q_bias, y * half_cols, half_cols, 0)[None, :]
     kv_bias_here = lax.dynamic_slice_in_dim(kv_bias, (2 * tensor + y) * HD, HD, 1)
     inverse_freq = THETA ** (-2.0 * jnp.arange(HD // 2, dtype=jnp.float32) / HD)
+    m_swap = across_middle(after(swap, m_own))
     own, swap, m_own, normed, quarter, end2 = barrier((own, swap, m_own, normed, quarter, end2))
 
     rows_of = {0: [normed]}
-    m_swap = across_middle(swap[:, : begin[2]])
     e0 = to_middle(both(own, swap, 0))
+    next1, next2 = both(own, swap, 1), both(own, swap, 2)
     end3 = over_group(end2, MIDDLE, 1)
     across2 = over_x(end2)
     twin2 = over_core(end2)
@@ -392,24 +411,24 @@
         cosine = jnp.concatenate([cosine, cosine], axis=1)
         sine = jnp.concatenate([-sine, sine], axis=1)
         tables.append((cosine, sine, (places - offset)[:, None]))
-    (own, swap, m_swap, e0, end2, end3, across2, twin2, sums[0], tables, quarter) = barrier(
-        (own, swap, m_swap, e0, end2, end3, across2, twin2, sums[0], tables, quarter)
-    )
-
-    m_e0 = across_middle(e0)
-    e1 = to_middle(both(own, swap, 1))
+    m_e0 = across_middle(after(e0, m_swap))
+    (next1, next2, m_swap, e0, end2, end3, across2, twin2, sums[0], tables, quarter) = barrier(
+        (next1, next2, m_swap, e0, end2, end3, across2, twin2, sums[0], tables, quarter)
+    )
+
+    e1 = to_middle(next1)
     end1 = over_group(quarter, MIDDLE, 1)
     across3 = over_x(end3)
     far2 = over_core(across2)
     rows_of[2] = [end2, twin2, across2, far2]
     sums[2] = projected([2], (0, 1, 6), early, None)[0]
-    (own, swap, m_e0, e0, e1, end1, end3, across3, far2, sums[2]) = barrier(
-        (own, swap, m_e0, e0, e1, end1, end3, across3, far2, sums[2])
+    m_e1 = across_middle(after(e1, m_e0))
+    (next2, m_e0, e0, e1, end1, end3, across3, far2, sums[2]) = barrier(
+        (next2, m_e0, e0, e1, end1, end3, across3, far2, sums[2])
     )
     rows_of[2] = [end2, twin2, across2, far2]
 
-    m_e1 = across_middle(e1)
-    e2 = to_middle(both(own, swap, 2))
+    e2 = to_middle(next2)
     across1 = over_x(end1)
     twin3 = over_core(end3)
     far3 = over_core(across3)
@@ -445,35 +464,36 @@
 
     late = (7, 2, 3, 4, 5)
     late0 = {7: (m_swap, None), 2: (e0, 0), 3: (e0, 1), 4: (m_e0, 0), 5: (m_e0, 1)}
+    late1 = {7: (m_swap, None), 2: (e1, 0), 3: (e1, 1)}
     three = (2, 3, 0)
     totals = projected(three, late, late0, 0, [sums[c] for c in three])
     for code, total in zip(three, totals):
         attended(code, 0, total)
     back = {(code, 0): send_back(code, 0) for code in (2, 3)}
-    (swap, m_e1, e1, e2, end1, across1, back[2, 0], back[3, 0], outs[0, 0], sums[3]) = barrier(
-        (swap, m_e1, e1, e2, end1, across1, back[2, 0], back[3, 0], outs[0, 0], sums[3])
-    )
-
-    last = jnp.concatenate([swap[None, :, begin[2] :], e2])
-    m_last = across_middle(last)
+    part1 = projected(three, late[:3], late1, 1, [sums[c] for c in three])
+    m_e2 = across_middle(after(e2, m_e1))
+    (m_e1, e2, end1, across1, outs[0, 0], part1, sums[3]) = barrier(
+        (m_e1, e2, end1, across1, outs[0, 0], part1, sums[3])
+    )
+
     twin1 = over_core(end1)
     far1 = over_core(across1)
     rows_of[1] = [end1, twin1, across1, far1]
-    late1 = {7: (m_swap, None), 2: (e1, 0), 3: (e1, 1), 4: (m_e1, 0), 5: (m_e1, 1)}
-    totals = projected(three, late, late1, 1, [sums[c] for c in three])
+    late1 = {**late1, 4: (m_e1, 0), 5: (m_e1, 1)}
+    totals = projected(three, late[3:], late1, 1, part1)
     for code, total in zip(three, totals):
         attended(code, 1, total)
+    for code in (2, 3):
+        back[code, 1] = send_back(code, 1)
     sums[1] = projected([1], (0, 1, 6), early, None)[0]
     for chunk, pieces in ((0, late0), (1, late1)):
         attended(1, chunk, projected([1], late, pieces, chunk, [sums[1]])[0])
-    back[1, 0] = send_back(1, 0)
-    for code in (2, 3, 1):
-        back[code, 1] = send_back(code, 1)
-    (m_last, *ready) = barrier((m_last, *[outs[c, 1] for c in range(4)]))
+        back[1, chunk] = send_back(1, chunk)
+    (m_e2, *ready) = barrier((m_e2, *[outs[c, 1] for c in range(4)]))
     for code in range(4):
         outs[code, 1] = ready[code]
 
-    late2 = {7: (m_last, 0), 2: (e2, 0), 3: (e2, 1), 4: (m_last, 1), 5: (m_last, 2)}
+    late2 = {7: (m_swap, None), 2: (e2, 0), 3: (e2, 1), 4: (m_e2, 0), 5: (m_e2, 1)}
     order = (3, 2, 1, 0)
     totals = projected(order, late, late2, 2, [sums[c] for c in order])
     for code, total in zip(order, totals):

time: 406 us -> 384 us (0.946)
  waiting for transfers between devices: 143 us -> 123 us
  local copies, waits for them, and re-layouts: 30.9 us -> 24.9 us
  starting transfers between devices: 55 us -> 60 us
    ppermute x21, waiting for transfers between devices: 131 us -> 115 us  [over_group(): return lax.ppermute(value, 'group', pairs_from(sources, code))]
    ppermute x21, starting transfers between devices: 51.3 us -> 56.3 us  [over_group(): return lax.ppermute(value, 'group', pairs_from(sources, code))]
    ppermute x3, waiting for transfers between devices: 12.5 us -> 7.52 us  [over_x(): return lax.ppermute(value, 'tensor', pairs_from(range(4), 2))]
    pallas_call x9 -> x10, Pallas kernels: 114 us -> 111 us  [project(): pl.pallas_call(functools.partial(project_kernel, sources, leads, first_co...]
    unnamed x97 -> x93, local copies, waits for them, and re-layouts: 9.02 us -> 9.87 us
  transfers between devices with their start and end apart: 30 -> 30, of which waited for: 9 -> 7; matrix products, arithmetic and copies ran while one was open for 9% -> 7% of each run, Pallas kernels for 35% -> 37%
where the time goes in v4:
time: 384 us; the launch traced here: 377 us
  Pallas kernels  140 us (36%)
  waiting for transfers between devices  123 us (32%)
  starting transfers between devices  60 us (16%)
  other arithmetic  26.9 us (7%)
  local copies, waits for them, and re-layouts  24.9 us (6%)
    ppermute x21, waiting for transfers between devices, over_group(): return lax.ppermute(value, 'group', pairs_from(sources, code))  115 us
    pallas_call x10, Pallas kernels, project(): pl.pallas_call(functools.partial(project_kernel, sources, leads, first_co...  111 us
    ppermute x21, starting transfers between devices, over_group(): return lax.ppermute(value, 'group', pairs_from(sources, code))  56.3 us
    pallas_call x12, Pallas kernels, attend(): pl.pallas_call(attention_kernel, out_shape=jax.ShapeDtypeStruct((rows, he...  23 us
    unnamed x93, local copies, waits for them, and re-layouts  9.87 us
  transfers between devices with their start and end apart: 30, of which 7 were waited for; matrix products, arithmetic and copies ran while one was open for 7% of the time, Pallas kernels for 37%

profile of v4, /device:TPU:0, one launch (start us, length us, event | category | flops | bytes accessed | tf_op | source)
XLA Modules:
  0.0 376.9 jit_solution(16492912835896418113)
XLA Ops:
  2.7 2.8 constant_dynamic-slice_fusion.1
  7.3 3.0 collective-permute-start
  10.6 2.4 collective-permute-start.1
  13.0 6.2 %shard_map.95 = (bf16[512,8192]{1,0:T(8,128)(2,1)S(1)}, bf16[512,2048]{1,0:T(8,128)(2,1)}) custom-call(s32[1]{0:T(128)} %bitcast.part_ref, bf16[512,8192]{1,0:T(8,128)(2,1)S(1)} %bitcast.79, f32[1,8192]{1,0:T(1,128)S(1)} %bitcast.80), custom_call_target="tpu_custom_call" | custom-call | flops 16777216 | bytes 20971520 | tf_op jit(solution)/shard_map/pallas_call | solution.py:177
  19.2 3.3 copy-done.2
  22.5 5.9 %collective-permute-start.2 = (bf16[512,2048]{1,0:T(8,128)(2,1)}, bf16[512,2048]{1,0:T(8,128)(2,1)}, u32[]{:S(2)}, u32[]{:S(2)}) collective-permute-start(bf16[512,2048]{1,0:T(8,128)(2,1)} %get-tuple-element.83), channel_id=1, source_target_pairs={{0,8},{4,12},{24,16},{28,20},{1,9},{5,13},{25,17},{29,21},{2,10},{... | collective-permute-start | bytes 6291464 | tf_op jit(solution)/shard_map/ppermute | solution.py:339
  29.8 3.7 fusion.20
  33.6 38.2 %collective-permute-done.2.refs_0_.refs_4_ = bf16[512,2048]{1,0:T(8,128)(2,1)} collective-permute-done((bf16[512,2048]{1,0:T(8,128)(2,1)}, bf16[512,2048]{1,0:T(8,128)(2,1)}, u32[]{:S(2)}, u32[]{:S(2)}) %collective-permute-start.2) | collective-permute-done | bytes 2097184 | tf_op jit(solution)/shard_map/ppermute | solution.py:339
  75.2 2.2 collective-permute-start.3
  79.6 6.5 %collective-permute-start.4 = (bf16[2,1024,512]{2,1,0:T(8,128)(2,1)S(1)}, bf16[2,1024,512]{2,1,0:T(8,128)(2,1)}, u32[]{:S(2)}, u32[]{:S(2)}) collective-permute-start(bf16[2,1024,512]{2,1,0:T(8,128)(2,1)S(1)} %pad_maximum_fusion.3), channel_id=1, source_target_pairs={{0,8},{4,12},{24,16},{28,20},{1,9},{5,13},{25,17},{29,21},{2,10},{... | collective-permute-start | bytes 6291464 | tf_op jit(solution)/shard_map/ppermute | solution.py:339
  91.2 9.8 %shard_map.96.refs_16_.refs_14_.refs_21_ = f32[512,1280]{1,0:T(8,128)} custom-call(s32[1,2,3]{2,1,0:T(2,128)S(1)} %pad_bitcast_fusion.3.pick_ref, bf16[512,8192]{1,0:T(8,128)(2,1)} %copy-done.2, bf16[1024,1280]{1,0:T(8,128)(2,1)} %copy-done.18, bf16[1024,1280]{1,0:T(8,128)(2,1)} %collective-permute-done.refs_2_.refs_5_, ...), custom_call_target="tpu_custom_call" | custom-call | flops 4026531840 | bytes 16252928 | tf_op jit(solution)/shard_map/pallas_call | solution.py:290
  101.0 28.9 %collective-permute-done.4.refs_10_.refs_11_.refs_5_.refs_6_ = bf16[2,1024,512]{2,1,0:T(8,128)(2,1)} collective-permute-done((bf16[2,1024,512]{2,1,0:T(8,128)(2,1)S(1)}, bf16[2,1024,512]{2,1,0:T(8,128)(2,1)}, u32[]{:S(2)}, u32[]{:S(2)}) %collective-permute-start.4) | collective-permute-done | bytes 2097184 | tf_op jit(solution)/shard_map/ppermute | solution.py:339
  130.0 12.9 %collective-permute-start.8 = (bf16[2,1024,512]{2,1,0:T(8,128)(2,1)}, bf16[2,1024,512]{2,1,0:T(8,128)(2,1)}, u32[]{:S(2)}, u32[]{:S(2)}) collective-permute-start(bf16[2,1024,512]{2,1,0:T(8,128)(2,1)} %pad_maximum_fusion.2), channel_id=1, source_target_pairs={{0,8},{4,12},{24,16},{28,20},{1,9},{5,13},{25,17},{29,21},{2,10},{... | collective-permute-start | bytes 6291464 | tf_op jit(solution)/shard_map/ppermute | solution.py:339
  147.8 9.8 %shard_map.97.refs_14_.refs_12_.refs_19_ = f32[512,1280]{1,0:T(8,128)} custom-call(s32[1,2,3]{2,1,0:T(2,128)S(1)} %add_bitcast_fusion.pick_ref, bf16[512,2048]{1,0:T(8,128)(2,1)} %collective-permute-done.2.refs_0_.refs_4_, bf16[512,2048]{1,0:T(8,128)(2,1)} %collective-permute-done.7.refs_1_.refs_5_, ...), custom_call_target="tpu_custom_call" | custom-call | flops 4026531840 | bytes 16252928 | tf_op jit(solution)/shard_map/pallas_call | solution.py:290
  157.6 29.9 %collective-permute-done.8.refs_10_.refs_11_.refs_5_.refs_6_ = bf16[2,1024,512]{2,1,0:T(8,128)(2,1)} collective-permute-done((bf16[2,1024,512]{2,1,0:T(8,128)(2,1)}, bf16[2,1024,512]{2,1,0:T(8,128)(2,1)}, u32[]{:S(2)}, u32[]{:S(2)}) %collective-permute-start.8) | collective-permute-done | bytes 2097184 | tf_op jit(solution)/shard_map/ppermute | solution.py:339
  187.4 7.5 %collective-permute-done.12.refs_2_.refs_6_ = bf16[512,2048]{1,0:T(8,128)(2,1)} collective-permute-done((bf16[512,2048]{1,0:T(8,128)(2,1)}, bf16[512,2048]{1,0:T(8,128)(2,1)}, u32[]{:S(2)}, u32[]{:S(2)}) %collective-permute-start.12) | collective-permute-done | bytes 2097184 | tf_op jit(solution)/shard_map/ppermute | solution.py:348
  198.0 3.6 collective-permute-start.14
  202.5 9.8 %shard_map.98.refs_15_.refs_13_.refs_18_ = f32[512,1280]{1,0:T(8,128)} custom-call(s32[1,2,3]{2,1,0:T(2,128)S(1)} %add_bitcast_fusion.pick_ref, bf16[512,2048]{1,0:T(8,128)(2,1)} %collective-permute-done.5.refs_0_.refs_4_, bf16[512,2048]{1,0:T(8,128)(2,1)} %collective-permute-done.16.refs_1_.refs_5_, ...), custom_call_target="tpu_custom_call" | custom-call | flops 4026531840 | bytes 16252928 | tf_op jit(solution)/shard_map/pallas_call | solution.py:290
  212.3 17.6 %shard_map.99 = (f32[512,512]{1,0:T(8,128)S(1)}, f32[512,512]{1,0:T(8,128)}, f32[512,512]{1,0:T(8,128)}) custom-call(s32[3,2,5]{2,1,0:T(2,128)S(1)} %pad_add_fusion.1.pick_ref, bf16[512,2048]{1,0:T(8,128)(2,1)} %collective-permute-done.2.refs_0_.refs_4_, bf16[512,2048]{1,0:T(8,128)(2,1)} %collective-permute-done.7.refs_1_.refs_5_, ...), custom_call_target="tpu_custom_call" | custom-call | flops 8053063680 | bytes 27262976 | tf_op jit(solution)/shard_map/pallas_call | solution.py:290
  230.0 2.5 add_convert_fusion.2
  235.4 12.7 %shard_map.101 = (f32[512,512]{1,0:T(8,128)S(1)}, f32[512,512]{1,0:T(8,128)}, f32[512,512]{1,0:T(8,128)}) custom-call(s32[3,2,3]{2,1,0:T(2,128)S(1)} %pad_add_fusion.2.pick_ref, bf16[512,2048]{1,0:T(8,128)(2,1)} %collective-permute-done.2.refs_0_.refs_4_, bf16[512,2048]{1,0:T(8,128)(2,1)} %collective-permute-done.7.refs_1_.refs_5_, ...), custom_call_target="tpu_custom_call" | custom-call | flops 4831838208 | bytes 18874368 | tf_op jit(solution)/shard_map/pallas_call | solution.py:290
  262.8 9.9 %shard_map.103 = (f32[512,512]{1,0:T(8,128)S(1)}, f32[512,512]{1,0:T(8,128)}, f32[512,512]{1,0:T(8,128)}) custom-call(s32[3,2,2]{2,1,0:T(2,128)S(1)} %copy-done.17, bf16[512,2048]{1,0:T(8,128)(2,1)} %collective-permute-done.2.refs_0_.refs_4_, bf16[512,2048]{1,0:T(8,128)(2,1)} %collective-permute-done.7.refs_1_.refs_5_, ...), custom_call_target="tpu_custom_call" | custom-call | flops 3221225472 | bytes 14680064 | tf_op jit(solution)/shard_map/pallas_call | solution.py:290
  274.1 2.2 shard_map.110
  277.8 2.2 shard_map.104
  280.1 2.2 shard_map.109
  284.4 9.9 %shard_map.105.refs_9_.refs_20_ = f32[512,1280]{1,0:T(8,128)} custom-call(s32[1,2,3]{2,1,0:T(2,128)S(1)} %copy-done.15, bf16[512,2048]{1,0:T(8,128)(2,1)} %collective-permute-done.11.refs_0_.refs_8_, bf16[512,2048]{1,0:T(8,128)(2,1)} %collective-permute-done.20.refs_1_.refs_9_, bf16[512,2048]{1,0:T(8,128)(2,1)} %collective-permute-done.15.refs_2_.refs_10_, ...), custom_call_target="tpu_custom_call" | custom-call | flops 4026531840 | bytes 16252928 | tf_op jit(solution)/shard_map/pallas_call | solution.py:290
  294.3 7.7 %shard_map.107.q_ref = f32[512,512]{1,0:T(8,128)S(1)} custom-call(s32[1,2,5]{2,1,0:T(2,128)S(1)} %add_bitcast_fusion.1.pick_ref, bf16[512,2048]{1,0:T(8,128)(2,1)} %collective-permute-done.11.refs_0_.refs_8_, bf16[512,2048]{1,0:T(8,128)(2,1)} %collective-permute-done.20.refs_1_.refs_9_, bf16[512,2048]{1,0:T(8,128)(2,1)} %collective-permute-done.15.refs_2_.refs_10_, ...), custom_call_target="tpu_custom_call" | custom-call | flops 2684354560 | bytes 12582912 | tf_op jit(solution)/shard_map/pallas_call | solution.py:290
  306.4 7.7 %shard_map.106.q_ref = f32[512,512]{1,0:T(8,128)S(1)} custom-call(s32[1,2,5]{2,1,0:T(2,128)S(1)} %add_bitcast_fusion.1.pick_ref, bf16[512,2048]{1,0:T(8,128)(2,1)} %collective-permute-done.11.refs_0_.refs_8_, bf16[512,2048]{1,0:T(8,128)(2,1)} %collective-permute-done.20.refs_1_.refs_9_, bf16[512,2048]{1,0:T(8,128)(2,1)} %collective-permute-done.15.refs_2_.refs_10_, ...), custom_call_target="tpu_custom_call" | custom-call | flops 2684354560 | bytes 12582912 | tf_op jit(solution)/shard_map/pallas_call | solution.py:290
  314.1 2.2 shard_map.108
  317.3 15.8 %shard_map.111 = (f32[512,256]{1,0:T(8,128)S(1)}, f32[512,256]{1,0:T(8,128)S(1)}, f32[512,256]{1,0:T(8,128)S(1)}, f32[512,256]{1,0:T(8,128)}) custom-call(s32[4,2,5]{2,1,0:T(2,128)S(1)} %copy-done.16, bf16[512,2048]{1,0:T(8,128)(2,1)} %collective-permute-done.5.refs_0_.refs_4_, bf16[512,2048]{1,0:T(8,128)(2,1)} %collective-permute-done.16.refs_1_.refs_5_, ...), custom_call_target="tpu_custom_call" | custom-call | flops 5368709120 | bytes 27787264 | tf_op jit(solution)/shard_map/pallas_call | solution.py:290
  344.7 16.2 %collective-permute-done.29 = bf16[512,256]{1,0:T(8,128)(2,1)S(1)} collective-permute-done((bf16[512,256]{1,0:T(8,128)(2,1)S(1)}, bf16[512,256]{1,0:T(8,128)(2,1)S(1)}, u32[]{:S(2)}, u32[]{:S(2)}) %collective-permute-start.29) | collective-permute-done | bytes 262176 | tf_op jit(solution)/shard_map/ppermute | solution.py:339
  371.7 3.3 broadcast_select_fusion
  (243 shorter events, 76.1 us)
Async XLA Ops:
  0.6 195.1 %copy-start = (f32[2,1024]{1,0:T(2,128)S(1)}, f32[2,1024]{1,0:T(2,128)}, u32[]{:S(2)}) copy-start(f32[2,1024]{1,0:T(2,128)} %param.13) | copy-start | bytes 24580
  7.3 64.4 %collective-permute-start = (bf16[1024,1280]{1,0:T(8,128)(2,1)}, bf16[1024,1280]{1,0:T(8,128)(2,1)}, u32[]{:S(2)}, u32[]{:S(2)}) collective-permute-start(bf16[1024,1280]{1,0:T(8,128)(2,1)} %pad_maximum_fusion.1), channel_id=1, source_target_pairs={{0,4},{4,0},{8,12},{12,8},{16,20},{20,16},{24,28},{28,24},{1,5},{5... | collective-permute-start | bytes 7864328 | tf_op jit(solution)/shard_map/ppermute | solution.py:339
  10.6 66.9 %copy-start.18 = (bf16[1024,1280]{1,0:T(8,128)(2,1)}, bf16[1024,1280]{1,0:T(8,128)(2,1)S(1)}, u32[]{:S(2)}) copy-start(bf16[1024,1280]{1,0:T(8,128)(2,1)S(1)} %pad_maximum_fusion.refs_1_.refs_4_) | copy-start | bytes 7864324
  10.6 61.2 %collective-permute-start.1 = (bf16[1024,1280]{1,0:T(8,128)(2,1)S(1)}, bf16[1024,1280]{1,0:T(8,128)(2,1)}, u32[]{:S(2)}, u32[]{:S(2)}) collective-permute-start(bf16[1024,1280]{1,0:T(8,128)(2,1)S(1)} %pad_maximum_fusion.refs_1_.refs_4_), channel_id=1, source_target_pairs={{8,16},{12,20},{16,8},{20,12},{9,17},{13,21},{17,9},{21,13},{10,18... | collective-permute-start | bytes 7864328 | tf_op jit(solution)/shard_map/ppermute | solution.py:339
  22.5 49.2 %collective-permute-start.2 = (bf16[512,2048]{1,0:T(8,128)(2,1)}, bf16[512,2048]{1,0:T(8,128)(2,1)}, u32[]{:S(2)}, u32[]{:S(2)}) collective-permute-start(bf16[512,2048]{1,0:T(8,128)(2,1)} %get-tuple-element.83), channel_id=1, source_target_pairs={{0,8},{4,12},{24,16},{28,20},{1,9},{5,13},{25,17},{29,21},{2,10},{... | collective-permute-start | bytes 6291464 | tf_op jit(solution)/shard_map/ppermute | solution.py:339
  71.7 58.2 %collective-permute-start.5 = (bf16[512,2048]{1,0:T(8,128)(2,1)}, bf16[512,2048]{1,0:T(8,128)(2,1)}, u32[]{:S(2)}, u32[]{:S(2)}) collective-permute-start(bf16[512,2048]{1,0:T(8,128)(2,1)} %collective-permute-done.2.refs_0_.refs_4_), channel_id=1, source_target_pairs={{8,12},{12,8},{16,20},{20,16},{9,13},{13,9},{17,21},{21,17},{10,14... | collective-permute-start | bytes 6291464 | tf_op jit(solution)/shard_map/ppermute | solution.py:339
  73.7 56.2 %collective-permute-start.6 = (bf16[512,2048]{1,0:T(8,128)(2,1)}, bf16[512,2048]{1,0:T(8,128)(2,1)}, u32[]{:S(2)}, u32[]{:S(2)}) collective-permute-start(bf16[512,2048]{1,0:T(8,128)(2,1)} %collective-permute-done.2.refs_0_.refs_4_), channel_id=1, source_target_pairs={{0,2},{1,3},{2,0},{3,1},{4,6},{5,7},{6,4},{7,5},{8,10},{9,11},{10,... | collective-permute-start | bytes 6291464 | tf_op jit(solution)/shard_map/ppermute | solution.py:348
  75.2 54.7 %collective-permute-start.7 = (bf16[512,2048]{1,0:T(8,128)(2,1)}, bf16[512,2048]{1,0:T(8,128)(2,1)}, u32[]{:S(2)}, u32[]{:S(2)}) collective-permute-start(bf16[512,2048]{1,0:T(8,128)(2,1)} %collective-permute-done.2.refs_0_.refs_4_), channel_id=1, source_target_pairs={{0,1},{1,0},{2,3},{3,2},{4,5},{5,4},{6,7},{7,6},{8,9},{9,8},{10,11... | collective-permute-start | bytes 6291464 | tf_op jit(solution)/shard_map/ppermute | solution.py:351
  75.2 54.7 %collective-permute-start.3 = (bf16[1024,1280]{1,0:T(8,128)(2,1)}, bf16[1024,1280]{1,0:T(8,128)(2,1)}, u32[]{:S(2)}, u32[]{:S(2)}) collective-permute-start(bf16[1024,1280]{1,0:T(8,128)(2,1)} %collective-permute-done.refs_2_.refs_5_), channel_id=1, source_target_pairs={{8,16},{12,20},{16,8},{20,12},{9,17},{13,21},{17,9},{21,13},{10,18... | collective-permute-start | bytes 7864328 | tf_op jit(solution)/shard_map/ppermute | solution.py:339
  79.6 50.3 %collective-permute-start.4 = (bf16[2,1024,512]{2,1,0:T(8,128)(2,1)S(1)}, bf16[2,1024,512]{2,1,0:T(8,128)(2,1)}, u32[]{:S(2)}, u32[]{:S(2)}) collective-permute-start(bf16[2,1024,512]{2,1,0:T(8,128)(2,1)S(1)} %pad_maximum_fusion.3), channel_id=1, source_target_pairs={{0,8},{4,12},{24,16},{28,20},{1,9},{5,13},{25,17},{29,21},{2,10},{... | collective-permute-start | bytes 6291464 | tf_op jit(solution)/shard_map/ppermute | solution.py:339
  130.0 17.8 %collective-permute-start.13 = (bf16[512,2048]{1,0:T(8,128)(2,1)}, bf16[512,2048]{1,0:T(8,128)(2,1)}, u32[]{:S(2)}, u32[]{:S(2)}) collective-permute-start(bf16[512,2048]{1,0:T(8,128)(2,1)} %collective-permute-done.6.refs_2_.refs_6_), channel_id=1, source_target_pairs={{0,1},{1,0},{2,3},{3,2},{4,5},{5,4},{6,7},{7,6},{8,9},{9,8},{10,11... | collective-permute-start | bytes 6291464 | tf_op jit(solution)/shard_map/ppermute | solution.py:351
  130.0 57.4 %collective-permute-start.8 = (bf16[2,1024,512]{2,1,0:T(8,128)(2,1)}, bf16[2,1024,512]{2,1,0:T(8,128)(2,1)}, u32[]{:S(2)}, u32[]{:S(2)}) collective-permute-start(bf16[2,1024,512]{2,1,0:T(8,128)(2,1)} %pad_maximum_fusion.2), channel_id=1, source_target_pairs={{0,8},{4,12},{24,16},{28,20},{1,9},{5,13},{25,17},{29,21},{2,10},{... | collective-permute-start | bytes 6291464 | tf_op jit(solution)/shard_map/ppermute | solution.py:339
  142.9 44.5 %collective-permute-start.9 = (bf16[2,1024,512]{2,1,0:T(8,128)(2,1)}, bf16[2,1024,512]{2,1,0:T(8,128)(2,1)}, u32[]{:S(2)}, u32[]{:S(2)}) collective-permute-start(bf16[2,1024,512]{2,1,0:T(8,128)(2,1)} %collective-permute-done.4.refs_10_.refs_11_.refs_5_.refs_6_), channel_id=1, source_target_pairs={{8,16},{12,20},{16,8},{20,12},{9,17},{13,21},{17,9},{21,13},{10,18... | collective-permute-start | bytes 6291464 | tf_op jit(solution)/shard_map/ppermute | solution.py:339
  144.9 42.5 %collective-permute-start.11 = (bf16[512,2048]{1,0:T(8,128)(2,1)}, bf16[512,2048]{1,0:T(8,128)(2,1)}, u32[]{:S(2)}, u32[]{:S(2)}) collective-permute-start(bf16[512,2048]{1,0:T(8,128)(2,1)} %get-tuple-element.83), channel_id=1, source_target_pairs={{8,12},{12,8},{16,20},{20,16},{9,13},{13,9},{17,21},{21,17},{10,14... | collective-permute-start | bytes 6291464 | tf_op jit(solution)/shard_map/ppermute | solution.py:339
  146.9 48.1 %collective-permute-start.12 = (bf16[512,2048]{1,0:T(8,128)(2,1)}, bf16[512,2048]{1,0:T(8,128)(2,1)}, u32[]{:S(2)}, u32[]{:S(2)}) collective-permute-start(bf16[512,2048]{1,0:T(8,128)(2,1)} %collective-permute-done.5.refs_0_.refs_4_), channel_id=1, source_target_pairs={{0,2},{1,3},{2,0},{3,1},{4,6},{5,7},{6,4},{7,5},{8,10},{9,11},{10,... | collective-permute-start | bytes 6291464 | tf_op jit(solution)/shard_map/ppermute | solution.py:348
  195.0 7.2 %collective-permute-start.16 = (bf16[512,2048]{1,0:T(8,128)(2,1)}, bf16[512,2048]{1,0:T(8,128)(2,1)}, u32[]{:S(2)}, u32[]{:S(2)}) collective-permute-start(bf16[512,2048]{1,0:T(8,128)(2,1)} %collective-permute-done.5.refs_0_.refs_4_), channel_id=1, source_target_pairs={{0,1},{1,0},{2,3},{3,2},{4,5},{5,4},{6,7},{7,6},{8,9},{9,8},{10,11... | collective-permute-start | bytes 6291464 | tf_op jit(solution)/shard_map/ppermute | solution.py:351
  195.0 7.5 %collective-permute-start.17 = (bf16[512,2048]{1,0:T(8,128)(2,1)}, bf16[512,2048]{1,0:T(8,128)(2,1)}, u32[]{:S(2)}, u32[]{:S(2)}) collective-permute-start(bf16[512,2048]{1,0:T(8,128)(2,1)} %collective-permute-done.12.refs_2_.refs_6_), channel_id=1, source_target_pairs={{0,1},{1,0},{2,3},{3,2},{4,5},{5,4},{6,7},{7,6},{8,9},{9,8},{10,11... | collective-permute-start | bytes 6291464 | tf_op jit(solution)/shard_map/ppermute | solution.py:351
  196.0 54.0 %collective-permute-start.10 = (bf16[2,1024,512]{2,1,0:T(8,128)(2,1)}, bf16[2,1024,512]{2,1,0:T(8,128)(2,1)}, u32[]{:S(2)}, u32[]{:S(2)}) collective-permute-start(bf16[2,1024,512]{2,1,0:T(8,128)(2,1)} %collective-permute-done.8.refs_10_.refs_11_.refs_5_.refs_6_), channel_id=1, source_target_pairs={{8,16},{12,20},{16,8},{20,12},{9,17},{13,21},{17,9},{21,13},{10,18... | collective-permute-start | bytes 6291464 | tf_op jit(solution)/shard_map/ppermute | solution.py:339
  198.0 51.1 %collective-permute-start.14 = (bf16[2,1024,256]{2,1,0:T(8,128)(2,1)}, bf16[2,1024,256]{2,1,0:T(8,128)(2,1)S(1)}, u32[]{:S(2)}, u32[]{:S(2)}) collective-permute-start(bf16[2,1024,256]{2,1,0:T(8,128)(2,1)} %pad_maximum_fusion.4), channel_id=1, source_target_pairs={{0,8},{4,12},{24,16},{28,20},{1,9},{5,13},{25,17},{29,21},{2,10},{... | collective-permute-start | bytes 3145736 | tf_op jit(solution)/shard_map/ppermute | solution.py:339
  201.6 48.5 %collective-permute-start.15 = (bf16[512,2048]{1,0:T(8,128)(2,1)}, bf16[512,2048]{1,0:T(8,128)(2,1)}, u32[]{:S(2)}, u32[]{:S(2)}) collective-permute-start(bf16[512,2048]{1,0:T(8,128)(2,1)} %collective-permute-done.11.refs_0_.refs_8_), channel_id=1, source_target_pairs={{0,2},{1,3},{2,0},{3,1},{4,6},{5,7},{6,4},{7,5},{8,10},{9,11},{10,... | collective-permute-start | bytes 6291464 | tf_op jit(solution)/shard_map/ppermute | solution.py:348
  250.0 33.1 %collective-permute-start.20 = (bf16[512,2048]{1,0:T(8,128)(2,1)}, bf16[512,2048]{1,0:T(8,128)(2,1)}, u32[]{:S(2)}, u32[]{:S(2)}) collective-permute-start(bf16[512,2048]{1,0:T(8,128)(2,1)} %collective-permute-done.11.refs_0_.refs_8_), channel_id=1, source_target_pairs={{0,1},{1,0},{2,3},{3,2},{4,5},{5,4},{6,7},{7,6},{8,9},{9,8},{10,11... | collective-permute-start | bytes 6291464 | tf_op jit(solution)/shard_map/ppermute | solution.py:351
  250.2 34.2 %collective-permute-start.21 = (bf16[512,2048]{1,0:T(8,128)(2,1)}, bf16[512,2048]{1,0:T(8,128)(2,1)}, u32[]{:S(2)}, u32[]{:S(2)}) collective-permute-start(bf16[512,2048]{1,0:T(8,128)(2,1)} %collective-permute-done.15.refs_2_.refs_10_), channel_id=1, source_target_pairs={{0,1},{1,0},{2,3},{3,2},{4,5},{5,4},{6,7},{7,6},{8,9},{9,8},{10,11... | collective-permute-start | bytes 6291464 | tf_op jit(solution)/shard_map/ppermute | solution.py:351
  257.1 25.2 %collective-permute-start.18 = (bf16[512,512]{1,0:T(8,128)(2,1)S(1)}, bf16[512,512]{1,0:T(8,128)(2,1)S(1)}, u32[]{:S(2)}, u32[]{:S(2)}) collective-permute-start(bf16[512,512]{1,0:T(8,128)(2,1)S(1)} %pad_maximum_fusion.6), channel_id=1, source_target_pairs={{8,0},{12,4},{16,24},{20,28},{9,1},{13,5},{17,25},{21,29},{10,2},{... | collective-permute-start | bytes 1572872 | tf_op jit(solution)/shard_map/ppermute | solution.py:339
  261.5 78.8 %collective-permute-start.25 = (bf16[512,512]{1,0:T(8,128)(2,1)}, bf16[512,512]{1,0:T(8,128)(2,1)S(1)}, u32[]{:S(2)}, u32[]{:S(2)}) collective-permute-start(bf16[512,512]{1,0:T(8,128)(2,1)} %pad_maximum_fusion.8), channel_id=1, source_target_pairs={{8,4},{12,0},{16,28},{20,24},{9,5},{13,1},{17,29},{21,25},{10,6},{... | collective-permute-start | bytes 1572872 | tf_op jit(solution)/shard_map/ppermute | solution.py:339
  276.3 66.9 %collective-permute-start.27 = (bf16[512,512]{1,0:T(8,128)(2,1)S(1)}, bf16[512,512]{1,0:T(8,128)(2,1)S(1)}, u32[]{:S(2)}, u32[]{:S(2)}) collective-permute-start(bf16[512,512]{1,0:T(8,128)(2,1)S(1)} %shard_map.110), channel_id=1, source_target_pairs={{8,4},{12,0},{16,28},{20,24},{9,5},{13,1},{17,29},{21,25},{10,6},{... | collective-permute-start | bytes 1572872 | tf_op jit(solution)/shard_map/ppermute | solution.py:339
  282.3 34.1 %collective-permute-start.19 = (bf16[2,1024,256]{2,1,0:T(8,128)(2,1)S(1)}, bf16[2,1024,256]{2,1,0:T(8,128)(2,1)S(1)}, u32[]{:S(2)}, u32[]{:S(2)}) collective-permute-start(bf16[2,1024,256]{2,1,0:T(8,128)(2,1)S(1)} %copy-done.20), channel_id=1, source_target_pairs={{8,16},{12,20},{16,8},{20,12},{9,17},{13,21},{17,9},{21,13},{10,18... | collective-permute-start | bytes 3145736 | tf_op jit(solution)/shard_map/ppermute | solution.py:339
  283.1 77.9 %collective-permute-start.22 = (bf16[512,512]{1,0:T(8,128)(2,1)S(1)}, bf16[512,512]{1,0:T(8,128)(2,1)S(1)}, u32[]{:S(2)}, u32[]{:S(2)}) collective-permute-start(bf16[512,512]{1,0:T(8,128)(2,1)S(1)} %shard_map.109), channel_id=1, source_target_pairs={{8,0},{12,4},{16,24},{20,28},{9,1},{13,5},{17,25},{21,29},{10,2},{... | collective-permute-start | bytes 1572872 | tf_op jit(solution)/shard_map/ppermute | solution.py:339
  305.0 36.0 %collective-permute-start.24 = (bf16[512,512]{1,0:T(8,128)(2,1)}, bf16[512,512]{1,0:T(8,128)(2,1)}, u32[]{:S(2)}, u32[]{:S(2)}) collective-permute-start(bf16[512,512]{1,0:T(8,128)(2,1)} %pad_maximum_fusion.7), channel_id=1, source_target_pairs={{8,12},{12,8},{16,20},{20,16},{9,13},{13,9},{17,21},{21,17},{10,14... | collective-permute-start | bytes 1572872 | tf_op jit(solution)/shard_map/ppermute | solution.py:339
  316.4 28.1 %collective-permute-start.26 = (bf16[512,512]{1,0:T(8,128)(2,1)S(1)}, bf16[512,512]{1,0:T(8,128)(2,1)S(1)}, u32[]{:S(2)}, u32[]{:S(2)}) collective-permute-start(bf16[512,512]{1,0:T(8,128)(2,1)S(1)} %shard_map.108), channel_id=1, source_target_pairs={{8,12},{12,8},{16,20},{20,16},{9,13},{13,9},{17,21},{21,17},{10,14... | collective-permute-start | bytes 1572872 | tf_op jit(solution)/shard_map/ppermute | solution.py:339
  340.3 4.3 %collective-permute-start.28 = (bf16[512,256]{1,0:T(8,128)(2,1)S(1)}, bf16[512,256]{1,0:T(8,128)(2,1)S(1)}, u32[]{:S(2)}, u32[]{:S(2)}) collective-permute-start(bf16[512,256]{1,0:T(8,128)(2,1)S(1)} %shard_map.116), channel_id=1, source_target_pairs={{8,12},{12,8},{16,20},{20,16},{9,13},{13,9},{17,21},{21,17},{10,14... | collective-permute-start | bytes 786440 | tf_op jit(solution)/shard_map/ppermute | solution.py:339
  341.0 19.8 %collective-permute-start.29 = (bf16[512,256]{1,0:T(8,128)(2,1)S(1)}, bf16[512,256]{1,0:T(8,128)(2,1)S(1)}, u32[]{:S(2)}, u32[]{:S(2)}) collective-permute-start(bf16[512,256]{1,0:T(8,128)(2,1)S(1)} %shard_map.117), channel_id=1, source_target_pairs={{8,4},{12,0},{16,28},{20,24},{9,5},{13,1},{17,29},{21,25},{10,6},{... | collective-permute-start | bytes 786440 | tf_op jit(solution)/shard_map/ppermute | solution.py:339
  343.2 20.4 %collective-permute-start.23 = (bf16[512,256]{1,0:T(8,128)(2,1)S(1)}, bf16[512,256]{1,0:T(8,128)(2,1)S(1)}, u32[]{:S(2)}, u32[]{:S(2)}) collective-permute-start(bf16[512,256]{1,0:T(8,128)(2,1)S(1)} %shard_map.113), channel_id=1, source_target_pairs={{8,0},{12,4},{16,24},{20,28},{9,1},{13,5},{17,25},{21,29},{10,2},{... | collective-permute-start | bytes 786440 | tf_op jit(solution)/shard_map/ppermute | solution.py:339
  (43 other events, 449.9 us)

commit v5 on v0

--- a/solution.py
+++ b/solution.py
@@ -1,8 +1,11 @@
+import functools
 import math
 
 import jax
 import jax.numpy as jnp
 from jax import lax
+from jax.experimental import pallas as pl
+from jax.experimental.pallas import tpu as pltpu
 from jax.sharding import PartitionSpec as P
 
 HD = 128
@@ -10,6 +13,8 @@
 
 EPS = 1e-06
 THETA = 1000000.0
+QROWS = 128
+MAXLEN = 256
 
 
 def token_layout(prefix_lens, assignment, group_id, tok_rows):
@@ -49,7 +54,16 @@
     return jnp.dot(normed, portion, preferred_element_type=jnp.float32)
 
 
-def on_device(hidden, norm_gain, q_weight, q_bias, kv_weight, kv_bias, prefix_lens, assignment):
+def normalise(hidden, norm_gain):
+    widened = hidden.astype(jnp.float32)
+    return (
+        widened * lax.rsqrt(jnp.mean(widened * widened, axis=-1, keepdims=True) + EPS) * norm_gain
+    ).astype(jnp.bfloat16)
+
+
+def gathered_form(
+    hidden, norm_gain, q_weight, q_bias, kv_weight, kv_bias, prefix_lens, assignment
+):
     tok_rows, features = hidden.shape
     slice_rows = kv_weight.shape[0]
     q_cols = q_weight.shape[1]
@@ -57,10 +71,7 @@
     heads_here = q_cols // HD
     tensor_pos = lax.axis_index("tensor")
     kv_cols = kv_total // lax.axis_size("tensor")
-    widened = hidden.astype(jnp.float32)
-    normed = (
-        widened * lax.rsqrt(jnp.mean(widened * widened, axis=-1, keepdims=True) + EPS) * norm_gain
-    ).astype(jnp.bfloat16)
+    normed = normalise(hidden, norm_gain)
     queries = add_product(normed, lax.all_gather(q_weight, "group", axis=0, tiled=True)) + q_bias
     head_span = max(kv_cols, HD)
     head_base = tensor_pos * kv_cols // head_span * head_span
@@ -103,6 +114,504 @@
     return (context, kv_cache)
 
 
+def norm_kernel(part_ref, hidden_ref, gain_ref, out_ref, part_out_ref):
+    widened = hidden_ref[...].astype(jnp.float32)
+    scale = lax.rsqrt(jnp.mean(widened * widened, axis=-1, keepdims=True) + EPS)
+    normed = (widened * scale * gain_ref[...]).astype(jnp.bfloat16)
+    depth = out_ref.shape[2]
+    for block in range(out_ref.shape[0]):
+        out_ref[block] = normed[:, block * depth : (block + 1) * depth]
+    count = part_out_ref.shape[0]
+    part_out_ref[...] = out_ref[pl.ds(part_ref[0] * count, count)]
+
+
+def norm(hidden, norm_gain, part, depth, count):
+    rows, features = hidden.shape
+    blocks = features // depth
+    step = 64
+    return pl.pallas_call(
+        norm_kernel,
+        grid_spec=pltpu.PrefetchScalarGridSpec(
+            num_scalar_prefetch=1,
+            grid=(rows // step,),
+            in_specs=[
+                pl.BlockSpec((step, features), lambda i, part: (i, 0)),
+                pl.BlockSpec((1, features), lambda i, part: (0, 0)),
+            ],
+            out_specs=[
+                pl.BlockSpec((blocks, step, depth), lambda i, part: (0, i, 0)),
+                pl.BlockSpec((count, step, depth), lambda i, part: (0, i, 0)),
+            ],
+        ),
+        out_shape=[
+            jax.ShapeDtypeStruct((blocks, rows, depth), jnp.bfloat16),
+            jax.ShapeDtypeStruct((count, rows, depth), jnp.bfloat16),
+        ],
+        compiler_params=pltpu.CompilerParams(vmem_limit_bytes=32 * 2**20),
+        cost_estimate=pl.CostEstimate(
+            flops=4 * rows * features, bytes_accessed=5 * rows * features, transcendentals=rows
+        ),
+    )(part[None], hidden, norm_gain[None])
+
+
+TILE = 2 * HD
+
+
+def turn(value, cosine, sine):
+    return (value * cosine + pltpu.roll(value, HD // 2, 1) * sine).astype(jnp.bfloat16)
+
+
+def attention(queries, keys, values, first_ref, out_ref, skip):
+    heads = len(queries)
+    rows = out_ref.shape[0]
+    for block in range(rows // QROWS):
+        top = block * QROWS
+        low = max(0, top - MAXLEN)
+        end = top + QROWS
+        span = end - low
+        stacked = jnp.concatenate([query[top:end] for query in queries], axis=0)
+        scores = lax.dot_general(
+            stacked, keys[low:end], (((1,), (1,)), ((), ())), preferred_element_type=jnp.float32
+        ) * (1.0 / math.sqrt(HD))
+        row = lax.broadcasted_iota(jnp.int32, (QROWS, span), 0) + top
+        col = lax.broadcasted_iota(jnp.int32, (QROWS, span), 1) + low
+        visible = (col <= row) & (col >= first_ref[top:end])
+        scores = jnp.where(visible[None], scores.reshape(heads, QROWS, span), -jnp.inf)
+        exponent = jnp.exp(scores - jnp.max(scores, axis=-1, keepdims=True))
+        weights = (exponent / jnp.sum(exponent, axis=-1, keepdims=True)).astype(jnp.bfloat16)
+        context = jnp.dot(
+            weights.reshape(heads * QROWS, span), values[low:end], preferred_element_type=jnp.float32
+        ).astype(jnp.bfloat16)
+        for head in range(heads):
+            out_ref[top:end, skip + head * HD : skip + (head + 1) * HD] = context[
+                head * QROWS : (head + 1) * QROWS
+            ]
+
+
+def heads_kernel(plan, pick_ref, *refs):
+    sources, places, tiles, with_totals, finish, with_keys = plan
+    sets, count = len(sources), len(places)
+    refs = list(refs)
+
+    def take(number):
+        taken = refs[:number]
+        del refs[:number]
+        return taken
+
+    row_refs = [take(number) for number in sources]
+    weight_refs = take(count)
+    totals = take(sets) if with_totals else [None] * sets
+    if finish:
+        (bias_ref,) = take(1)
+        tables = [take(3) for _ in range(sets)]
+        caches = [None] * sets if with_keys else take(sets)
+    outs = take(sets)
+    row_buf, weight_buf, *rest = refs
+    acc = rest.pop(0) if finish else None
+    row_sem, weight_sem = rest
+
+    def weight_copy(piece):
+        return pltpu.make_async_copy(
+            weight_refs[piece].at[pl.ds(places[piece], tiles)],
+            weight_buf.at[piece],
+            weight_sem.at[piece],
+        )
+
+    def row_copy(which, piece, source):
+        return pltpu.make_async_copy(
+            row_refs[which][source].at[pick_ref[which, 1, piece]],
+            row_buf.at[which, piece],
+            row_sem.at[which, piece],
+        )
+
+    for piece in range(count):
+        weight_copy(piece).start()
+        for which in range(sets):
+            if sources[which] == 1:
+                row_copy(which, piece, 0).start()
+            else:
+                for source in range(sources[which]):
+
+                    @pl.when(pick_ref[which, 0, piece] == source)
+                    def _():
+                        row_copy(which, piece, source).start()
+
+    done = 0
+    while done < count:
+        ready = min(count, done + (1 if done < 2 else 2))
+        for piece in range(done, ready):
+            weight_copy(piece).wait()
+        for which in range(sets):
+            for piece in range(done, ready):
+                row_copy(which, piece, 0).wait()
+            total_ref = acc.at[which] if finish else outs[which]
+            for tile in range(tiles):
+                cols = slice(tile * TILE, (tile + 1) * TILE)
+                term = None
+                if done > 0:
+                    term = total_ref[:, cols]
+                elif totals[which] is not None:
+                    term = totals[which][:, cols]
+                for piece in range(done, ready):
+                    product = jnp.dot(
+                        row_buf[which, piece],
+                        weight_buf[piece, tile],
+                        preferred_element_type=jnp.float32,
+                    )
+                    term = product if term is None else term + product
+                total_ref[:, cols] = term
+        done = ready
+    if not finish:
+        return
+
+    for which in range(sets):
+        cos_ref, sin_ref, first_ref = tables[which]
+        cosine, sine = cos_ref[...], sin_ref[...]
+        out_ref = outs[which]
+        skip = TILE if with_keys else 0
+        if with_keys:
+            out_ref[:, :HD] = turn(acc[which, :, :HD] + bias_ref[:, :HD], cosine, sine)
+            out_ref[:, HD:TILE] = (acc[which, :, HD:TILE] + bias_ref[:, HD:TILE]).astype(jnp.bfloat16)
+        cache = out_ref if with_keys else caches[which]
+        queries = []
+        for col in range(skip, out_ref.shape[1], HD):
+            cols = slice(col, col + HD)
+            queries.append(turn(acc[which, :, cols] + bias_ref[:, cols], cosine, sine))
+        attention(queries, cache.at[:, :HD], cache.at[:, HD:TILE], first_ref, out_ref, skip)
+
+
+def heads_of(row_sets, picks, pieces, tiles, totals=None, finish=None):
+    sets, count = len(row_sets), len(pieces)
+    sources = tuple(len(rows) for rows in row_sets)
+    tokens, depth = row_sets[0][0].shape[1:]
+    width = tiles * TILE
+    operands = [array for rows in row_sets for array in rows] + [array for array, _ in pieces]
+    in_specs = [pl.BlockSpec(memory_space=pl.ANY)] * len(operands)
+
+    def block(shape, column=0):
+        return pl.BlockSpec(shape, functools.partial(lambda at, i, pick: (0, at), column))
+
+    if totals is not None:
+        for total, column in totals:
+            in_specs.append(block((tokens, width), column))
+            operands.append(total)
+    with_keys = False
+    scratch = [
+        pltpu.VMEM((sets, count, tokens, depth), jnp.bfloat16),
+        pltpu.VMEM((count, tiles, depth, TILE), jnp.bfloat16),
+    ]
+    kind = jnp.float32
+    if finish is not None:
+        bias, tables, caches = finish
+        kind = jnp.bfloat16
+        in_specs.append(block((1, width)))
+        operands.append(bias)
+        for table in tables:
+            for array in table:
+                in_specs.append(block(array.shape))
+                operands.append(array)
+        with_keys = caches is None
+        if not with_keys:
+            for cache in caches:
+                in_specs.append(block((tokens, TILE)))
+                operands.append(cache)
+        scratch.append(pltpu.VMEM((sets, tokens, width), jnp.float32))
+    scratch += [pltpu.SemaphoreType.DMA((sets, count)), pltpu.SemaphoreType.DMA((count,))]
+    plan = (
+        sources,
+        tuple(place for _, place in pieces),
+        tiles,
+        totals is not None,
+        finish is not None,
+        with_keys,
+    )
+    return pl.pallas_call(
+        functools.partial(heads_kernel, plan),
+        grid_spec=pltpu.PrefetchScalarGridSpec(
+            num_scalar_prefetch=1,
+            grid=(1,),
+            in_specs=in_specs,
+            out_specs=[block((tokens, width))] * sets,
+            scratch_shapes=scratch,
+        ),
+        out_shape=[jax.ShapeDtypeStruct((tokens, width), kind)] * sets,
+        compiler_params=pltpu.CompilerParams(vmem_limit_bytes=56 * 2**20),
+        cost_estimate=pl.CostEstimate(
+            flops=2 * sets * count * tokens * depth * width,
+            bytes_accessed=2 * count * depth * (sets * tokens + width) + 8 * sets * tokens * width,
+            transcendentals=0,
+        ),
+    )(jnp.stack(picks), *operands)
+
+
+def gather_kernel(parts, flag_ref, *refs):
+    near, beside, back, other = (refs[i * parts : (i + 1) * parts] for i in range(4))
+    out_ref, sem = refs[-2:]
+    half = out_ref.shape[1] // 2
+    y, middle = flag_ref[0], flag_ref[1]
+
+    def copies(sources, side, start):
+        place = 0
+        for part, source in enumerate(sources):
+            skip = TILE if part == 0 else 0
+            width = source.shape[1] - skip
+            at = pl.multiple_of(side * half + place, TILE)
+            copy = pltpu.make_async_copy(
+                source.at[:, skip : skip + width],
+                out_ref.at[:, pl.ds(at, width)],
+                sem.at[start + part],
+            )
+            copy.start()
+            place += width
+
+    def waits(sources, start):
+        for part, source in enumerate(sources):
+            skip = TILE if part == 0 else 0
+            width = source.shape[1] - skip
+            pltpu.make_async_copy(
+                source.at[:, skip : skip + width], out_ref.at[:, :width], sem.at[start + part]
+            ).wait()
+
+    @pl.when(middle == 1)
+    def _():
+        copies(near, y, 0)
+        copies(beside, 1 - y, parts)
+
+    @pl.when(middle == 0)
+    def _():
+        copies(back, y, 0)
+        copies(other, 1 - y, parts)
+
+    waits(near, 0)
+    waits(beside, parts)
+
+
+def gather_context(flags, near, beside, back, other, rows, cols):
+    parts = len(near)
+    operands = [*near, *beside, *back, *other]
+    return pl.pallas_call(
+        functools.partial(gather_kernel, parts),
+        grid_spec=pltpu.PrefetchScalarGridSpec(
+            num_scalar_prefetch=1,
+            grid=(1,),
+            in_specs=[pl.BlockSpec(memory_space=pl.ANY)] * len(operands),
+            out_specs=pl.BlockSpec(memory_space=pl.ANY),
+            scratch_shapes=[pltpu.SemaphoreType.DMA((2 * parts,))],
+        ),
+        out_shape=jax.ShapeDtypeStruct((rows, cols), jnp.bfloat16),
+        cost_estimate=pl.CostEstimate(flops=0, bytes_accessed=4 * rows * cols, transcendentals=0),
+    )(flags, *operands)
+
+
+MIDDLE = (2, 3, 4, 5)
+ENDS = (0, 1, 6, 7)
+
+
+def after(value, *others):
+    return lax.optimization_barrier((value,) + others)[0]
+
+
+def pairs_from(sources, code):
+    return [(s, s ^ code) for s in sources]
+
+
+def middle_form(hidden, norm_gain, q_weight, q_bias, kv_weight, kv_bias, prefix_lens, assignment):
+    tok_rows, features = hidden.shape
+    slice_rows, q_cols = q_weight.shape
+    half_cols = q_cols // 2
+    group = lax.axis_index("group")
+    tensor = lax.axis_index("tensor")
+    y = group & 1
+    is_middle = (group >= 2) & (group < 6)
+    barrier = lax.optimization_barrier
+
+    def over_group(value, sources, code):
+        return lax.ppermute(value, "group", pairs_from(sources, code))
+
+    def to_middle(value):
+        return over_group(value, ENDS, 2)
+
+    def across_middle(value):
+        return over_group(value, MIDDLE, 6)
+
+    def over_x(value):
+        return lax.ppermute(value, "tensor", pairs_from(range(4), 2))
+
+    def over_core(value):
+        return lax.ppermute(value, "tensor", pairs_from(range(4), 1))
+
+    tiles = (2, 2, 1)
+    begin = (0, 2, 4)
+
+    def columns(half):
+        head = (2 * tensor + half) * HD
+        kv_part = lax.dynamic_slice_in_dim(kv_weight, head, HD, 2).reshape(slice_rows, TILE)
+        return jnp.stack(
+            [kv_part]
+            + [
+                lax.dynamic_slice_in_dim(q_weight, half * half_cols + at, TILE, 1)
+                for at in range(0, half_cols, TILE)
+            ]
+        )
+
+    def both(one, two, chunk):
+        low, high = begin[chunk], begin[chunk] + tiles[chunk]
+        return jnp.concatenate([one[low:high], two[low:high]])
+
+    def pick(code_of_rows, codes):
+        block = jnp.stack([group ^ code for code in codes])
+        if code_of_rows == 0:
+            return jnp.stack([block * 0, block])
+        return jnp.stack([(block >> 1) ^ tensor, block & 1])
+
+    def rows_and_picks(sets, codes):
+        return [rows_of[c] for c in sets], [pick(c, codes) for c in sets]
+
+    own = columns(y)
+    other = columns(1 - y)
+    m_own = across_middle(own)
+    swap = over_group(other, range(8), 1)
+    normed, quarter = norm(hidden, norm_gain, tensor, slice_rows, 2)
+    end2 = to_middle(quarter)
+
+    bias = lax.dynamic_slice_in_dim(q_bias, y * half_cols, half_cols, 0)
+    kv_bias_here = lax.dynamic_slice_in_dim(kv_bias, (2 * tensor + y) * HD, HD, 1)
+    bias = jnp.concatenate([kv_bias_here[0], kv_bias_here[1], bias])[None, :]
+    inverse_freq = THETA ** (-2.0 * jnp.arange(HD // 2, dtype=jnp.float32) / HD)
+    m_swap = across_middle(after(swap, m_own))
+    own, swap, m_own, normed, quarter, end2 = barrier((own, swap, m_own, normed, quarter, end2))
+
+    rows_of = {0: [normed]}
+    e0 = to_middle(both(own, swap, 0))
+    next1, next2 = both(own, swap, 1), both(own, swap, 2)
+    end3 = over_group(end2, MIDDLE, 1)
+    across2 = over_x(end2)
+    twin2 = over_core(end2)
+    tables = []
+    for code in range(4):
+        _, offset, places = token_layout(prefix_lens, assignment, group ^ code, tok_rows)
+        angles = offset.astype(jnp.float32)[:, None] * inverse_freq[None, :]
+        cosine, sine = jnp.cos(angles), jnp.sin(angles)
+        cosine = jnp.concatenate([cosine, cosine], axis=1)
+        sine = jnp.concatenate([-sine, sine], axis=1)
+        tables.append((cosine, sine, (places - offset)[:, None]))
+    m_e0 = across_middle(after(e0, m_swap))
+    (next1, next2, m_swap, e0, end2, end3, across2, twin2, tables, quarter) = barrier(
+        (next1, next2, m_swap, e0, end2, end3, across2, twin2, tables, quarter)
+    )
+
+    first_codes, last_codes = (0, 1, 6, 7), (2, 3, 4, 5)
+    first_pieces = {0: own, 1: swap, 6: m_own, 7: m_swap}
+
+    def first_sums(sets):
+        rows, picks = rows_and_picks(sets, first_codes)
+        return heads_of(rows, picks, [(first_pieces[c], begin[1]) for c in first_codes], 3)
+
+    outs = {}
+
+    def finished(sets, chunk, last_pieces, totals=None):
+        codes = last_codes if totals is not None else first_codes + last_codes
+        rows, picks = rows_and_picks(sets, codes)
+        width = tiles[chunk]
+        places = {2: 0, 3: width, 4: 0, 5: width}
+        pieces = [
+            (first_pieces[c], begin[chunk]) if c in first_codes else (last_pieces[c], places[c])
+            for c in codes
+        ]
+        if totals is not None:
+            totals = [(total, (begin[chunk] - begin[1]) // width) for total in totals]
+        made = heads_of(
+            rows,
+            picks,
+            pieces,
+            width,
+            totals,
+            (
+                bias[:, begin[chunk] * TILE : (begin[chunk] + width) * TILE],
+                [tables[c] for c in sets],
+                None if chunk == 0 else [outs[c, 0] for c in sets],
+            ),
+        )
+        for code, out in zip(sets, made):
+            outs[code, chunk] = out
+
+    e1 = to_middle(next1)
+    end1 = over_group(quarter, MIDDLE, 1)
+    across3 = over_x(end3)
+    far2 = over_core(across2)
+    rows_of[2] = [end2, twin2, across2, far2]
+    sums = dict(zip((0, 2), first_sums((0, 2))))
+    m_e1 = across_middle(after(e1, m_e0))
+    (next2, m_e0, e0, e1, end1, end3, across3, far2, sums) = barrier(
+        (next2, m_e0, e0, e1, end1, end3, across3, far2, sums)
+    )
+    rows_of[2] = [end2, twin2, across2, far2]
+
+    e2 = to_middle(next2)
+    across1 = over_x(end1)
+    twin3 = over_core(end3)
+    far3 = over_core(across3)
+    rows_of[3] = [end3, twin3, across3, far3]
+
+    def send_back(code, chunk):
+        return over_group(outs[code, chunk], MIDDLE, code)
+
+    pieces0 = {2: e0, 3: e0, 4: m_e0, 5: m_e0}
+    finished((2, 3, 0), 0, pieces0)
+    back = {(code, 0): send_back(code, 0) for code in (2, 3)}
+    (sums[3],) = first_sums((3,))
+    m_e2 = across_middle(after(e2, m_e1))
+    (m_e1, e2, end1, across1, outs[0, 0], outs[2, 0], outs[3, 0], sums) = barrier(
+        (m_e1, e2, end1, across1, outs[0, 0], outs[2, 0], outs[3, 0], sums)
+    )
+
+    twin1 = over_core(end1)
+    far1 = over_core(across1)
+    rows_of[1] = [end1, twin1, across1, far1]
+    pieces1 = {2: e1, 3: e1, 4: m_e1, 5: m_e1}
+    three = (2, 3, 0)
+    finished(three, 1, pieces1, [sums[c] for c in three])
+    for code in (2, 3):
+        back[code, 1] = send_back(code, 1)
+    finished((1,), 0, pieces0)
+    back[1, 0] = send_back(1, 0)
+    (sums[1],) = first_sums((1,))
+    finished((1,), 1, pieces1, [after(sums[1], m_e2)])
+    back[1, 1] = send_back(1, 1)
+    (m_e2, sums, *ready) = barrier((m_e2, sums, *[outs[c, 1] for c in range(4)]))
+    for code in range(4):
+        outs[code, 1] = ready[code]
+
+    pieces2 = {2: e2, 3: e2, 4: m_e2, 5: m_e2}
+    order = (3, 2, 1, 0)
+    finished(order, 2, pieces2, [sums[c] for c in order])
+    for code in (3, 2, 1):
+        back[code, 2] = send_back(code, 2)
+
+    parts = range(3)
+    context = gather_context(
+        jnp.stack([y, is_middle.astype(jnp.int32)]),
+        [outs[0, part] for part in parts],
+        [back[1, part] for part in parts],
+        [back[2, part] for part in parts],
+        [back[3, part] for part in parts],
+        tok_rows,
+        q_cols,
+    )
+
+    def cache(part):
+        return part[:, :TILE].reshape(tok_rows, 2, HD)
+
+    mine = jnp.where(is_middle, cache(outs[0, 0]), cache(back[2, 0]))
+    its = jnp.where(is_middle, cache(back[1, 0]), cache(back[3, 0]))
+    kv_cache = jnp.where(
+        y == 0,
+        jnp.concatenate([mine, its], axis=-1),
+        jnp.concatenate([its, mine], axis=-1),
+    )
+    return (context, kv_cache)
+
+
 def solution(mesh):
     placed = (
         P("group", None),
@@ -114,8 +623,9 @@
         P(),
         P(),
     )
+    fits = mesh.shape["group"] == 8 and mesh.shape["tensor"] == 4
     return jax.shard_map(
-        on_device,
+        middle_form if fits else gathered_form,
         mesh=mesh,
         in_specs=placed,
         out_specs=(P("group", "tensor"), P("group", None, "tensor")),

time: 846 us -> 445 us (0.53)
  waiting for transfers between devices: 745 us -> 118 us
  Pallas kernels: 0 us -> 202 us
  starting transfers between devices: 0.08 us -> 64.4 us
  matrix products: 50.6 us -> 0 us
  local copies, waits for them, and re-layouts: 9.42 us -> 29.9 us
  between operations: 14.3 us -> 1.8 us
    all_gather x2 -> x0, waiting for transfers between devices: 744 us -> none  [the longest x1 624 us: on_device(): lax.all_gather(q_weight, 'group', axis=0, tiled=True)]
    pallas_call x0 -> x10, Pallas kernels: none -> 202 us  [the longest x8 131 us: heads_of(): pl.pallas_call(functools.partial(heads_kernel, plan), grid_spec=pltpu.Pre...]
    ppermute x0 -> x30, waiting for transfers between devices: none -> 118 us  [the longest x21 99 us: over_group(): return lax.ppermute(value, 'group', pairs_from(sources, code))]
    ppermute x0 -> x30, starting transfers between devices: none -> 64.4 us  [the longest x21 59.7 us: over_group(): return lax.ppermute(value, 'group', pairs_from(sources, code))]
    dot_general x4 -> x0, matrix products: 50.6 us -> none  [the longest x2 35.4 us: add_product(): return jnp.dot(normed, portion, preferred_element_type=jnp.float32)]
    sub x2 -> x0, other arithmetic: 17.4 us -> none  [the longest x1 17.3 us: on_device(): exponent = jnp.exp(scores - row_max)]
    concatenate x0 -> x12, other arithmetic: none -> 9.5 us  [the longest x4 3.39 us: middle_form(): cosine = jnp.concatenate([cosine, cosine], axis=1)]
  transfers between devices with their start and end apart: 2 -> 30, of which waited for: 2 -> 6; matrix products, arithmetic and copies ran while one was open for 2% -> 8% of each run, Pallas kernels for 0% -> 31%
where the time goes in v5:
time: 445 us; the launch traced here: 437 us
  Pallas kernels  202 us (45%)
  waiting for transfers between devices  118 us (27%)
  starting transfers between devices  64.4 us (14%)
  local copies, waits for them, and re-layouts  29.9 us (7%)
  other arithmetic  20.6 us (5%)
    pallas_call x8, Pallas kernels, heads_of(): pl.pallas_call(functools.partial(heads_kernel, plan), grid_spec=pltpu.Pre...  131 us
    ppermute x21, waiting for transfers between devices, over_group(): return lax.ppermute(value, 'group', pairs_from(sources, code))  99 us
    pallas_call x1, Pallas kernels, gather_context(): pl.pallas_call(functools.partial(gather_kernel, parts), grid_spec=pltpu.P...  65.4 us
    ppermute x21, starting transfers between devices, over_group(): return lax.ppermute(value, 'group', pairs_from(sources, code))  59.7 us
    ppermute x3, waiting for transfers between devices, over_x(): return lax.ppermute(value, 'tensor', pairs_from(range(4), 2))  18.5 us
    unnamed x46, local copies, waits for them, and re-layouts  12.8 us
  transfers between devices with their start and end apart: 30, of which 6 were waited for; matrix products, arithmetic and copies ran while one was open for 8% of the time, Pallas kernels for 31%

profile of v5, /device:TPU:0, one launch (start us, length us, event | category | flops | bytes accessed | tf_op | source)
XLA Modules:
  0.0 436.6 jit_solution(3176985265521525867)
XLA Ops:
  4.3 2.4 bitcast_dynamic-update-slice_fusion.3
  6.7 2.9 bitcast_dynamic-update-slice_fusion.2
  9.7 2.3 bitcast_dynamic-update-slice_fusion.1
  11.9 2.3 bitcast_dynamic-update-slice_fusion
  14.2 3.0 collective-permute-start
  17.2 2.2 collective-permute-start.1
  19.4 6.1 %shard_map.95 = (bf16[8,512,1024]{2,1,0:T(8,128)(2,1)S(1)}, bf16[2,512,1024]{2,1,0:T(8,128)(2,1)S(1)}) custom-call(s32[1]{0:T(128)} %bitcast.10.part_ref, bf16[512,8192]{1,0:T(8,128)(2,1)S(1)} %copy-done.3, f32[1,8192]{1,0:T(1,128)S(1)} %bitcast.69), custom_call_target="tpu_custom_call" | custom-call | flops 16777216 | bytes 20971520 | tf_op jit(solution)/shard_map/pallas_call | solution.py:132
  25.5 3.3 copy-done.2
  28.8 6.1 %collective-permute-start.2 = (bf16[2,512,1024]{2,1,0:T(8,128)(2,1)S(1)}, bf16[2,512,1024]{2,1,0:T(8,128)(2,1)}, u32[]{:S(2)}, u32[]{:S(2)}) collective-permute-start(bf16[2,512,1024]{2,1,0:T(8,128)(2,1)S(1)} %get-tuple-element.86), channel_id=1, source_target_pairs={{0,8},{4,12},{24,16},{28,20},{1,9},{5,13},{25,17},{29,21},{2,10},{... | collective-permute-start | bytes 6291464 | tf_op jit(solution)/shard_map/ppermute | solution.py:429
  36.2 41.6 %collective-permute-done.2.refs_1_.refs_0_.refs_4_ = bf16[2,512,1024]{2,1,0:T(8,128)(2,1)} collective-permute-done((bf16[2,512,1024]{2,1,0:T(8,128)(2,1)S(1)}, bf16[2,512,1024]{2,1,0:T(8,128)(2,1)}, u32[]{:S(2)}, u32[]{:S(2)}) %collective-permute-start.2) | collective-permute-done | bytes 2097184 | tf_op jit(solution)/shard_map/ppermute | solution.py:429
  77.8 2.1 collective-permute-start.5
  85.8 7.8 %collective-permute-start.4 = (bf16[4,1024,256]{2,1,0:T(8,128)(2,1)S(1)}, bf16[4,1024,256]{2,1,0:T(8,128)(2,1)}, u32[]{:S(2)}, u32[]{:S(2)}) collective-permute-start(bf16[4,1024,256]{2,1,0:T(8,128)(2,1)S(1)} %pad_maximum_fusion.1), channel_id=1, source_target_pairs={{0,8},{4,12},{24,16},{28,20},{1,9},{5,13},{25,17},{29,21},{2,10},{... | collective-permute-start | bytes 6291464 | tf_op jit(solution)/shard_map/ppermute | solution.py:429
  93.6 3.7 fusion.3
  108.8 28.7 %collective-permute-done.4.refs_13_.refs_14_.refs_8_.refs_9_ = bf16[4,1024,256]{2,1,0:T(8,128)(2,1)} collective-permute-done((bf16[4,1024,256]{2,1,0:T(8,128)(2,1)S(1)}, bf16[4,1024,256]{2,1,0:T(8,128)(2,1)}, u32[]{:S(2)}, u32[]{:S(2)}) %collective-permute-start.4) | collective-permute-done | bytes 2097184 | tf_op jit(solution)/shard_map/ppermute | solution.py:429
  137.6 2.5 collective-permute-start.9
  140.1 2.0 collective-permute-start.11
  142.6 13.0 %collective-permute-start.8 = (bf16[4,1024,256]{2,1,0:T(8,128)(2,1)}, bf16[4,1024,256]{2,1,0:T(8,128)(2,1)}, u32[]{:S(2)}, u32[]{:S(2)}) collective-permute-start(bf16[4,1024,256]{2,1,0:T(8,128)(2,1)} %pad_maximum_fusion), channel_id=1, source_target_pairs={{0,8},{4,12},{24,16},{28,20},{1,9},{5,13},{25,17},{29,21},{2,10},{... | collective-permute-start | bytes 6291464 | tf_op jit(solution)/shard_map/ppermute | solution.py:429
  156.4 15.0 %shard_map.96 = (f32[512,768]{1,0:T(8,128)}, f32[512,768]{1,0:T(8,128)}) custom-call(s32[2,2,4]{2,1,0:T(2,128)} %pad_add_fusion.3.pick_ref, bf16[8,512,1024]{2,1,0:T(8,128)(2,1)} %copy-done.2, bf16[2,512,1024]{2,1,0:T(8,128)(2,1)} %collective-permute-done.2.refs_1_.refs_0_.refs_4_, bf16[2,512,1024]{2,1,0:T(8,128)(2,1)} %copy-done.7, ...), custom_call_target="tpu_custom_call" | custom-call | flops 6442450944 | bytes 20971520 | tf_op jit(solution)/shard_map/pallas_call | solution.py:328
  171.5 18.5 %collective-permute-done.12.refs_6_.refs_2_ = bf16[2,512,1024]{2,1,0:T(8,128)(2,1)} collective-permute-done((bf16[2,512,1024]{2,1,0:T(8,128)(2,1)}, bf16[2,512,1024]{2,1,0:T(8,128)(2,1)}, u32[]{:S(2)}, u32[]{:S(2)}) %collective-permute-start.12) | collective-permute-done | bytes 2097184 | tf_op jit(solution)/shard_map/ppermute | solution.py:438
  190.0 9.1 %collective-permute-done.8.refs_9_.refs_10_.refs_4_.refs_5_ = bf16[4,1024,256]{2,1,0:T(8,128)(2,1)} collective-permute-done((bf16[4,1024,256]{2,1,0:T(8,128)(2,1)}, bf16[4,1024,256]{2,1,0:T(8,128)(2,1)}, u32[]{:S(2)}, u32[]{:S(2)}) %collective-permute-start.8) | collective-permute-done | bytes 2097184 | tf_op jit(solution)/shard_map/ppermute | solution.py:429
  201.3 2.0 collective-permute-start.10
  207.3 6.3 %collective-permute-start.14 = (bf16[2,1024,256]{2,1,0:T(8,128)(2,1)}, bf16[2,1024,256]{2,1,0:T(8,128)(2,1)S(1)}, u32[]{:S(2)}, u32[]{:S(2)}) collective-permute-start(bf16[2,1024,256]{2,1,0:T(8,128)(2,1)} %pad_maximum_fusion.2), channel_id=1, source_target_pairs={{0,8},{4,12},{24,16},{28,20},{1,9},{5,13},{25,17},{29,21},{2,10},{... | collective-permute-start | bytes 3145736 | tf_op jit(solution)/shard_map/ppermute | solution.py:429
  213.6 9.5 %shard_map.98.refs_14_.refs_17_ = f32[512,768]{1,0:T(8,128)} custom-call(s32[1,2,4]{2,1,0:T(2,128)} %copy-done.16, bf16[2,512,1024]{2,1,0:T(8,128)(2,1)} %collective-permute-done.5.refs_4_.refs_0_, bf16[2,512,1024]{2,1,0:T(8,128)(2,1)} %collective-permute-done.16.refs_5_.refs_1_, bf16[2,512,1024]{2,1,0:T(8,128)(2,1)} %collective-permute-done.12.refs_6_.refs_2_, ...), custom_call_target="tpu_custom_call" | custom-call | flops 3221225472 | bytes 13631488 | tf_op jit(solution)/shard_map/pallas_call | solution.py:328
  223.1 29.8 %shard_map.97 = (bf16[512,512]{1,0:T(8,128)(2,1)}, bf16[512,512]{1,0:T(8,128)(2,1)}, bf16[512,512]{1,0:T(8,128)(2,1)}) custom-call(s32[3,2,8]{2,1,0:T(2,128)} %pad_add_fusion.1.pick_ref, bf16[2,512,1024]{2,1,0:T(8,128)(2,1)} %collective-permute-done.2.refs_1_.refs_0_.refs_4_, bf16[2,512,1024]{2,1,0:T(8,128)(2,1)} %copy-done.7, ...), custom_call_target="tpu_custom_call" | custom-call | flops 12884901888 | bytes 39845888 | tf_op jit(solution)/shard_map/pallas_call | solution.py:328
  261.6 21.5 %shard_map.100 = (bf16[512,512]{1,0:T(8,128)(2,1)}, bf16[512,512]{1,0:T(8,128)(2,1)}, bf16[512,512]{1,0:T(8,128)(2,1)}) custom-call(s32[3,2,4]{2,1,0:T(2,128)} %pad_add_fusion.2.pick_ref, bf16[2,512,1024]{2,1,0:T(8,128)(2,1)} %collective-permute-done.2.refs_1_.refs_0_.refs_4_, bf16[2,512,1024]{2,1,0:T(8,128)(2,1)} %copy-done.7, ...), custom_call_target="tpu_custom_call" | custom-call | flops 6442450944 | bytes 23068672 | tf_op jit(solution)/shard_map/pallas_call | solution.py:328
  287.8 11.9 %shard_map.101.refs_13_.refs_36_ = bf16[512,512]{1,0:T(8,128)(2,1)} custom-call(s32[1,2,8]{2,1,0:T(2,128)} %copy-done.18, bf16[2,512,1024]{2,1,0:T(8,128)(2,1)} %collective-permute-done.11.refs_0_.refs_8_, bf16[2,512,1024]{2,1,0:T(8,128)(2,1)} %collective-permute-done.19.refs_1_.refs_9_, bf16[2,512,1024]{2,1,0:T(8,128)(2,1)} %copy-done.6, ...), custom_call_target="tpu_custom_call" | custom-call | flops 4294967296 | bytes 18874368 | tf_op jit(solution)/shard_map/pallas_call | solution.py:328
  300.4 9.5 %shard_map.99.refs_8_.refs_19_ = f32[512,768]{1,0:T(8,128)} custom-call(s32[1,2,4]{2,1,0:T(2,128)} %copy-done.16, bf16[2,512,1024]{2,1,0:T(8,128)(2,1)} %collective-permute-done.11.refs_0_.refs_8_, bf16[2,512,1024]{2,1,0:T(8,128)(2,1)} %collective-permute-done.19.refs_1_.refs_9_, bf16[2,512,1024]{2,1,0:T(8,128)(2,1)} %copy-done.6, ...), custom_call_target="tpu_custom_call" | custom-call | flops 3221225472 | bytes 13631488 | tf_op jit(solution)/shard_map/pallas_call | solution.py:328
  309.9 9.6 %shard_map.102 = bf16[512,512]{1,0:T(8,128)(2,1)} custom-call(s32[1,2,4]{2,1,0:T(2,128)} %copy-done.17, bf16[2,512,1024]{2,1,0:T(8,128)(2,1)} %collective-permute-done.11.refs_0_.refs_8_, bf16[2,512,1024]{2,1,0:T(8,128)(2,1)} %collective-permute-done.19.refs_1_.refs_9_, bf16[2,512,1024]{2,1,0:T(8,128)(2,1)} %copy-done.6, ...), custom_call_target="tpu_custom_call" | custom-call | flops 2147483648 | bytes 10485760 | tf_op jit(solution)/shard_map/pallas_call | solution.py:328
  320.5 24.0 %shard_map.103 = (bf16[512,256]{1,0:T(8,128)(2,1)}, bf16[512,256]{1,0:T(8,128)(2,1)}, bf16[512,256]{1,0:T(8,128)(2,1)}, bf16[512,256]{1,0:T(8,128)(2,1)}) custom-call(s32[4,2,4]{2,1,0:T(2,128)} %pad_add_fusion.pick_ref, bf16[2,512,1024]{2,1,0:T(8,128)(2,1)} %collective-permute-done.5.refs_4_.refs_0_, ...), custom_call_target="tpu_custom_call" | custom-call | flops 4294967296 | bytes 23068672 | tf_op jit(solution)/shard_map/pallas_call | solution.py:328
  350.4 16.6 %collective-permute-done.26.refs_8_ = bf16[512,256]{1,0:T(8,128)(2,1)S(1)} collective-permute-done((bf16[512,256]{1,0:T(8,128)(2,1)}, bf16[512,256]{1,0:T(8,128)(2,1)S(1)}, u32[]{:S(2)}, u32[]{:S(2)}) %collective-permute-start.26) | collective-permute-done | bytes 262176 | tf_op jit(solution)/shard_map/ppermute | solution.py:429
  367.0 2.9 collective-permute-done.29.refs_11_
  370.8 65.4 %shard_map.104 = bf16[512,2048]{1,0:T(8,128)(2,1)} custom-call(s32[2]{0:T(128)} %pad_add_fusion.4.flag_ref, bf16[512,512]{1,0:T(8,128)(2,1)} %get-tuple-element.117.refs_28_.refs_37_.refs_0_, bf16[512,512]{1,0:T(8,128)(2,1)} %get-tuple-element.135.refs_1_, bf16[512,256]{1,0:T(8,128)(2,1)} %get-tuple-element.142.refs_2_, bf16[512,512]{1,0:T(8,128)(2,1)} %copy-done.11, ...), custom_call_target="tpu_custom_call" | custom-call | bytes 4194304 | tf_op jit(solution)/shard_map/pallas_call | solution.py:392
  (160 shorter events, 51.2 us)
Async XLA Ops:
  0.6 199.1 %copy-start = (f32[2,1024]{1,0:T(2,128)S(1)}, f32[2,1024]{1,0:T(2,128)}, u32[]{:S(2)}) copy-start(f32[2,1024]{1,0:T(2,128)} %param.13) | copy-start | bytes 24580
  14.2 63.6 %collective-permute-start = (bf16[5,1024,256]{2,1,0:T(8,128)(2,1)}, bf16[5,1024,256]{2,1,0:T(8,128)(2,1)}, u32[]{:S(2)}, u32[]{:S(2)}) collective-permute-start(bf16[5,1024,256]{2,1,0:T(8,128)(2,1)} %get-tuple-element.158), channel_id=1, source_target_pairs={{0,4},{4,0},{8,12},{12,8},{16,20},{20,16},{24,28},{28,24},{1,5},{5... | collective-permute-start | bytes 7864328 | tf_op jit(solution)/shard_map/ppermute | solution.py:429
  17.2 60.7 %collective-permute-start.1 = (bf16[5,1024,256]{2,1,0:T(8,128)(2,1)}, bf16[5,1024,256]{2,1,0:T(8,128)(2,1)}, u32[]{:S(2)}, u32[]{:S(2)}) collective-permute-start(bf16[5,1024,256]{2,1,0:T(8,128)(2,1)} %get-tuple-element.76.refs_5_.refs_9_.refs_4_), channel_id=1, source_target_pairs={{8,16},{12,20},{16,8},{20,12},{9,17},{13,21},{17,9},{21,13},{10,18... | collective-permute-start | bytes 7864328 | tf_op jit(solution)/shard_map/ppermute | solution.py:429
  28.8 49.1 %collective-permute-start.2 = (bf16[2,512,1024]{2,1,0:T(8,128)(2,1)S(1)}, bf16[2,512,1024]{2,1,0:T(8,128)(2,1)}, u32[]{:S(2)}, u32[]{:S(2)}) collective-permute-start(bf16[2,512,1024]{2,1,0:T(8,128)(2,1)S(1)} %get-tuple-element.86), channel_id=1, source_target_pairs={{0,8},{4,12},{24,16},{28,20},{1,9},{5,13},{25,17},{29,21},{2,10},{... | collective-permute-start | bytes 6291464 | tf_op jit(solution)/shard_map/ppermute | solution.py:429
  77.8 59.6 %collective-permute-start.5 = (bf16[2,512,1024]{2,1,0:T(8,128)(2,1)}, bf16[2,512,1024]{2,1,0:T(8,128)(2,1)}, u32[]{:S(2)}, u32[]{:S(2)}) collective-permute-start(bf16[2,512,1024]{2,1,0:T(8,128)(2,1)} %collective-permute-done.2.refs_1_.refs_0_.refs_4_), channel_id=1, source_target_pairs={{8,12},{12,8},{16,20},{20,16},{9,13},{13,9},{17,21},{21,17},{10,14... | collective-permute-start | bytes 6291464 | tf_op jit(solution)/shard_map/ppermute | solution.py:429
  79.9 57.6 %collective-permute-start.6 = (bf16[2,512,1024]{2,1,0:T(8,128)(2,1)}, bf16[2,512,1024]{2,1,0:T(8,128)(2,1)}, u32[]{:S(2)}, u32[]{:S(2)}) collective-permute-start(bf16[2,512,1024]{2,1,0:T(8,128)(2,1)} %collective-permute-done.2.refs_1_.refs_0_.refs_4_), channel_id=1, source_target_pairs={{0,2},{1,3},{2,0},{3,1},{4,6},{5,7},{6,4},{7,5},{8,10},{9,11},{10,... | collective-permute-start | bytes 6291464 | tf_op jit(solution)/shard_map/ppermute | solution.py:438
  81.4 56.1 %collective-permute-start.7 = (bf16[2,512,1024]{2,1,0:T(8,128)(2,1)}, bf16[2,512,1024]{2,1,0:T(8,128)(2,1)S(1)}, u32[]{:S(2)}, u32[]{:S(2)}) collective-permute-start(bf16[2,512,1024]{2,1,0:T(8,128)(2,1)} %collective-permute-done.2.refs_1_.refs_0_.refs_4_), channel_id=1, source_target_pairs={{0,1},{1,0},{2,3},{3,2},{4,5},{5,4},{6,7},{7,6},{8,9},{9,8},{10,11... | collective-permute-start | bytes 6291464 | tf_op jit(solution)/shard_map/ppermute | solution.py:441
  81.4 56.1 %collective-permute-start.3 = (bf16[5,1024,256]{2,1,0:T(8,128)(2,1)}, bf16[5,1024,256]{2,1,0:T(8,128)(2,1)S(1)}, u32[]{:S(2)}, u32[]{:S(2)}) collective-permute-start(bf16[5,1024,256]{2,1,0:T(8,128)(2,1)} %collective-permute-done.refs_6_.refs_10_.refs_5_), channel_id=1, source_target_pairs={{8,16},{12,20},{16,8},{20,12},{9,17},{13,21},{17,9},{21,13},{10,18... | collective-permute-start | bytes 7864328 | tf_op jit(solution)/shard_map/ppermute | solution.py:429
  85.8 51.7 %collective-permute-start.4 = (bf16[4,1024,256]{2,1,0:T(8,128)(2,1)S(1)}, bf16[4,1024,256]{2,1,0:T(8,128)(2,1)}, u32[]{:S(2)}, u32[]{:S(2)}) collective-permute-start(bf16[4,1024,256]{2,1,0:T(8,128)(2,1)S(1)} %pad_maximum_fusion.1), channel_id=1, source_target_pairs={{0,8},{4,12},{24,16},{28,20},{1,9},{5,13},{25,17},{29,21},{2,10},{... | collective-permute-start | bytes 6291464 | tf_op jit(solution)/shard_map/ppermute | solution.py:429
  137.5 18.9 %collective-permute-start.13 = (bf16[2,512,1024]{2,1,0:T(8,128)(2,1)}, bf16[2,512,1024]{2,1,0:T(8,128)(2,1)}, u32[]{:S(2)}, u32[]{:S(2)}) collective-permute-start(bf16[2,512,1024]{2,1,0:T(8,128)(2,1)} %collective-permute-done.6.refs_3_.refs_2_.refs_6_), channel_id=1, source_target_pairs={{0,1},{1,0},{2,3},{3,2},{4,5},{5,4},{6,7},{7,6},{8,9},{9,8},{10,11... | collective-permute-start | bytes 6291464 | tf_op jit(solution)/shard_map/ppermute | solution.py:441
  137.6 33.8 %collective-permute-start.9 = (bf16[4,1024,256]{2,1,0:T(8,128)(2,1)}, bf16[4,1024,256]{2,1,0:T(8,128)(2,1)}, u32[]{:S(2)}, u32[]{:S(2)}) collective-permute-start(bf16[4,1024,256]{2,1,0:T(8,128)(2,1)} %collective-permute-done.4.refs_13_.refs_14_.refs_8_.refs_9_), channel_id=1, source_target_pairs={{8,16},{12,20},{16,8},{20,12},{9,17},{13,21},{17,9},{21,13},{10,18... | collective-permute-start | bytes 6291464 | tf_op jit(solution)/shard_map/ppermute | solution.py:429
  140.1 31.4 %collective-permute-start.11 = (bf16[2,512,1024]{2,1,0:T(8,128)(2,1)S(1)}, bf16[2,512,1024]{2,1,0:T(8,128)(2,1)}, u32[]{:S(2)}, u32[]{:S(2)}) collective-permute-start(bf16[2,512,1024]{2,1,0:T(8,128)(2,1)S(1)} %get-tuple-element.86), channel_id=1, source_target_pairs={{8,12},{12,8},{16,20},{20,16},{9,13},{13,9},{17,21},{21,17},{10,14... | collective-permute-start | bytes 6291464 | tf_op jit(solution)/shard_map/ppermute | solution.py:429
  142.0 47.9 %collective-permute-start.12 = (bf16[2,512,1024]{2,1,0:T(8,128)(2,1)}, bf16[2,512,1024]{2,1,0:T(8,128)(2,1)}, u32[]{:S(2)}, u32[]{:S(2)}) collective-permute-start(bf16[2,512,1024]{2,1,0:T(8,128)(2,1)} %collective-permute-done.5.refs_4_.refs_0_), channel_id=1, source_target_pairs={{0,2},{1,3},{2,0},{3,1},{4,6},{5,7},{6,4},{7,5},{8,10},{9,11},{10,... | collective-permute-start | bytes 6291464 | tf_op jit(solution)/shard_map/ppermute | solution.py:438
  142.6 56.5 %collective-permute-start.8 = (bf16[4,1024,256]{2,1,0:T(8,128)(2,1)}, bf16[4,1024,256]{2,1,0:T(8,128)(2,1)}, u32[]{:S(2)}, u32[]{:S(2)}) collective-permute-start(bf16[4,1024,256]{2,1,0:T(8,128)(2,1)} %pad_maximum_fusion), channel_id=1, source_target_pairs={{0,8},{4,12},{24,16},{28,20},{1,9},{5,13},{25,17},{29,21},{2,10},{... | collective-permute-start | bytes 6291464 | tf_op jit(solution)/shard_map/ppermute | solution.py:429
  199.1 14.5 %collective-permute-start.16 = (bf16[2,512,1024]{2,1,0:T(8,128)(2,1)}, bf16[2,512,1024]{2,1,0:T(8,128)(2,1)}, u32[]{:S(2)}, u32[]{:S(2)}) collective-permute-start(bf16[2,512,1024]{2,1,0:T(8,128)(2,1)} %collective-permute-done.5.refs_4_.refs_0_), channel_id=1, source_target_pairs={{0,1},{1,0},{2,3},{3,2},{4,5},{5,4},{6,7},{7,6},{8,9},{9,8},{10,11... | collective-permute-start | bytes 6291464 | tf_op jit(solution)/shard_map/ppermute | solution.py:441
  199.1 14.5 %collective-permute-start.17 = (bf16[2,512,1024]{2,1,0:T(8,128)(2,1)}, bf16[2,512,1024]{2,1,0:T(8,128)(2,1)}, u32[]{:S(2)}, u32[]{:S(2)}) collective-permute-start(bf16[2,512,1024]{2,1,0:T(8,128)(2,1)} %collective-permute-done.12.refs_6_.refs_2_), channel_id=1, source_target_pairs={{0,1},{1,0},{2,3},{3,2},{4,5},{5,4},{6,7},{7,6},{8,9},{9,8},{10,11... | collective-permute-start | bytes 6291464 | tf_op jit(solution)/shard_map/ppermute | solution.py:441
  199.8 53.2 %collective-permute-start.15 = (bf16[2,512,1024]{2,1,0:T(8,128)(2,1)}, bf16[2,512,1024]{2,1,0:T(8,128)(2,1)S(1)}, u32[]{:S(2)}, u32[]{:S(2)}) collective-permute-start(bf16[2,512,1024]{2,1,0:T(8,128)(2,1)} %collective-permute-done.11.refs_0_.refs_8_), channel_id=1, source_target_pairs={{0,2},{1,3},{2,0},{3,1},{4,6},{5,7},{6,4},{7,5},{8,10},{9,11},{10,... | collective-permute-start | bytes 6291464 | tf_op jit(solution)/shard_map/ppermute | solution.py:438
  201.3 51.7 %collective-permute-start.10 = (bf16[4,1024,256]{2,1,0:T(8,128)(2,1)}, bf16[4,1024,256]{2,1,0:T(8,128)(2,1)}, u32[]{:S(2)}, u32[]{:S(2)}) collective-permute-start(bf16[4,1024,256]{2,1,0:T(8,128)(2,1)} %collective-permute-done.8.refs_9_.refs_10_.refs_4_.refs_5_), channel_id=1, source_target_pairs={{8,16},{12,20},{16,8},{20,12},{9,17},{13,21},{17,9},{21,13},{10,18... | collective-permute-start | bytes 6291464 | tf_op jit(solution)/shard_map/ppermute | solution.py:429
  207.3 45.7 %collective-permute-start.14 = (bf16[2,1024,256]{2,1,0:T(8,128)(2,1)}, bf16[2,1024,256]{2,1,0:T(8,128)(2,1)S(1)}, u32[]{:S(2)}, u32[]{:S(2)}) collective-permute-start(bf16[2,1024,256]{2,1,0:T(8,128)(2,1)} %pad_maximum_fusion.2), channel_id=1, source_target_pairs={{0,8},{4,12},{24,16},{28,20},{1,9},{5,13},{25,17},{29,21},{2,10},{... | collective-permute-start | bytes 3145736 | tf_op jit(solution)/shard_map/ppermute | solution.py:429
  253.0 33.2 %collective-permute-start.19 = (bf16[2,512,1024]{2,1,0:T(8,128)(2,1)}, bf16[2,512,1024]{2,1,0:T(8,128)(2,1)}, u32[]{:S(2)}, u32[]{:S(2)}) collective-permute-start(bf16[2,512,1024]{2,1,0:T(8,128)(2,1)} %collective-permute-done.11.refs_0_.refs_8_), channel_id=1, source_target_pairs={{0,1},{1,0},{2,3},{3,2},{4,5},{5,4},{6,7},{7,6},{8,9},{9,8},{10,11... | collective-permute-start | bytes 6291464 | tf_op jit(solution)/shard_map/ppermute | solution.py:441
  253.1 34.7 %collective-permute-start.20 = (bf16[2,512,1024]{2,1,0:T(8,128)(2,1)S(1)}, bf16[2,512,1024]{2,1,0:T(8,128)(2,1)}, u32[]{:S(2)}, u32[]{:S(2)}) collective-permute-start(bf16[2,512,1024]{2,1,0:T(8,128)(2,1)S(1)} %collective-permute-done.15.refs_2_.refs_10_), channel_id=1, source_target_pairs={{0,1},{1,0},{2,3},{3,2},{4,5},{5,4},{6,7},{7,6},{8,9},{9,8},{10,11... | collective-permute-start | bytes 6291464 | tf_op jit(solution)/shard_map/ppermute | solution.py:441
  257.3 25.8 %collective-permute-start.24 = (bf16[512,512]{1,0:T(8,128)(2,1)}, bf16[512,512]{1,0:T(8,128)(2,1)S(1)}, u32[]{:S(2)}, u32[]{:S(2)}) collective-permute-start(bf16[512,512]{1,0:T(8,128)(2,1)} %get-tuple-element.126.refs_26_.refs_35_), channel_id=1, source_target_pairs={{8,0},{12,4},{16,24},{20,28},{9,1},{13,5},{17,25},{21,29},{10,2},{... | collective-permute-start | bytes 1572872 | tf_op jit(solution)/shard_map/ppermute | solution.py:429
  258.6 86.0 %collective-permute-start.27 = (bf16[512,512]{1,0:T(8,128)(2,1)}, bf16[512,512]{1,0:T(8,128)(2,1)}, u32[]{:S(2)}, u32[]{:S(2)}) collective-permute-start(bf16[512,512]{1,0:T(8,128)(2,1)} %get-tuple-element.127.refs_27_.refs_34_), channel_id=1, source_target_pairs={{8,4},{12,0},{16,28},{20,24},{9,5},{13,1},{17,29},{21,25},{10,6},{... | collective-permute-start | bytes 1572872 | tf_op jit(solution)/shard_map/ppermute | solution.py:429
  259.9 50.1 %collective-permute-start.18 = (bf16[2,1024,256]{2,1,0:T(8,128)(2,1)S(1)}, bf16[2,1024,256]{2,1,0:T(8,128)(2,1)}, u32[]{:S(2)}, u32[]{:S(2)}) collective-permute-start(bf16[2,1024,256]{2,1,0:T(8,128)(2,1)S(1)} %collective-permute-done.14.refs_13_.refs_14_), channel_id=1, source_target_pairs={{8,16},{12,20},{16,8},{20,12},{9,17},{13,21},{17,9},{21,13},{10,18... | collective-permute-start | bytes 3145736 | tf_op jit(solution)/shard_map/ppermute | solution.py:429
  283.1 62.1 %collective-permute-start.25 = (bf16[512,512]{1,0:T(8,128)(2,1)}, bf16[512,512]{1,0:T(8,128)(2,1)}, u32[]{:S(2)}, u32[]{:S(2)}) collective-permute-start(bf16[512,512]{1,0:T(8,128)(2,1)} %get-tuple-element.133), channel_id=1, source_target_pairs={{8,0},{12,4},{16,24},{20,28},{9,1},{13,5},{17,25},{21,29},{10,2},{... | collective-permute-start | bytes 1572872 | tf_op jit(solution)/shard_map/ppermute | solution.py:429
  286.2 64.1 %collective-permute-start.28 = (bf16[512,512]{1,0:T(8,128)(2,1)}, bf16[512,512]{1,0:T(8,128)(2,1)}, u32[]{:S(2)}, u32[]{:S(2)}) collective-permute-start(bf16[512,512]{1,0:T(8,128)(2,1)} %get-tuple-element.134), channel_id=1, source_target_pairs={{8,4},{12,0},{16,28},{20,24},{9,5},{13,1},{17,29},{21,25},{10,6},{... | collective-permute-start | bytes 1572872 | tf_op jit(solution)/shard_map/ppermute | solution.py:429
  299.7 46.8 %collective-permute-start.21 = (bf16[512,512]{1,0:T(8,128)(2,1)}, bf16[512,512]{1,0:T(8,128)(2,1)S(1)}, u32[]{:S(2)}, u32[]{:S(2)}) collective-permute-start(bf16[512,512]{1,0:T(8,128)(2,1)} %shard_map.101.refs_13_.refs_36_), channel_id=1, source_target_pairs={{8,12},{12,8},{16,20},{20,16},{9,13},{13,9},{17,21},{21,17},{10,14... | collective-permute-start | bytes 1572872 | tf_op jit(solution)/shard_map/ppermute | solution.py:429
  319.5 50.4 %collective-permute-start.22 = (bf16[512,512]{1,0:T(8,128)(2,1)}, bf16[512,512]{1,0:T(8,128)(2,1)S(1)}, u32[]{:S(2)}, u32[]{:S(2)}) collective-permute-start(bf16[512,512]{1,0:T(8,128)(2,1)} %shard_map.102), channel_id=1, source_target_pairs={{8,12},{12,8},{16,20},{20,16},{9,13},{13,9},{17,21},{21,17},{10,14... | collective-permute-start | bytes 1572872 | tf_op jit(solution)/shard_map/ppermute | solution.py:429
  344.5 5.8 %collective-permute-start.23 = (bf16[512,256]{1,0:T(8,128)(2,1)}, bf16[512,256]{1,0:T(8,128)(2,1)S(1)}, u32[]{:S(2)}, u32[]{:S(2)}) collective-permute-start(bf16[512,256]{1,0:T(8,128)(2,1)} %get-tuple-element.143), channel_id=1, source_target_pairs={{8,12},{12,8},{16,20},{20,16},{9,13},{13,9},{17,21},{21,17},{10,14... | collective-permute-start | bytes 786440 | tf_op jit(solution)/shard_map/ppermute | solution.py:429
  345.2 21.8 %collective-permute-start.26 = (bf16[512,256]{1,0:T(8,128)(2,1)}, bf16[512,256]{1,0:T(8,128)(2,1)S(1)}, u32[]{:S(2)}, u32[]{:S(2)}) collective-permute-start(bf16[512,256]{1,0:T(8,128)(2,1)} %get-tuple-element.144), channel_id=1, source_target_pairs={{8,0},{12,4},{16,24},{20,28},{9,1},{13,5},{17,25},{21,29},{10,2},{... | collective-permute-start | bytes 786440 | tf_op jit(solution)/shard_map/ppermute | solution.py:429
  346.5 23.4 %collective-permute-start.29 = (bf16[512,256]{1,0:T(8,128)(2,1)}, bf16[512,256]{1,0:T(8,128)(2,1)S(1)}, u32[]{:S(2)}, u32[]{:S(2)}) collective-permute-start(bf16[512,256]{1,0:T(8,128)(2,1)} %get-tuple-element.145), channel_id=1, source_target_pairs={{8,4},{12,0},{16,28},{20,24},{9,5},{13,1},{17,29},{21,25},{10,6},{... | collective-permute-start | bytes 786440 | tf_op jit(solution)/shard_map/ppermute | solution.py:429
  369.9 66.3 %copy-start.1 = (f32[2,1024]{1,0:T(2,128)S(1)}, f32[2,1024]{1,0:T(2,128)}, u32[]{:S(2)}) copy-start(f32[2,1024]{1,0:T(2,128)} %param.13) | copy-start | bytes 24580
  (20 other events, 317.1 us)
